TPU v7x, 256 devices: a whole 4x4x8 slice. The times are simulated.
256 devices in a mesh: dp: 8 (over z_hi, core), expert: 32 (over x, y, z_lo).
Axes of the slice: x: 4, y: 4, z: 8 (z_hi: 4, z_lo: 2; z = z_hi * 2 + z_lo), core: 2. Of those that a mesh axis runs over, the one named last changes fastest.
Arguments:
- tokens: bfloat16 [16384, 2048], P(('dp', 'expert')), may hold values from -6 to 6
- out_grad: bfloat16 [16384, 2048], P(('dp', 'expert')), may hold values from -6 to 6
- expert_ids: int32 [16384, 8], P(('dp', 'expert')), may hold values from 0 to 63, as said below
- slot_positions: int32 [16384, 8], P(('dp', 'expert')), may hold values from 0 to 9, as said below
- keep_mask: int32 [16384, 8], P(('dp', 'expert')), may hold values from 0 to 1, as said below
- router_weight: bfloat16 [2048, 64], replicated, may hold values from -0.125 to 0.125
- w_gate: bfloat16 [64, 2048, 384], P('expert', 'dp'), may hold values from -0.125 to 0.125
- w_up: bfloat16 [64, 2048, 384], P('expert', 'dp'), may hold values from -0.125 to 0.125
- w_down: bfloat16 [64, 384, 2048], P('expert', None, 'dp'), may hold values from -0.3125 to 0.3125
Outputs:
- grad_tokens: bfloat16 [16384, 2048], P(('dp', 'expert'))
- grad_w_gate: bfloat16 [64, 2048, 384], P('expert', 'dp')
- grad_w_up: bfloat16 [64, 2048, 384], P('expert', 'dp')
- grad_w_down: bfloat16 [64, 384, 2048], P('expert', None, 'dp')
- grad_router: float32 [64, 2048], P('expert', 'dp')
Inputs may be any that keep to these rules, and one draw needn't show every extreme that they name: `expert_ids`: each row names 8 different experts. `slot_positions`: within each block of 64 tokens, with choices taken in order of token and then of k, a choice's position is the number of earlier choices of the block that named the same expert; where that number is 10 or more the choice is dropped and its position is given as 9. Kept choices of one block never share an expert and a position. In every group of 32 blocks one expert has all 10 slots taken in every block. `keep_mask`: 1 exactly where the arrival count described for slot_positions is below 10; every block drops some choices.
All inputs are finite; a program needn't handle non-finite values.
Results may differ from a plain program's by a relative error of at most 0.027.
Values may be sent and summed in bfloat16 or wider, within the bound.
No kernel may reach another device: no remote copies, remote signals or barrier semaphores. Data moves between devices by JAX's collectives and lax.ppermute only.
A program may use at most 128 MiB of HBM per device.

v0:
```python
import jax
import jax.numpy as jnp
from jax import lax
from jax.sharding import PartitionSpec as P


def silu_parts(gate_pre):
    sigmoid_gate = jax.nn.sigmoid(gate_pre)
    return (gate_pre * sigmoid_gate, sigmoid_gate * (1.0 + gate_pre * (1.0 - sigmoid_gate)))


def routing_gates(tokens, expert_ids, router_weight):
    logits = jnp.dot(tokens, router_weight, preferred_element_type=jnp.float32)
    columns = jnp.arange(router_weight.shape[1], dtype=jnp.int32)
    chosen = expert_ids[:, :, None] == columns[None, None, :]
    picked = jnp.sum(jnp.where(chosen, logits[:, None, :], jnp.zeros((), logits.dtype)), axis=2)
    probits = jax.nn.sigmoid(picked)
    totals = jnp.sum(probits, axis=1, keepdims=True)
    return (chosen, probits, totals, probits / totals)


def router_backward(chosen, probits, totals, gate_share, taken_score):
    mean_score = jnp.sum(gate_share * taken_score, axis=1, keepdims=True)
    dlogit = (taken_score - mean_score) / totals * probits * (1.0 - probits)
    spread = jnp.where(chosen, dlogit[:, :, None], jnp.zeros((), dlogit.dtype))
    return jnp.sum(spread, axis=1).astype(jnp.bfloat16)


def expert_block(slot_tokens, slot_out_grad, slot_gate, gate_w, up_w, down_w):
    gate_pre = jnp.einsum("sxrd,xdf->sxrf", slot_tokens, gate_w, preferred_element_type=jnp.float32)
    up_pre = jnp.einsum("sxrd,xdf->sxrf", slot_tokens, up_w, preferred_element_type=jnp.float32)
    active, slope_term = silu_parts(gate_pre)
    hidden = (active * up_pre).astype(jnp.bfloat16)
    expert_out = jnp.einsum("sxrf,xfd->sxrd", hidden, down_w, preferred_element_type=jnp.float32)
    score_rows = jnp.sum(expert_out * slot_out_grad.astype(jnp.float32), axis=3).astype(
        jnp.bfloat16
    )
    scaled = (slot_gate.astype(jnp.float32)[..., None] * slot_out_grad.astype(jnp.float32)).astype(
        jnp.bfloat16
    )
    hidden_grad = jnp.einsum("sxrd,xfd->sxrf", scaled, down_w, preferred_element_type=jnp.float32)
    gate_grad = (hidden_grad * up_pre * slope_term).astype(jnp.bfloat16)
    up_grad = (hidden_grad * active).astype(jnp.bfloat16)
    input_grad = (
        jnp.einsum("sxrf,xdf->sxrd", gate_grad, gate_w, preferred_element_type=jnp.float32)
        + jnp.einsum("sxrf,xdf->sxrd", up_grad, up_w, preferred_element_type=jnp.float32)
    ).astype(jnp.bfloat16)
    return (input_grad, score_rows, hidden, scaled, gate_grad, up_grad)


def per_device(
    tokens, out_grad, expert_ids, slot_positions, keep_mask, router_weight, w_gate, w_up, w_down
):
    tok_rows = tokens.shape[0]
    feature_width = tokens.shape[1]
    top_count = expert_ids.shape[1]
    expert_total = router_weight.shape[1]
    groups = lax.axis_size("expert")
    local_experts = w_gate.shape[0]
    capacity = (5 * tok_rows * top_count + 4 * expert_total - 1) // (4 * expert_total)
    slot_count = expert_total * capacity
    chosen, probits, totals, gate_share = routing_gates(tokens, expert_ids, router_weight)
    kept_flag = keep_mask > 0
    slot_index = expert_ids * capacity + slot_positions
    target = jnp.where(kept_flag, slot_index, slot_count).reshape(-1)
    owners = jnp.broadcast_to(
        jnp.arange(tok_rows, dtype=jnp.int32)[:, None], expert_ids.shape
    ).reshape(-1)
    slot_owner = jnp.zeros((slot_count + 1,), jnp.int32).at[target].set(owners)[:slot_count]
    slot_live = (
        jnp.zeros((slot_count + 1,), jnp.int32).at[target].set(jnp.ones_like(owners))[:slot_count]
    )
    slot_weight = (
        jnp.zeros((slot_count + 1,), jnp.float32)
        .at[target]
        .set(gate_share.reshape(-1))[:slot_count]
    )
    live_flag = (slot_live > 0)[:, None]
    send_tokens = jnp.where(live_flag, tokens[slot_owner], jnp.zeros((), tokens.dtype))
    send_tokens = send_tokens.reshape(groups, local_experts, capacity, feature_width)
    send_grads = jnp.where(live_flag, out_grad[slot_owner], jnp.zeros((), out_grad.dtype))
    send_grads = send_grads.reshape(groups, local_experts, capacity, feature_width)
    send_gates = slot_weight.astype(jnp.bfloat16).reshape(groups, local_experts, capacity)
    gate_w, up_w, down_w = (
        lax.all_gather(w_gate, "dp", axis=1, tiled=True),
        lax.all_gather(w_up, "dp", axis=1, tiled=True),
        lax.all_gather(w_down, "dp", axis=2, tiled=True),
    )
    slot_tokens, slot_grads, slot_gates = (
        lax.all_to_all(send_tokens, "expert", split_axis=0, concat_axis=0, tiled=True),
        lax.all_to_all(send_grads, "expert", split_axis=0, concat_axis=0, tiled=True),
        lax.all_to_all(send_gates, "expert", split_axis=0, concat_axis=0, tiled=True),
    )
    input_grad, score_rows, hidden, scaled, gate_grad, up_grad = expert_block(
        slot_tokens, slot_grads, slot_gates, gate_w, up_w, down_w
    )
    back_grad, back_score = (
        lax.all_to_all(input_grad, "expert", split_axis=0, concat_axis=0, tiled=True),
        lax.all_to_all(score_rows, "expert", split_axis=0, concat_axis=0, tiled=True),
    )
    gate_term = jnp.einsum(
        "sxrd,sxrf->xdf", slot_tokens, gate_grad, preferred_element_type=jnp.float32
    )
    up_term = jnp.einsum("sxrd,sxrf->xdf", slot_tokens, up_grad, preferred_element_type=jnp.float32)
    down_term = jnp.einsum("sxrf,sxrd->xfd", hidden, scaled, preferred_element_type=jnp.float32)
    grad_gate, grad_up, grad_down = (
        lax.psum_scatter(
            gate_term.astype(jnp.bfloat16), "dp", scatter_dimension=1, tiled=True
        ).astype(jnp.float32),
        lax.psum_scatter(
            up_term.astype(jnp.bfloat16), "dp", scatter_dimension=1, tiled=True
        ).astype(jnp.float32),
        lax.psum_scatter(
            down_term.astype(jnp.bfloat16), "dp", scatter_dimension=2, tiled=True
        ).astype(jnp.float32),
    )
    slot_back = back_grad.reshape(slot_count, feature_width)
    score_back = back_score.reshape(slot_count)
    slot_pick = jnp.where(kept_flag, slot_index, 0)
    keep_float = keep_mask.astype(jnp.float32)
    expert_part = jnp.sum(slot_back[slot_pick].astype(jnp.float32) * keep_float[:, :, None], axis=1)
    taken_score = score_back[slot_pick].astype(jnp.float32) * keep_float
    dlogits = router_backward(chosen, probits, totals, gate_share, taken_score)
    grad_tokens = (
        expert_part + jnp.dot(dlogits, router_weight.T, preferred_element_type=jnp.float32)
    ).astype(jnp.bfloat16)
    router_term = jnp.dot(dlogits.T, tokens, preferred_element_type=jnp.float32)
    by_expert = lax.psum_scatter(
        router_term.astype(jnp.bfloat16), "expert", scatter_dimension=0, tiled=True
    ).astype(jnp.float32)
    grad_router = lax.psum_scatter(by_expert, "dp", scatter_dimension=1, tiled=True)
    return (
        grad_tokens,
        grad_gate.astype(jnp.bfloat16),
        grad_up.astype(jnp.bfloat16),
        grad_down.astype(jnp.bfloat16),
        grad_router,
    )


def solution(mesh):
    return jax.shard_map(
        per_device,
        mesh=mesh,
        in_specs=(
            P(("dp", "expert"), None),
            P(("dp", "expert"), None),
            P(("dp", "expert"), None),
            P(("dp", "expert"), None),
            P(("dp", "expert"), None),
            P(),
            P("expert", "dp", None),
            P("expert", "dp", None),
            P("expert", None, "dp"),
        ),
        out_specs=(
            P(("dp", "expert"), None),
            P("expert", "dp", None),
            P("expert", "dp", None),
            P("expert", None, "dp"),
            P("expert", "dp"),
        ),
        check_vma=False,
    )
```

profile of v0, /device:TPU:1, one launch (start us, length us, event | category | flops | bytes accessed | tf_op | source)
XLA Modules:
  0.0 726.3 jit_solution(13430193225287229873)
XLA Ops:
  12.9 3.4 gather_fusion
  19.2 3.4 gather_fusion.1
  28.0 5.2 broadcast_select_fusion.1
  33.2 4.2 copy.119
  37.4 9.3 %all-to-all-start.2 = ((bf16[32,2,10,2048]{3,1,2,0:T(2,128)(2,1)}), bf16[32,2,10,2048]{3,1,2,0:T(2,128)(2,1)S(1)}, u32[]{:S(2)}, u32[]{:S(2)}) async-start(bf16[32,2,10,2048]{3,1,2,0:T(2,128)(2,1)} %copy.119), calls=%async_computation.2 | async-start | bytes 5242880 | tf_op jit(solution)/shard_map/all_to_all | solution.py:90
  47.4 6.5 copy.117
  53.9 60.5 %all-to-all-done.2 = bf16[32,2,10,2048]{3,1,2,0:T(2,128)(2,1)S(1)} async-done(((bf16[32,2,10,2048]{3,1,2,0:T(2,128)(2,1)}), bf16[32,2,10,2048]{3,1,2,0:T(2,128)(2,1)S(1)}, u32[]{:S(2)}, u32[]{:S(2)}) %all-to-all-start.2) | async-done | bytes 2621472 | tf_op jit(solution)/shard_map/all_to_all | solution.py:90
  114.4 6.2 all-to-all-start.1
  121.5 5.9 fusion.33
  127.4 6.4 multiply_convert_fusion
  133.8 40.0 %all-to-all-done.1 = bf16[32,2,10,2048]{3,1,2,0:T(2,128)(2,1)} async-done(((bf16[32,2,10,2048]{3,1,2,0:T(2,128)(2,1)}), bf16[32,2,10,2048]{3,1,2,0:T(2,128)(2,1)}, u32[]{:S(2)}, u32[]{:S(2)}) %all-to-all-start.1) | async-done | bytes 2621472 | tf_op jit(solution)/shard_map/all_to_all | solution.py:91
  173.8 6.4 all-gather.4.cloned.1.call-done
  180.2 6.5 fusion.1
  187.5 8.3 %all-to-all-start.4 = ((bf16[32,2,10]{2,1,0:T(2,128)(2,1)}), bf16[32,2,10]{2,1,0:T(2,128)(2,1)S(1)}, u32[]{:S(2)}, u32[]{:S(2)}) async-start(bf16[32,2,10]{2,1,0:T(2,128)(2,1)} %copy.127), calls=%async_computation.4 | async-start | bytes 32768 | tf_op jit(solution)/shard_map/all_to_all | solution.py:99
  196.3 6.5 all-to-all-done.4
  203.0 3.5 gather_fusion.3
  211.5 3.8 all-to-all-start
  216.6 5.7 all-to-all-done
  222.4 271.8 %all-reduce.3.cloned.1.call-done = bf16[64,2048]{1,0:T(8,128)(2,1)} async-done(((bf16[64,2048]{1,0:T(8,128)(2,1)}), bf16[64,2048]{1,0:T(8,128)(2,1)}) %all-reduce.3.cloned.1.call-update) | async-done | bytes 262160
  496.4 7.5 %bitcast_convert_fusion = bf16[2,384,2048]{2,1,0:T(8,128)(2,1)} fusion(bf16[32,2,10,384]{3,0,2,1:T(8,128)(2,1)} %get-tuple-element.14, f32[32,2,10]{0,2,1:T(8,128)S(1)} %copy.116, bf16[32,2,10,2048]{3,1,2,0:T(2,128)(2,1)} %all-to-all-done.1), kind=kOutput, calls=%fused_computation.9 | convolution fusion | flops 1012137984 | bytes 6261248 | tf_op jit(solution)/shard_map/sxrf,sxrd->xfd/dot_general | solution.py:105
  504.1 7.6 %multiply_convert_fusion.1 = (bf16[32,2,10,384]{3,0,2,1:T(8,128)(2,1)S(1)}, bf16[32,2,10,384]{3,0,2,1:T(8,128)(2,1)}) fusion(f32[32,2,10,384]{3,0,2,1:T(8,128)} %fusion.33, f32[32,2,10,384]{3,0,2,1:T(8,128)} %get-tuple-element.15, bf16[2,384,2048]{2,1,0:T(8,128)(2,1)} %all-gather.4.cloned.1.call-done, f32[32,2,10]{0,2,1:T(8,128)S(1)} %copy.116, ...), kind=kOutput, calls=%fused_computation.41 | convolution fusion | flops 1013760000 | bytes 8718848 | tf_op jit(solution)/shard_map/sxrd,xfd->sxrf/dot_general | solution.py:41
  511.7 6.5 bitcast_convert_fusion.1
  519.2 6.7 bitcast_convert_fusion.2
  532.2 4.2 copy.122
  536.4 7.4 %all-to-all-start.3 = ((bf16[32,2,10,2048]{3,1,2,0:T(2,128)(2,1)}), bf16[32,2,10,2048]{3,1,2,0:T(2,128)(2,1)S(1)}, u32[]{:S(2)}, u32[]{:S(2)}) async-start(bf16[32,2,10,2048]{3,1,2,0:T(2,128)(2,1)} %copy.122), calls=%async_computation.3 | async-start | bytes 5242880 | tf_op jit(solution)/shard_map/all_to_all | solution.py:98
  543.9 11.2 %reduce-scatter.13.cloned.1.call-done = f32[256,2]{1,0:T(8,128)} async-done(((f32[2048,2]{1,0:T(8,128)}), f32[256,2]{1,0:T(8,128)}) %reduce-scatter.13.cloned.1.call-update) | async-done | bytes 2064
  556.7 12.7 %all-to-all-done.3 = bf16[32,2,10,2048]{3,1,2,0:T(2,128)(2,1)S(1)} async-done(((bf16[32,2,10,2048]{3,1,2,0:T(2,128)(2,1)}), bf16[32,2,10,2048]{3,1,2,0:T(2,128)(2,1)S(1)}, u32[]{:S(2)}, u32[]{:S(2)}) %all-to-all-start.3) | async-done | bytes 2621472 | tf_op jit(solution)/shard_map/all_to_all | solution.py:98
  572.7 4.1 reshape.90
  580.2 3.5 fusion.2
  584.6 28.8 %reduce-scatter.11.cloned.1.call-done = bf16[2,384,256]{2,1,0:T(8,128)(2,1)} async-done(((bf16[2,384,2048]{2,1,0:T(8,128)(2,1)}), bf16[2,384,256]{2,1,0:T(8,128)(2,1)}) %reduce-scatter.11.cloned.1.call-update) | async-done | bytes 393232 | tf_op jit(solution)/shard_map/reduce_scatter | solution.py:113
  613.3 52.8 %reduce-scatter.9.cloned.1.call-done = bf16[2,256,384]{2,1,0:T(8,128)(2,1)} async-done(((bf16[2,2048,384]{2,1,0:T(8,128)(2,1)}), bf16[2,256,384]{2,1,0:T(8,128)(2,1)}) %reduce-scatter.9.cloned.1.call-update) | async-done | bytes 393232 | tf_op jit(solution)/shard_map/reduce_scatter | solution.py:110
  666.2 52.8 %reduce-scatter.7.cloned.1.call-done = bf16[2,256,384]{2,1,0:T(8,128)(2,1)} async-done(((bf16[2,2048,384]{2,1,0:T(8,128)(2,1)}), bf16[2,256,384]{2,1,0:T(8,128)(2,1)}) %reduce-scatter.7.cloned.1.call-update) | async-done | bytes 393232 | tf_op jit(solution)/shard_map/reduce_scatter | solution.py:107
  (94 shorter events, 41.3 us)
Async XLA Ops:
  7.2 12.0 %copy-start = (bf16[64,2048]{1,0:T(8,128)(2,1)S(1)}, bf16[64,2048]{1,0:T(8,128)(2,1)}, u32[]{:S(2)}) copy-start(bf16[64,2048]{1,0:T(8,128)(2,1)} %param.9) | copy-start | bytes 786436
  7.2 5.7 copy-start.2
  7.2 114.3 %all-gather.8.cloned.1.call-start = ((), (), s32[]{:S(2)}) async-start(), calls=%async_computation.11 | async-start | bytes 3538944 | tf_op jit(solution)/shard_map/all_gather | solution.py:85
  7.9 119.5 %all-gather.6.cloned.1.call-start = ((), (), s32[]{:S(2)}) async-start(), calls=%async_computation.10 | async-start | bytes 3538944 | tf_op jit(solution)/shard_map/all_gather | solution.py:86
  37.4 77.0 %all-to-all-start.2 = ((bf16[32,2,10,2048]{3,1,2,0:T(2,128)(2,1)}), bf16[32,2,10,2048]{3,1,2,0:T(2,128)(2,1)S(1)}, u32[]{:S(2)}, u32[]{:S(2)}) async-start(bf16[32,2,10,2048]{3,1,2,0:T(2,128)(2,1)} %copy.119), calls=%async_computation.2 | async-start | bytes 5242880 | tf_op jit(solution)/shard_map/all_to_all | solution.py:90
  46.7 133.5 %all-gather.4.cloned.1.call-start = ((), (), s32[]{:S(2)}) async-start(), calls=%async_computation.9 | async-start | bytes 3538944 | tf_op jit(solution)/shard_map/all_gather | solution.py:87
  53.9 66.8 %copy-start.11 = (s32[64,8]{0,1:T(8,128)S(1)}, s32[64,8]{0,1:T(8,128)}, u32[]{:S(2)}) copy-start(s32[64,8]{0,1:T(8,128)} %param.11) | copy-start | bytes 6148
  53.9 67.0 %copy-start.5 = (bf16[2048,64]{0,1:T(8,128)(2,1)S(1)}, bf16[2048,64]{0,1:T(8,128)(2,1)}, u32[]{:S(2)}) copy-start(bf16[2048,64]{0,1:T(8,128)(2,1)} %param.14) | copy-start | bytes 786436
  114.4 59.4 %all-to-all-start.1 = ((bf16[32,2,10,2048]{3,1,2,0:T(2,128)(2,1)}), bf16[32,2,10,2048]{3,1,2,0:T(2,128)(2,1)}, u32[]{:S(2)}, u32[]{:S(2)}) async-start(bf16[32,2,10,2048]{3,1,2,0:T(2,128)(2,1)} %copy.117), calls=%async_computation.1 | async-start | bytes 5242880 | tf_op jit(solution)/shard_map/all_to_all | solution.py:91
  187.5 15.4 %all-to-all-start.4 = ((bf16[32,2,10]{2,1,0:T(2,128)(2,1)}), bf16[32,2,10]{2,1,0:T(2,128)(2,1)S(1)}, u32[]{:S(2)}, u32[]{:S(2)}) async-start(bf16[32,2,10]{2,1,0:T(2,128)(2,1)} %copy.127), calls=%async_computation.4 | async-start | bytes 32768 | tf_op jit(solution)/shard_map/all_to_all | solution.py:99
  195.8 298.4 %all-reduce.3.cloned.1.call-start = ((), (), s32[]{:S(2)}) async-start(), calls=%async_computation.16 | async-start | bytes 524288
  203.0 3.7 copy-start.10
  203.0 12.3 %copy-start.12 = (u32[256]{0:T(256)S(1)}, u32[256]{0:T(256)}, u32[]{:S(2)}) copy-start(u32[256]{0:T(256)} %constant.35) | copy-start | bytes 3076
  211.5 10.8 %all-to-all-start = ((bf16[32,2,10]{2,1,0:T(2,128)(2,1)}), bf16[32,2,10]{2,1,0:T(2,128)(2,1)S(1)}, u32[]{:S(2)}, u32[]{:S(2)}) async-start(bf16[32,2,10]{2,1,0:T(2,128)(2,1)} %convert_element_type.69), calls=%async_computation | async-start | bytes 32768 | tf_op jit(solution)/shard_map/all_to_all | solution.py:92
  215.3 339.8 %reduce-scatter.13.cloned.1.call-start = ((), (), s32[]{:S(2)}) async-start(), calls=%async_computation.15 | async-start | bytes 1179648
  496.3 117.0 %reduce-scatter.11.cloned.1.call-start = ((), (), s32[]{:S(2)}) async-start(), calls=%async_computation.14 | async-start | bytes 3538944 | tf_op jit(solution)/shard_map/reduce_scatter | solution.py:113
  503.8 162.3 %reduce-scatter.9.cloned.1.call-start = ((), (), s32[]{:S(2)}) async-start(), calls=%async_computation.13 | async-start | bytes 3538944 | tf_op jit(solution)/shard_map/reduce_scatter | solution.py:110
  511.7 6.5 copy-start.7
  518.2 1.0 copy-start.9
  518.2 200.8 %reduce-scatter.7.cloned.1.call-start = ((), (), s32[]{:S(2)}) async-start(), calls=%async_computation.12 | async-start | bytes 3538944 | tf_op jit(solution)/shard_map/reduce_scatter | solution.py:107
  525.9 1.9 copy-start.3
  527.8 2.8 copy-start.4
  527.8 2.8 copy-start.8
  536.4 33.0 %all-to-all-start.3 = ((bf16[32,2,10,2048]{3,1,2,0:T(2,128)(2,1)}), bf16[32,2,10,2048]{3,1,2,0:T(2,128)(2,1)S(1)}, u32[]{:S(2)}, u32[]{:S(2)}) async-start(bf16[32,2,10,2048]{3,1,2,0:T(2,128)(2,1)} %copy.122), calls=%async_computation.3 | async-start | bytes 5242880 | tf_op jit(solution)/shard_map/all_to_all | solution.py:98
  576.8 6.8 copy-start.6
  576.9 142.2 %copy-start.1 = (bf16[64,2048]{1,0:T(8,128)(2,1)S(1)}, bf16[64,2048]{1,0:T(8,128)(2,1)}, u32[]{:S(2)}) copy-start(bf16[64,2048]{1,0:T(8,128)(2,1)} %param.9) | copy-start | bytes 786436
Sparse Core Ops, SparseCore 0:
  9.9 51.7 all-gather.7
  63.5 49.1 all-gather.5
  114.5 65.6 all-gather.3
  208.2 285.9 all-reduce.2
  496.7 58.3 reduce-scatter.12
  558.2 55.0 reduce-scatter.10
  616.6 49.5 reduce-scatter.8
  669.5 49.4 reduce-scatter.6
where the time goes:
time: 738 us; the launch traced here: 726 us
  waiting for transfers between devices  551 us (75%)
  local copies, waits for them, and re-layouts  58 us (8%)
  matrix products  53.6 us (7%)
  starting transfers between devices  36.1 us (5%)
  between operations  15.6 us (2%)
  other arithmetic  11.5 us (2%)
    unnamed x10, waiting for transfers between devices  285 us
    all_to_all x1, waiting for transfers between devices, per_device(): lax.all_to_all(send_tokens, 'expert', split_axis=0, concat_axis=0, tiled=...  60.5 us
    reduce_scatter x1, waiting for transfers between devices, per_device(): lax.psum_scatter(up_term.astype(jnp.bfloat16), 'dp', scatter_dimension=1,...  52.8 us
    reduce_scatter x1, waiting for transfers between devices, per_device(): lax.psum_scatter(gate_term.astype(jnp.bfloat16), 'dp', scatter_dimension=...  52.8 us
    all_to_all x1, waiting for transfers between devices, per_device(): lax.all_to_all(send_grads, 'expert', split_axis=0, concat_axis=0, tiled=T...  40 us
    reduce_scatter x1, waiting for transfers between devices, per_device(): lax.psum_scatter(down_term.astype(jnp.bfloat16), 'dp', scatter_dimension=...  28.8 us
  transfers between devices with their start and end apart: 13, of which 11 were waited for; matrix products, arithmetic and copies ran while one was open for 15% of the time, Pallas kernels for 0%

commit v1 on v0

v1 whole, which is shorter than its diff:
```python
import jax
import jax.numpy as jnp
from jax import lax
from jax.experimental import pallas as pl
from jax.experimental.pallas import tpu as pltpu
from jax.sharding import Mesh
from jax.sharding import PartitionSpec as P

F32, BF16 = jnp.float32, jnp.bfloat16
AXES = ("zh", "core", "x", "y", "zl")
PLANE = ("x", "y")
CAP = 10
EXPERTS = 64
PLUS = [(i, (i + 1) % 4) for i in range(4)]
MINUS = [(i, (i + 3) % 4) for i in range(4)]
SWAP = [(0, 1), (1, 0)]


def mm(a, b, dims=((1,), (0,))):
    return lax.dot_general(a, b, (dims, ((), ())), preferred_element_type=F32)


def rolled(a, steps):
    q = a.shape[1] // 4
    out = a
    for i in range(1, 4):
        out = jnp.where(steps == i, jnp.concatenate([a[:, i * q :], a[:, : i * q]], axis=1), out)
    return out


def quad(a, other):
    pair = jnp.concatenate([a, other], axis=0)
    return jnp.concatenate([pair, lax.ppermute(pair, "core", SWAP)], axis=0)


def quad_sum(a):
    rows = a.shape[0] // 4
    a = a[: 2 * rows] + lax.ppermute(a[2 * rows :].astype(BF16), "core", SWAP).astype(F32)
    return a[:rows] + lax.ppermute(a[rows:].astype(BF16), "zl", SWAP).astype(F32)


def both_ways(up, down):
    return lax.ppermute(up, "zh", PLUS), lax.ppermute(down, "zh", MINUS)


def scatter_first(a):
    h = a.shape[0] // 8
    return both_ways(a[3 * h : 5 * h], a[5 * h : 7 * h])


def scatter_second(a, got_up, got_down):
    h = a.shape[0] // 8
    up = (a[2 * h : 3 * h].astype(F32) + got_up[h:].astype(F32)).astype(BF16)
    down = (a[7 * h :].astype(F32) + got_down[:h].astype(F32)).astype(BF16)
    return both_ways(*lax.optimization_barrier((up, down)))


def scatter_end(a, first, second):
    h = a.shape[0] // 8
    low = a[:h].astype(F32) + second[0].astype(F32) + first[1][h:].astype(F32)
    high = a[h : 2 * h].astype(F32) + first[0][:h].astype(F32) + second[1].astype(F32)
    return jnp.concatenate([low, high], axis=0).astype(BF16)


def a2a(a, axes):
    return lax.all_to_all(a, axes, split_axis=0, concat_axis=0, tiled=True)


def alone(ids, *arrays):
    return lax.cond(
        ids[0, 0] >= 0, lambda *v: tuple(a2a(w, PLANE) for w in v), lambda *v: v, *arrays
    )


def forward_kernel(x, s, own, after, far_lo, far_hi, prev, pre_grad, share, g_pre, g_down, hidden):
    hid = own.shape[1] // 3
    rows = x.shape[0] // 2
    pieces = []
    at = 0
    for w in (own, after, far_lo, far_hi, prev):
        pieces.append((w, at))
        at += w.shape[0]

    @pl.loop(0, 2)
    def _(i):
        tile = pl.ds(pl.multiple_of(i * rows, rows), rows)
        pre = jnp.zeros((rows, 2 * hid), F32)
        for w, at in pieces:
            pre += mm(x[tile, at : at + w.shape[0]], w[:, : 2 * hid])
        hgrad = jnp.zeros((rows, hid), F32)
        for w, at in pieces:
            hgrad += mm(s[tile, at : at + w.shape[0]], w[:, 2 * hid :])
        gate_pre, up_pre = pre[:, :hid], pre[:, hid:]
        sg = jax.nn.sigmoid(gate_pre)
        act = gate_pre * sg
        h = (act * up_pre).astype(BF16)
        hidden[tile, :] = h
        share[tile, :] = jnp.sum(h.astype(F32) * hgrad, axis=1, keepdims=True)
        slope = sg * (1.0 + gate_pre * (1.0 - sg))
        pre_grad[tile, :hid] = (hgrad * up_pre * slope).astype(BF16)
        pre_grad[tile, hid:] = (hgrad * act).astype(BF16)

    q = x.shape[1] // 4

    @pl.loop(0, 4)
    def _(j):
        cols = pl.ds(pl.multiple_of(j * q, q), q)
        g_pre[cols, :] = mm(x[:, cols], pre_grad[...], ((0,), (0,))).astype(BF16)
        g_down[cols, :] = mm(s[:, cols], hidden[...], ((0,), (0,))).astype(BF16)


def back_kernel(pre_grad, own, after, far_lo, far_hi, prev, back):
    hid = own.shape[1] // 3
    rows = pre_grad.shape[0] // 2

    @pl.loop(0, 2)
    def _(i):
        tile = pl.ds(pl.multiple_of(i * rows, rows), rows)
        at = 0
        for w in (own, after, far_lo, far_hi, prev):
            n = w.shape[0]
            back[tile, at : at + n] = mm(
                pre_grad[tile, :], w[:, : 2 * hid], ((1,), (1,))
            ).astype(BF16)
            at += n


def call(kernel, outs, scratch, *args):
    vmem = pl.BlockSpec(memory_space=pltpu.VMEM)
    return pl.pallas_call(
        kernel,
        out_shape=outs,
        in_specs=[vmem] * len(args),
        out_specs=[vmem] * len(outs),
        scratch_shapes=scratch,
        compiler_params=pltpu.CompilerParams(vmem_limit_bytes=48 * 2**20),
    )(*args)


def per_device(tokens, out_grad, ids, pos, keep, router, w_gate, w_up, w_down):
    tok, width = tokens.shape
    hid = w_gate.shape[2]
    piece = w_gate.shape[1]
    zh, core, zl = (lax.axis_index(n) for n in ("zh", "core", "zl"))
    chips = 16
    slots = chips * 4 * CAP

    experts = jnp.arange(EXPERTS, dtype=jnp.int32)
    hit = ids.T[None] == experts[:, None, None]
    chosen = jnp.any(hit, axis=1)
    held = hit & (keep.T > 0)[None]
    slot_t = (jnp.sum(jnp.where(held, pos.T[None] + 1, 0), axis=1) - 1).astype(BF16)
    logits = mm(router, tokens, ((0,), (1,)))
    sig = jax.nn.sigmoid(logits)
    prob = jnp.where(chosen, sig, 0.0)
    gate = prob / jnp.sum(prob, axis=0, keepdims=True)

    def mine(table):
        parts = table.reshape(chips, 4, table.shape[1])
        which = 2 * zl + core
        out = parts[:, 0]
        for i in range(1, 4):
            out = jnp.where(which == i, parts[:, i], out)
        return out

    zeros = jnp.zeros((tok, EXPERTS), BF16)
    tok_e = jnp.concatenate([rolled(tokens, zh), slot_t.T, zeros], axis=1)
    grad_e = jnp.concatenate([rolled(out_grad, zh), gate.astype(BF16).T, zeros], axis=1)
    tok_z, grad_z = (lax.ppermute(v, "zl", SWAP) for v in (tok_e, grad_e))
    shard = a2a(jnp.concatenate([w_gate, w_up, jnp.swapaxes(w_down, 1, 2)], axis=2), "core")
    shard, tok_z, grad_z = lax.optimization_barrier((shard, tok_z, grad_z))
    tok_q, grad_q = quad(tok_e, tok_z), quad(grad_e, grad_z)
    slot_q = mine(tok_q[:, width : width + EXPERTS].T)
    gate_q = mine(grad_q[:, width : width + EXPERTS].T)
    tok_q, grad_q = tok_q[:, :width], grad_q[:, :width]

    place = jnp.arange(4 * CAP, dtype=jnp.int32)
    block = jnp.arange(4 * tok, dtype=jnp.int32) // tok
    match = (slot_q.astype(jnp.int32)[:, None, :] == (place % CAP)[None, :, None]) & (
        (place // CAP)[:, None] == block[None, :]
    )
    pick = jnp.where(match, 1.0, 0.0).astype(BF16).reshape(slots, 4 * tok)
    pick_g = jnp.where(match, gate_q.astype(F32)[:, None, :], 0.0).astype(BF16).reshape(slots, 4 * tok)

    send_x = mm(pick, tok_q).astype(BF16).reshape(chips, 4 * CAP, width)
    send_s = mm(pick_g, grad_q).astype(BF16).reshape(chips, 4 * CAP, width)
    shard = shard.reshape(2 * piece, 3 * hid)
    after_before = both_ways(shard, shard)
    (x,) = alone(ids, send_x)
    x, send_s, (before, after) = lax.optimization_barrier((x, send_s, after_before))
    far = both_ways(before[:piece], after[piece:])
    (s,) = alone(ids, send_s)
    s, far = lax.optimization_barrier((s, far))
    x, s = x.reshape(slots, width), s.reshape(slots, width)
    weight = (shard, after, *far, before)

    of = jax.ShapeDtypeStruct
    pre_grad, share, g_pre, g_down = call(
        forward_kernel,
        (
            of((slots, 2 * hid), BF16),
            of((slots, 1), F32),
            of((width, 2 * hid), BF16),
            of((width, hid), BF16),
        ),
        [pltpu.VMEM((slots, hid), BF16)],
        x,
        s,
        *weight,
    )
    w_grads = g_pre, g_down

    share = share.reshape(chips, 2, 2, CAP)
    share = jnp.where(core == 0, share, share[:, ::-1])
    share = jnp.where(zl == 0, share, share[:, :, ::-1])
    share = jnp.swapaxes(share, 0, 1)
    share = a2a(share.reshape(64, 1, CAP), ("core", "x", "y", "zl"))
    share = share.reshape(2, 2 * chips, CAP).swapaxes(0, 1).reshape(EXPERTS, CAP)
    share, w_grads = lax.optimization_barrier((share, w_grads))
    firsts = [scatter_first(g) for g in w_grads]
    taken = jnp.zeros((EXPERTS, tok), F32)
    for i in range(CAP):
        taken += jnp.where(slot_t == i, share[:, i : i + 1], 0.0)
    mean = jnp.sum(taken, axis=0, keepdims=True)
    dlogits = jnp.where(chosen, (taken - gate * mean) * (1.0 - sig), 0.0).astype(BF16)
    term = mm(dlogits, tokens).astype(BF16).reshape(32, 2, width)
    own_part = mm(dlogits, router, ((0,), (1,)))

    (back,) = call(back_kernel, (of((slots, width), BF16),), [], pre_grad, *weight)
    back, term, own_part = lax.optimization_barrier((back, term, own_part))
    (back,) = alone(ids, back.reshape(chips, 4 * CAP, width))
    back, firsts, term = lax.optimization_barrier((back, firsts, term))
    seconds = [scatter_second(g, *f) for g, f in zip(w_grads, firsts)]
    part = quad_sum(mm(pick, back.reshape(slots, width), ((0,), (0,))))
    grad_tokens = (rolled(part, (4 - zh) % 4) + own_part).astype(BF16)
    term = jnp.sum(a2a(term, PLANE + ("zl",)).astype(F32), axis=0)
    term = term.reshape(2, 8, width // 8).swapaxes(0, 1)
    grad_router = jnp.sum(a2a(term, ("zh", "core")), axis=0)

    g_gate_up, g_down = (
        a2a(scatter_end(*g).reshape(2, piece, g[0].shape[1]), "core")
        for g in zip(w_grads, firsts, seconds)
    )
    return (
        grad_tokens,
        g_gate_up[:, :, :hid],
        g_gate_up[:, :, hid:],
        jnp.swapaxes(g_down, 1, 2),
        grad_router,
    )


def solution(mesh):
    grid = Mesh(mesh.devices.reshape(4, 2, 4, 4, 2), AXES)
    dp, ex = ("zh", "core"), ("x", "y", "zl")
    rows = P(AXES, None)
    return jax.shard_map(
        per_device,
        mesh=grid,
        in_specs=(rows,) * 5 + (P(), P(ex, dp, None), P(ex, dp, None), P(ex, None, dp)),
        out_specs=(rows, P(ex, dp, None), P(ex, dp, None), P(ex, None, dp), P(ex, dp)),
        check_vma=False,
    )
```

time: 738 us -> 286 us (0.39); the launches traced: 726 us -> 284 us
  waiting for transfers between devices: 551 us -> 19.7 us
  blocking collectives: 0 us -> 117 us
  matrix products: 53.6 us -> 9.97 us
  starting transfers between devices: 36.1 us -> 66.3 us
  local copies, waits for them, and re-layouts: 58 us -> 29.2 us
  Pallas kernels: 0 us -> 19.1 us
  between operations: 15.6 us -> 1.98 us
  other arithmetic: 11.5 us -> 21.5 us
    unnamed x10 -> x0, waiting for transfers between devices: 285 us -> none
    reduce_scatter x3 -> x0, waiting for transfers between devices: 134 us -> none  [the longest x1 52.8 us: per_device(): lax.psum_scatter(up_term.astype(jnp.bfloat16), 'dp', scatter_dimension=1,...]
    all_to_all x0 -> x4, blocking collectives: none -> 117 us  [a2a(): return lax.all_to_all(a, axes, split_axis=0, concat_axis=0, tiled=True)]
    all_to_all x5, waiting for transfers between devices: 126 us -> 10.7 us  [a2a(): return lax.all_to_all(a, axes, split_axis=0, concat_axis=0, tiled=True)]
    dot_general x12 -> x6, matrix products: 53.6 us -> 9.97 us  [mm(): return lax.dot_general(a, b, (dims, ((), ())), preferred_element_type=F32)]
    ppermute x0 -> x18, starting transfers between devices: none -> 32 us  [the longest x12 24 us: both_ways(): return (lax.ppermute(up, 'zh', PLUS), lax.ppermute(down, 'zh', MINUS))]
    gather x6 -> x0, local copies, waits for them, and re-layouts: 19.2 us -> none  [the longest x2 6.22 us: per_device(): out_grad[slot_owner]]
    pallas_call x0 -> x2, Pallas kernels: none -> 19.1 us  [call(): pl.pallas_call(kernel, out_shape=outs, in_specs=[vmem] * len(args), out_s...]
  transfers between devices with their start and end apart: 13 -> 23, of which waited for: 11 -> 5; matrix products, arithmetic and copies ran while one was open for 15% -> 13% of each run, Pallas kernels for 0% -> 2%
where the time goes in v1:
time: 286 us; the launch traced here: 284 us
  blocking collectives  117 us (41%)
  starting transfers between devices  66.3 us (23%)
  local copies, waits for them, and re-layouts  29.2 us (10%)
  other arithmetic  21.5 us (8%)
  waiting for transfers between devices  19.7 us (7%)
  Pallas kernels  19.1 us (7%)
  matrix products  9.97 us (3%)
    all_to_all x4, blocking collectives, a2a(): return lax.all_to_all(a, axes, split_axis=0, concat_axis=0, tiled=True)  117 us
    all_to_all x5, starting transfers between devices, a2a(): return lax.all_to_all(a, axes, split_axis=0, concat_axis=0, tiled=True)  34.3 us
    ppermute x12, starting transfers between devices, both_ways(): return (lax.ppermute(up, 'zh', PLUS), lax.ppermute(down, 'zh', MINUS))  24 us
    pallas_call x2, Pallas kernels, call(): pl.pallas_call(kernel, out_shape=outs, in_specs=[vmem] * len(args), out_s...  19.1 us
    all_to_all x5, waiting for transfers between devices, a2a(): return lax.all_to_all(a, axes, split_axis=0, concat_axis=0, tiled=True)  10.7 us
    dot_general x6, matrix products, mm(): return lax.dot_general(a, b, (dims, ((), ())), preferred_element_type=F32)  9.97 us
    ppermute x12, waiting for transfers between devices, both_ways(): return (lax.ppermute(up, 'zh', PLUS), lax.ppermute(down, 'zh', MINUS))  8.62 us
    unnamed x63, local copies, waits for them, and re-layouts  6.36 us
  transfers between devices with their start and end apart: 23, of which 5 were waited for; matrix products, arithmetic and copies ran while one was open for 13% of the time, Pallas kernels for 2%

profile of v1, /device:TPU:1, one launch (start us, length us, event | category | flops | bytes accessed | tf_op | source)
XLA Modules:
  0.0 284.2 jit_solution(8881162585966040366)
XLA Ops:
  6.9 2.6 collective-permute-start.1
  12.1 6.4 %all-to-all-start.3 = ((bf16[2,256,1152]{1,2,0:T(8,128)(2,1)}), bf16[2,256,1152]{1,2,0:T(8,128)(2,1)S(1)}, u32[]{:S(2)}, u32[]{:S(2)}) async-start(bf16[2,256,1152]{1,2,0:T(8,128)(2,1)} %pad_maximum_fusion), calls=%async_computation.3 | async-start | bytes 2359296 | tf_op jit(solution)/shard_map/all_to_all | solution.py:66
  21.6 2.3 collective-permute-start.3
  25.5 3.1 %collective-permute-start.4 = (bf16[512,1152]{1,0:T(8,128)(2,1)S(1)}, bf16[512,1152]{1,0:T(8,128)(2,1)S(1)}, u32[]{:S(2)}, u32[]{:S(2)}) collective-permute-start(bf16[512,1152]{1,0:T(8,128)(2,1)S(1)} %bitcast.70), channel_id=1, source_target_pairs={{0,64},{64,128},{128,192},{192,0},{1,65},{65,129},{129,193},{193,1... | collective-permute-start | bytes 3538952 | tf_op jit(solution)/shard_map/ppermute | solution.py:43
  28.6 2.9 %collective-permute-start.5 = (bf16[512,1152]{1,0:T(8,128)(2,1)S(1)}, bf16[512,1152]{1,0:T(8,128)(2,1)}, u32[]{:S(2)}, u32[]{:S(2)}) collective-permute-start(bf16[512,1152]{1,0:T(8,128)(2,1)S(1)} %bitcast.71), channel_id=1, source_target_pairs={{0,192},{64,0},{128,64},{192,128},{1,193},{65,1},{129,65},{193,129... | collective-permute-start | bytes 3538952 | tf_op jit(solution)/shard_map/ppermute | solution.py:43
  38.0 3.5 %convolution_convert_fusion.1 = bf16[640,2048]{1,0:T(8,128)(2,1)} fusion(bf16[640,256]{1,0:T(8,128)(2,1)S(1)} %select_convert_fusion, bf16[128,2176]{1,0:T(8,128)(2,1)} %collective-permute-done.2, bf16[64,2176]{1,0:T(8,128)(2,1)} %copy-done.12, bf16[64,2176]{1,0:T(8,128)(2,1)S(1)} %concatenate.61), kind=kOutput, calls=%fused_computation.1 | convolution fusion | flops 675545088 | bytes 4063232 | tf_op jit(solution)/shard_map/dot_general | solution.py:20
  41.5 41.1 %conditional.3 = (bf16[16,40,2048]{2,1,0:T(8,128)(2,1)}) conditional(s32[]{:T(128)} %bitcast.7, bf16[16,40,2048]{2,1,0:T(8,128)(2,1)} %bitcast.76, bf16[16,40,2048]{2,1,0:T(8,128)(2,1)} %bitcast.77), branch_computations={%region_3.4_spmd, %region_4.5_spmd} | conditional | bytes 15728676 | solution.py:70
  43.3 39.4 %all_to_all.42 = bf16[16,40,2048]{2,1,0:T(8,128)(2,1)} all-to-all(bf16[16,40,2048]{2,1,0:T(8,128)(2,1)S(1)} %copy-done.4), channel_id=1, replica_groups=mesh['zh'=4,'core'=2,'x'=4,'y'=4,'zl'=2] {'x','y'}, dimensions={0} | all-to-all | bytes 5242880 | tf_op jit(solution)/shard_map/cond/branch_1_fun/all_to_all | solution.py:66
  82.7 3.5 %convolution_convert_fusion = bf16[640,2048]{1,0:T(8,128)(2,1)} fusion(bf16[640,256]{1,0:T(8,128)(2,1)} %fusion.5, bf16[128,2176]{1,0:T(8,128)(2,1)} %collective-permute-done.3, bf16[64,2176]{1,0:T(8,128)(2,1)S(1)} %collective-permute-done.1, bf16[64,2176]{1,0:T(8,128)(2,1)S(1)} %concatenate.66), kind=kOutput, calls=%fused_computation | convolution fusion | flops 675545088 | bytes 4063232 | tf_op jit(solution)/shard_map/dot_general | solution.py:20
  88.2 1.9 slice.237
  90.1 2.5 collective-permute-start.7
  92.6 38.0 %conditional.4 = (bf16[16,40,2048]{2,1,0:T(8,128)(2,1)}) conditional(s32[]{:T(128)} %bitcast.7, bf16[16,40,2048]{2,1,0:T(8,128)(2,1)} %bitcast.79, bf16[16,40,2048]{2,1,0:T(8,128)(2,1)} %bitcast.80), branch_computations={%region_5.6_spmd, %region_6.7_spmd} | conditional | bytes 15728676 | solution.py:70
  94.3 36.3 %all_to_all.43 = bf16[16,40,2048]{2,1,0:T(8,128)(2,1)} all-to-all(bf16[16,40,2048]{2,1,0:T(8,128)(2,1)S(1)} %copy-done.5), channel_id=1, replica_groups=mesh['zh'=4,'core'=2,'x'=4,'y'=4,'zl'=2] {'x','y'}, dimensions={0} | all-to-all | bytes 5242880 | tf_op jit(solution)/shard_map/cond/branch_1_fun/all_to_all | solution.py:66
  130.6 13.7 %shard_map.128 = (bf16[640,768]{1,0:T(8,128)(2,1)S(1)}, f32[640,1]{1,0:T(8,128)S(1)}, bf16[2048,768]{1,0:T(8,128)(2,1)}, bf16[2048,384]{1,0:T(8,128)(2,1)}) custom-call(bf16[640,2048]{1,0:T(8,128)(2,1)} %bitcast.78, bf16[640,2048]{1,0:T(8,128)(2,1)} %bitcast.81, bf16[512,1152]{1,0:T(8,128)(2,1)S(1)} %bitcast.72, ...), custom_call_target="tpu_custom_call" | custom-call | tf_op jit(solution)/shard_map/pallas_call | solution.py:130
  147.6 7.3 %all-to-all-start.4 = ((f32[64,1,10]{2,1,0:T(1,128)}), f32[64,1,10]{2,1,0:T(1,128)S(1)}, u32[]{:S(2)}, u32[]{:S(2)}) async-start(f32[64,1,10]{2,1,0:T(1,128)} %bitcast.19), calls=%async_computation.4 | async-start | bytes 65536 | tf_op jit(solution)/shard_map/all_to_all | solution.py:66
  156.2 5.3 %shard_map.129 = bf16[640,2048]{1,0:T(8,128)(2,1)} custom-call(bf16[640,768]{1,0:T(8,128)(2,1)S(1)} %copy-done.2, bf16[512,1152]{1,0:T(8,128)(2,1)S(1)} %bitcast.73, bf16[512,1152]{1,0:T(8,128)(2,1)} %collective-permute-done.5.after, bf16[256,1152]{1,0:T(8,128)(2,1)S(1)} %collective-permute-done.6.far_lo, bf16[256,1152]{1,0:T(8,128)(2,1)} %collective-permute-done.7.far_hi, ...), custom_call_target="tpu_custom_call" | custom-call | tf_op jit(solution)/shard_map/pallas_call | solution.py:130
  162.5 2.8 fusion.25
  165.3 2.0 collective-permute-start.8
  170.6 2.8 collective-permute-start.11
  175.4 37.4 %conditional.5 = (bf16[16,40,2048]{2,1,0:T(8,128)(2,1)S(1)}) conditional(s32[]{:T(128)} %bitcast.7, bf16[16,40,2048]{2,1,0:T(8,128)(2,1)S(1)} %bitcast.74, bf16[16,40,2048]{2,1,0:T(8,128)(2,1)S(1)} %bitcast.75), branch_computations={%region_8.9_spmd, %region_9.10_spmd} | conditional | bytes 10485768 | solution.py:70
  175.6 37.1 %all_to_all.44 = bf16[16,40,2048]{2,1,0:T(8,128)(2,1)S(1)} all-to-all(bf16[16,40,2048]{2,1,0:T(8,128)(2,1)S(1)} %copy.92), channel_id=1, replica_groups=mesh['zh'=4,'core'=2,'x'=4,'y'=4,'zl'=2] {'x','y'}, dimensions={0} | all-to-all | bytes 5242880 | tf_op jit(solution)/shard_map/cond/branch_1_fun/all_to_all | solution.py:66
  212.8 8.6 %collective-permute-done.11 = bf16[512,384]{1,0:T(8,128)(2,1)} collective-permute-done((bf16[512,384]{1,0:T(8,128)(2,1)}, bf16[512,384]{1,0:T(8,128)(2,1)}, u32[]{:S(2)}, u32[]{:S(2)}) %collective-permute-start.11) | collective-permute-done | bytes 393248 | tf_op jit(solution)/shard_map/ppermute | solution.py:43
  224.4 2.0 collective-permute-start.17
  226.4 2.4 add_convert_fusion.2
  229.2 3.2 %collective-permute-start.15 = (bf16[256,768]{1,0:T(8,128)(2,1)}, bf16[256,768]{1,0:T(8,128)(2,1)}, u32[]{:S(2)}, u32[]{:S(2)}) collective-permute-start(bf16[256,768]{1,0:T(8,128)(2,1)} %get-tuple-element.74), channel_id=1, source_target_pairs={{0,192},{64,0},{128,64},{192,128},{1,193},{65,1},{129,65},{193,129... | collective-permute-start | bytes 1179656 | tf_op jit(solution)/shard_map/ppermute | solution.py:43
  239.2 3.7 %all_to_all.45 = bf16[2,256,384]{1,2,0:T(8,128)(2,1)S(1)} all-to-all(bf16[2,256,384]{1,2,0:T(8,128)(2,1)S(1)} %copy.70), channel_id=1, replica_groups=mesh['zh'=4,'core'=2,'x'=4,'y'=4,'zl'=2] {'core'}, dimensions={0} | all-to-all | bytes 786432 | tf_op jit(solution)/shard_map/all_to_all | solution.py:66
  242.8 10.5 %all-to-all-start.7 = ((bf16[32,2,2048]{2,1,0:T(2,128)(2,1)}), bf16[32,2,2048]{2,1,0:T(2,128)(2,1)S(1)}, u32[]{:S(2)}, u32[]{:S(2)}) async-start(bf16[32,2,2048]{2,1,0:T(2,128)(2,1)} %reshape.163), calls=%async_computation.7 | async-start | bytes 524288 | tf_op jit(solution)/shard_map/all_to_all | solution.py:66
  253.3 2.0 add_convert_fusion.1
  258.4 3.7 %all-to-all-done.7 = bf16[32,2,2048]{2,1,0:T(2,128)(2,1)S(1)} async-done(((bf16[32,2,2048]{2,1,0:T(2,128)(2,1)}), bf16[32,2,2048]{2,1,0:T(2,128)(2,1)S(1)}, u32[]{:S(2)}, u32[]{:S(2)}) %all-to-all-start.7) | async-done | bytes 262176 | tf_op jit(solution)/shard_map/all_to_all | solution.py:66
  262.8 5.1 %all-to-all-start.5 = ((bf16[2,256,768]{2,1,0:T(8,128)(2,1)}), bf16[2,256,768]{2,1,0:T(8,128)(2,1)S(1)}, u32[]{:S(2)}, u32[]{:S(2)}) async-start(bf16[2,256,768]{2,1,0:T(8,128)(2,1)} %bitcast.26), calls=%async_computation.5 | async-start | bytes 1572864 | tf_op jit(solution)/shard_map/all_to_all | solution.py:66
  269.7 5.1 %all-to-all-start.8 = ((f32[8,2,256]{2,1,0:T(2,128)}), f32[8,2,256]{2,1,0:T(2,128)S(1)}, u32[]{:S(2)}, u32[]{:S(2)}) async-start(f32[8,2,256]{2,1,0:T(2,128)} %bitcast.30), calls=%async_computation.8 | async-start | bytes 32768 | tf_op jit(solution)/shard_map/all_to_all | solution.py:66
  275.7 6.1 %all-to-all-done.8 = f32[8,2,256]{2,1,0:T(2,128)S(1)} async-done(((f32[8,2,256]{2,1,0:T(2,128)}), f32[8,2,256]{2,1,0:T(2,128)S(1)}, u32[]{:S(2)}, u32[]{:S(2)}) %all-to-all-start.8) | async-done | bytes 16416 | tf_op jit(solution)/shard_map/all_to_all | solution.py:66
  (168 shorter events, 54.5 us)
Async XLA Ops:
  0.7 8.8 %copy-start.6 = (bf16[64,2048]{1,0:T(8,128)(2,1)S(1)}, bf16[64,2048]{1,0:T(8,128)(2,1)}, u32[]{:S(2)}) copy-start(bf16[64,2048]{1,0:T(8,128)(2,1)} %param.15) | copy-start | bytes 786436
  6.9 13.5 %collective-permute-start.1 = (bf16[64,2176]{1,0:T(8,128)(2,1)S(1)}, bf16[64,2176]{1,0:T(8,128)(2,1)S(1)}, u32[]{:S(2)}, u32[]{:S(2)}) collective-permute-start(bf16[64,2176]{1,0:T(8,128)(2,1)S(1)} %concatenate.66), channel_id=1, source_target_pairs={{0,1},{1,0},{2,3},{3,2},{4,5},{5,4},{6,7},{7,6},{8,9},{9,8},{10,11... | collective-permute-start | bytes 835592 | tf_op jit(solution)/shard_map/ppermute | solution.py:169
  10.5 10.2 %collective-permute-start = (bf16[64,2176]{1,0:T(8,128)(2,1)S(1)}, bf16[64,2176]{1,0:T(8,128)(2,1)S(1)}, u32[]{:S(2)}, u32[]{:S(2)}) collective-permute-start(bf16[64,2176]{1,0:T(8,128)(2,1)S(1)} %concatenate.61), channel_id=1, source_target_pairs={{0,1},{1,0},{2,3},{3,2},{4,5},{5,4},{6,7},{7,6},{8,9},{9,8},{10,11... | collective-permute-start | bytes 835592 | tf_op jit(solution)/shard_map/ppermute | solution.py:169
  12.1 8.2 %all-to-all-start.3 = ((bf16[2,256,1152]{1,2,0:T(8,128)(2,1)}), bf16[2,256,1152]{1,2,0:T(8,128)(2,1)S(1)}, u32[]{:S(2)}, u32[]{:S(2)}) async-start(bf16[2,256,1152]{1,2,0:T(8,128)(2,1)} %pad_maximum_fusion), calls=%async_computation.3 | async-start | bytes 2359296 | tf_op jit(solution)/shard_map/all_to_all | solution.py:66
  21.6 10.6 %collective-permute-start.3 = (bf16[128,2176]{1,0:T(8,128)(2,1)}, bf16[128,2176]{1,0:T(8,128)(2,1)}, u32[]{:S(2)}, u32[]{:S(2)}) collective-permute-start(bf16[128,2176]{1,0:T(8,128)(2,1)} %pad_maximum_fusion.11), channel_id=1, source_target_pairs={{0,32},{32,0},{1,33},{33,1},{2,34},{34,2},{3,35},{35,3},{4,36},{36... | collective-permute-start | bytes 1671176 | tf_op jit(solution)/shard_map/ppermute | solution.py:33
  24.8 8.3 %collective-permute-start.2 = (bf16[128,2176]{1,0:T(8,128)(2,1)}, bf16[128,2176]{1,0:T(8,128)(2,1)}, u32[]{:S(2)}, u32[]{:S(2)}) collective-permute-start(bf16[128,2176]{1,0:T(8,128)(2,1)} %pad_maximum_fusion.10), channel_id=1, source_target_pairs={{0,32},{32,0},{1,33},{33,1},{2,34},{34,2},{3,35},{35,3},{4,36},{36... | collective-permute-start | bytes 1671176 | tf_op jit(solution)/shard_map/ppermute | solution.py:33
  25.5 60.6 %collective-permute-start.4 = (bf16[512,1152]{1,0:T(8,128)(2,1)S(1)}, bf16[512,1152]{1,0:T(8,128)(2,1)S(1)}, u32[]{:S(2)}, u32[]{:S(2)}) collective-permute-start(bf16[512,1152]{1,0:T(8,128)(2,1)S(1)} %bitcast.70), channel_id=1, source_target_pairs={{0,64},{64,128},{128,192},{192,0},{1,65},{65,129},{129,193},{193,1... | collective-permute-start | bytes 3538952 | tf_op jit(solution)/shard_map/ppermute | solution.py:43
  28.6 57.6 %collective-permute-start.5 = (bf16[512,1152]{1,0:T(8,128)(2,1)S(1)}, bf16[512,1152]{1,0:T(8,128)(2,1)}, u32[]{:S(2)}, u32[]{:S(2)}) collective-permute-start(bf16[512,1152]{1,0:T(8,128)(2,1)S(1)} %bitcast.71), channel_id=1, source_target_pairs={{0,192},{64,0},{128,64},{192,128},{1,193},{65,1},{129,65},{193,129... | collective-permute-start | bytes 3538952 | tf_op jit(solution)/shard_map/ppermute | solution.py:43
  87.1 43.5 %collective-permute-start.6 = (bf16[256,1152]{1,0:T(8,128)(2,1)}, bf16[256,1152]{1,0:T(8,128)(2,1)S(1)}, u32[]{:S(2)}, u32[]{:S(2)}) collective-permute-start(bf16[256,1152]{1,0:T(8,128)(2,1)} %slice.236), channel_id=1, source_target_pairs={{0,64},{64,128},{128,192},{192,0},{1,65},{65,129},{129,193},{193,1... | collective-permute-start | bytes 1769480 | tf_op jit(solution)/shard_map/ppermute | solution.py:43
  90.1 40.5 %collective-permute-start.7 = (bf16[256,1152]{1,0:T(8,128)(2,1)}, bf16[256,1152]{1,0:T(8,128)(2,1)}, u32[]{:S(2)}, u32[]{:S(2)}) collective-permute-start(bf16[256,1152]{1,0:T(8,128)(2,1)} %slice.237), channel_id=1, source_target_pairs={{0,192},{64,0},{128,64},{192,128},{1,193},{65,1},{129,65},{193,129... | collective-permute-start | bytes 1769480 | tf_op jit(solution)/shard_map/ppermute | solution.py:43
  147.6 14.7 %all-to-all-start.4 = ((f32[64,1,10]{2,1,0:T(1,128)}), f32[64,1,10]{2,1,0:T(1,128)S(1)}, u32[]{:S(2)}, u32[]{:S(2)}) async-start(f32[64,1,10]{2,1,0:T(1,128)} %bitcast.19), calls=%async_computation.4 | async-start | bytes 65536 | tf_op jit(solution)/shard_map/all_to_all | solution.py:66
  162.4 11.3 %copy-start.18 = (s32[64,64]{0,1:T(8,128)S(1)}, s32[64,64]{0,1:T(8,128)}, u32[]{:S(2)}) copy-start(s32[64,64]{0,1:T(8,128)} %copy-done.17) | copy-start | bytes 49156
  162.4 11.5 %copy-start.7 = (bf16[64,2048]{1,0:T(8,128)(2,1)S(1)}, bf16[64,2048]{1,0:T(8,128)(2,1)}, u32[]{:S(2)}) copy-start(bf16[64,2048]{1,0:T(8,128)(2,1)} %param.15) | copy-start | bytes 786436
  162.4 11.5 %copy-start.20 = (f32[64,64]{0,1:T(8,128)S(1)}, f32[64,64]{0,1:T(8,128)}, u32[]{:S(2)}) copy-start(f32[64,64]{0,1:T(8,128)} %copy-done.19) | copy-start | bytes 49156
  162.5 11.5 %copy-start.23 = (pred[64,64]{0,1:T(32,128)(4,1)S(1)}, pred[64,64]{0,1:T(32,128)(4,1)}, u32[]{:S(2)}) copy-start(pred[64,64]{0,1:T(32,128)(4,1)} %copy-done.22) | copy-start | bytes 12292
  162.5 11.5 %copy-start.28 = (f32[64]{0:T(128)S(1)}, f32[64]{0:T(128)}, u32[]{:S(2)}) copy-start(f32[64]{0:T(128)} %copy-done.27) | copy-start | bytes 772
  165.2 10.2 %copy-start.3 = (bf16[640,2048]{1,0:T(8,128)(2,1)S(1)}, bf16[640,2048]{1,0:T(8,128)(2,1)}, u32[]{:S(2)}) copy-start(bf16[640,2048]{1,0:T(8,128)(2,1)} %shard_map.129) | copy-start | bytes 7864324
  165.3 56.1 %collective-permute-start.8 = (bf16[512,768]{1,0:T(8,128)(2,1)}, bf16[512,768]{1,0:T(8,128)(2,1)}, u32[]{:S(2)}, u32[]{:S(2)}) collective-permute-start(bf16[512,768]{1,0:T(8,128)(2,1)} %get-tuple-element.97), channel_id=1, source_target_pairs={{0,64},{64,128},{128,192},{192,0},{1,65},{65,129},{129,193},{193,1... | collective-permute-start | bytes 2359304 | tf_op jit(solution)/shard_map/ppermute | solution.py:43
  167.3 54.1 %collective-permute-start.9 = (bf16[512,768]{1,0:T(8,128)(2,1)}, bf16[512,768]{1,0:T(8,128)(2,1)}, u32[]{:S(2)}, u32[]{:S(2)}) collective-permute-start(bf16[512,768]{1,0:T(8,128)(2,1)} %get-tuple-element.96), channel_id=1, source_target_pairs={{0,192},{64,0},{128,64},{192,128},{1,193},{65,1},{129,65},{193,129... | collective-permute-start | bytes 2359304 | tf_op jit(solution)/shard_map/ppermute | solution.py:43
  169.8 43.0 %collective-permute-start.10 = (bf16[512,384]{1,0:T(8,128)(2,1)}, bf16[512,384]{1,0:T(8,128)(2,1)}, u32[]{:S(2)}, u32[]{:S(2)}) collective-permute-start(bf16[512,384]{1,0:T(8,128)(2,1)} %get-tuple-element.103), channel_id=1, source_target_pairs={{0,64},{64,128},{128,192},{192,0},{1,65},{65,129},{129,193},{193,1... | collective-permute-start | bytes 1179656 | tf_op jit(solution)/shard_map/ppermute | solution.py:43
  170.6 50.8 %collective-permute-start.11 = (bf16[512,384]{1,0:T(8,128)(2,1)}, bf16[512,384]{1,0:T(8,128)(2,1)}, u32[]{:S(2)}, u32[]{:S(2)}) collective-permute-start(bf16[512,384]{1,0:T(8,128)(2,1)} %get-tuple-element.102), channel_id=1, source_target_pairs={{0,192},{64,0},{128,64},{192,128},{1,193},{65,1},{129,65},{193,129... | collective-permute-start | bytes 1179656 | tf_op jit(solution)/shard_map/ppermute | solution.py:43
  212.8 19.6 %copy-start.21 = (pred[40,256]{1,0:T(8,128)(4,1)S(1)}, pred[40,256]{1,0:T(8,128)(4,1)}, u32[]{:S(2)}) copy-start(pred[40,256]{1,0:T(8,128)(4,1)} %broadcast_compare_fusion) | copy-start | bytes 30724
  212.8 19.6 %copy-start.26 = (s32[40]{0:T(128)S(1)}, s32[40]{0:T(128)}, u32[]{:S(2)}) copy-start(s32[40]{0:T(128)} %copy-done.25) | copy-start | bytes 484
  222.7 14.8 %collective-permute-start.16 = (bf16[256,384]{1,0:T(8,128)(2,1)S(1)}, bf16[256,384]{1,0:T(8,128)(2,1)S(1)}, u32[]{:S(2)}, u32[]{:S(2)}) collective-permute-start(bf16[256,384]{1,0:T(8,128)(2,1)S(1)} %get-tuple-element.77), channel_id=1, source_target_pairs={{0,64},{64,128},{128,192},{192,0},{1,65},{65,129},{129,193},{193,1... | collective-permute-start | bytes 589832 | tf_op jit(solution)/shard_map/ppermute | solution.py:43
  224.4 13.2 %collective-permute-start.17 = (bf16[256,384]{1,0:T(8,128)(2,1)S(1)}, bf16[256,384]{1,0:T(8,128)(2,1)S(1)}, u32[]{:S(2)}, u32[]{:S(2)}) collective-permute-start(bf16[256,384]{1,0:T(8,128)(2,1)S(1)} %get-tuple-element.78), channel_id=1, source_target_pairs={{0,192},{64,0},{128,64},{192,128},{1,193},{65,1},{129,65},{193,129... | collective-permute-start | bytes 589832 | tf_op jit(solution)/shard_map/ppermute | solution.py:43
  228.8 24.5 %collective-permute-start.14 = (bf16[256,768]{1,0:T(8,128)(2,1)}, bf16[256,768]{1,0:T(8,128)(2,1)}, u32[]{:S(2)}, u32[]{:S(2)}) collective-permute-start(bf16[256,768]{1,0:T(8,128)(2,1)} %get-tuple-element.73), channel_id=1, source_target_pairs={{0,64},{64,128},{128,192},{192,0},{1,65},{65,129},{129,193},{193,1... | collective-permute-start | bytes 1179656 | tf_op jit(solution)/shard_map/ppermute | solution.py:43
  229.2 24.2 %collective-permute-start.15 = (bf16[256,768]{1,0:T(8,128)(2,1)}, bf16[256,768]{1,0:T(8,128)(2,1)}, u32[]{:S(2)}, u32[]{:S(2)}) collective-permute-start(bf16[256,768]{1,0:T(8,128)(2,1)} %get-tuple-element.74), channel_id=1, source_target_pairs={{0,192},{64,0},{128,64},{192,128},{1,193},{65,1},{129,65},{193,129... | collective-permute-start | bytes 1179656 | tf_op jit(solution)/shard_map/ppermute | solution.py:43
  235.7 20.6 %collective-permute-start.12 = (bf16[128,2048]{1,0:T(8,128)(2,1)}, bf16[128,2048]{1,0:T(8,128)(2,1)S(1)}, u32[]{:S(2)}, u32[]{:S(2)}) collective-permute-start(bf16[128,2048]{1,0:T(8,128)(2,1)} %slice.338), channel_id=1, source_target_pairs={{0,32},{32,0},{1,33},{33,1},{2,34},{34,2},{3,35},{35,3},{4,36},{36... | collective-permute-start | bytes 1572872 | tf_op jit(solution)/shard_map/ppermute | solution.py:38
  242.8 19.3 %all-to-all-start.7 = ((bf16[32,2,2048]{2,1,0:T(2,128)(2,1)}), bf16[32,2,2048]{2,1,0:T(2,128)(2,1)S(1)}, u32[]{:S(2)}, u32[]{:S(2)}) async-start(bf16[32,2,2048]{2,1,0:T(2,128)(2,1)} %reshape.163), calls=%async_computation.7 | async-start | bytes 524288 | tf_op jit(solution)/shard_map/all_to_all | solution.py:66
  257.2 25.2 %collective-permute-start.13 = (bf16[64,2048]{1,0:T(8,128)(2,1)}, bf16[64,2048]{1,0:T(8,128)(2,1)S(1)}, u32[]{:S(2)}, u32[]{:S(2)}) collective-permute-start(bf16[64,2048]{1,0:T(8,128)(2,1)} %slice.339), channel_id=1, source_target_pairs={{0,1},{1,0},{2,3},{3,2},{4,5},{5,4},{6,7},{7,6},{8,9},{9,8},{10,11... | collective-permute-start | bytes 786440 | tf_op jit(solution)/shard_map/ppermute | solution.py:39
  262.8 6.8 %all-to-all-start.5 = ((bf16[2,256,768]{2,1,0:T(8,128)(2,1)}), bf16[2,256,768]{2,1,0:T(8,128)(2,1)S(1)}, u32[]{:S(2)}, u32[]{:S(2)}) async-start(bf16[2,256,768]{2,1,0:T(8,128)(2,1)} %bitcast.26), calls=%async_computation.5 | async-start | bytes 1572864 | tf_op jit(solution)/shard_map/all_to_all | solution.py:66
  269.7 12.1 %all-to-all-start.8 = ((f32[8,2,256]{2,1,0:T(2,128)}), f32[8,2,256]{2,1,0:T(2,128)S(1)}, u32[]{:S(2)}, u32[]{:S(2)}) async-start(f32[8,2,256]{2,1,0:T(2,128)} %bitcast.30), calls=%async_computation.8 | async-start | bytes 32768 | tf_op jit(solution)/shard_map/all_to_all | solution.py:66
  (22 other events, 67.1 us)

commit v2 on v1

v2 whole, which is shorter than its diff:
```python
import jax
import jax.numpy as jnp
from jax import lax
from jax.experimental import pallas as pl
from jax.experimental.pallas import tpu as pltpu
from jax.sharding import Mesh
from jax.sharding import PartitionSpec as P

F32, BF16 = jnp.float32, jnp.bfloat16
AXES = ("zh", "core", "x", "y", "zl")
PLANE = ("x", "y")
CAP = 10
EXPERTS = 64
PLUS = [(i, (i + 1) % 4) for i in range(4)]
MINUS = [(i, (i + 3) % 4) for i in range(4)]
OPPOSITE = [(i, (i + 2) % 4) for i in range(4)]
SWAP = [(0, 1), (1, 0)]


def mm(a, b, dims=((1,), (0,))):
    return lax.dot_general(a, b, (dims, ((), ())), preferred_element_type=F32)


def both_ways(up, down):
    return lax.ppermute(up, "zh", PLUS), lax.ppermute(down, "zh", MINUS)


def a2a(a, axes):
    return lax.all_to_all(a, axes, split_axis=0, concat_axis=0, tiled=True)


def alone(ids, *arrays):
    return lax.cond(
        ids[0, 0] >= 0, lambda *v: tuple(a2a(w, PLANE) for w in v), lambda *v: v, *arrays
    )


def at_unit(starts, unit, size):
    return pl.ds(pl.multiple_of(starts[unit], 256), size)


def forward_kernel(starts, x, s, own, after, far_lo, far_hi, prev, *refs):
    pre_out, spread, *outs = refs[:7]
    hidden, pre_grad, *grads, sems = refs[7:]
    hid = own.shape[1] // 3
    rows = x.shape[0] // 2
    pieces = ((own, 0), (after, 2), (far_lo, 4), (far_hi, 5), (prev, 6))

    @pl.loop(0, 2)
    def _(i):
        tile = pl.ds(pl.multiple_of(i * rows, rows), rows)
        pre = jnp.zeros((rows, 2 * hid), F32)
        for w, u in pieces:
            pre += mm(x[tile, at_unit(starts, u, w.shape[0])], w[:, : 2 * hid])
        hgrad = jnp.zeros((rows, hid), F32)
        for w, u in pieces:
            hgrad += mm(s[tile, at_unit(starts, u, w.shape[0])], w[:, 2 * hid :])
        gate_pre, up_pre = pre[:, :hid], pre[:, hid:]
        sg = jax.nn.sigmoid(gate_pre)
        act = gate_pre * sg
        h = (act * up_pre).astype(BF16)
        hidden[tile, :] = h
        share = jnp.sum(h.astype(F32) * hgrad, axis=1, keepdims=True)
        column = lax.broadcasted_iota(jnp.int32, (rows, spread.shape[1]), 1)
        spread[tile, :] = jnp.where(column == starts[8], share, 0.0)
        slope = sg * (1.0 + gate_pre * (1.0 - sg))
        pre_grad[tile, :hid] = (hgrad * up_pre * slope).astype(BF16)
        pre_grad[tile, hid:] = (hgrad * act).astype(BF16)

    copies = [pltpu.make_async_copy(pre_grad, pre_out, sems.at[len(outs)])]
    copies[0].start()
    firsts = (0, 2, 3, 5, 7)
    for k in (2, 3, 1, 4, 0):
        g = grads[k]
        for r in range(0, g.shape[0], 256):
            cols = at_unit(starts, firsts[k] + r // 256, 256)
            g[r : r + 256, : 2 * hid] = mm(x[:, cols], pre_grad[...], ((0,), (0,))).astype(BF16)
            g[r : r + 256, 2 * hid :] = mm(s[:, cols], hidden[...], ((0,), (0,))).astype(BF16)
        copies.append(pltpu.make_async_copy(g, outs[k], sems.at[k]))
        copies[-1].start()
    for copy in copies:
        copy.wait()


def back_kernel(starts, spread, pre_grad, own, after, far_lo, far_hi, prev, back):
    hid = own.shape[1] // 3
    rows = pre_grad.shape[0] // 2

    @pl.loop(0, 2)
    def _(i):
        tile = pl.ds(pl.multiple_of(i * rows, rows), rows)
        for w, u in ((own, 0), (after, 2), (far_lo, 4), (far_hi, 5), (prev, 6)):
            grad = mm(pre_grad[tile, :], w[:, : 2 * hid], ((1,), (1,)))
            back[tile, at_unit(starts, u, w.shape[0])] = grad.astype(BF16)
        back[tile, back.shape[1] - spread.shape[1] :] = spread[tile, :].astype(BF16)


def call(kernel, outs, spaces, scratch, *args):
    vmem = pl.BlockSpec(memory_space=pltpu.VMEM)
    smem = pl.BlockSpec(memory_space=pltpu.SMEM)
    return pl.pallas_call(
        kernel,
        out_shape=outs,
        in_specs=[smem if a.dtype == jnp.int32 else vmem for a in args],
        out_specs=[pl.BlockSpec(memory_space=space) for space in spaces],
        scratch_shapes=scratch,
        compiler_params=pltpu.CompilerParams(vmem_limit_bytes=40 * 2**20),
    )(*args)


def per_device(tokens, out_grad, ids, pos, keep, router, w_gate, w_up, w_down):
    tok, width = tokens.shape
    hid = w_gate.shape[2]
    piece = w_gate.shape[1]
    zh, core, zl = (lax.axis_index(n) for n in ("zh", "core", "zl"))
    chips = 16
    slots = chips * 4 * CAP

    experts = jnp.arange(EXPERTS, dtype=jnp.int32)
    hit = ids.T[None] == experts[:, None, None]
    chosen = jnp.any(hit, axis=1)
    held = hit & (keep.T > 0)[None]
    slot_t = (jnp.sum(jnp.where(held, pos.T[None] + 1, 0), axis=1) - 1).astype(BF16)
    logits = mm(router, tokens, ((0,), (1,)))
    sig = jax.nn.sigmoid(logits)
    prob = jnp.where(chosen, sig, 0.0)
    gate = prob / jnp.sum(prob, axis=0, keepdims=True)

    last = 2 * zl + core
    slot_c, gate_c = slot_t.T, gate.astype(BF16).T
    tok_e = jnp.concatenate([tokens, slot_c, jnp.zeros_like(gate_c)], axis=1)
    grad_e = jnp.concatenate([out_grad, slot_c, gate_c], axis=1)
    tok_z, grad_z = (lax.ppermute(v, "zl", SWAP) for v in (tok_e, grad_e))
    shard = a2a(jnp.concatenate([w_gate, w_up, jnp.swapaxes(w_down, 1, 2)], axis=2), "core")
    shard, tok_z, grad_z = lax.optimization_barrier((shard, tok_z, grad_z))
    shard = shard.reshape(2 * piece, 3 * hid)
    near = both_ways(shard, shard)
    far = [lax.ppermute(h, "zh", OPPOSITE) for h in (shard[:piece], shard[piece:])]

    def four(own, other):
        pair = jnp.concatenate([own, other], axis=0)
        return jnp.concatenate([pair, lax.ppermute(pair, "core", SWAP)], axis=0)

    every = 4 * jnp.arange(chips, dtype=jnp.int32) + last
    one = jnp.where(every[:, None] == experts[None, :], 1.0, 0.0).astype(BF16)

    def table(rows, at):
        return mm(one, rows[:, width + at : width + at + EXPERTS], ((1,), (1,)))

    place = jnp.arange(4 * CAP, dtype=jnp.int32)
    block = jnp.arange(4 * tok, dtype=jnp.int32) // tok
    same_block = (place // CAP)[:, None] == block[None, :]
    wanted = (place % CAP).astype(F32)[None, :, None]

    tok_q = four(tok_e, tok_z)
    grad_q = four(grad_e, grad_z)
    match = (table(tok_q, 0)[:, None, :] == wanted) & same_block
    pick = jnp.where(match, 1.0, 0.0).astype(BF16).reshape(slots, 4 * tok)
    pick_g = jnp.where(match, table(grad_q, EXPERTS)[:, None, :], 0.0).astype(BF16)
    send_x = mm(pick, tok_q[:, :width]).astype(BF16).reshape(chips, 4 * CAP, width)
    send_s = mm(pick_g.reshape(slots, 4 * tok), grad_q[:, :width]).astype(BF16)
    x, s = alone(ids, send_x, send_s.reshape(chips, 4 * CAP, width))
    x, s, (before, after), far = lax.optimization_barrier((x, s, near, far))
    x, s = x.reshape(slots, width), s.reshape(slots, width)
    weight = (shard, after, *far, before)

    starts = (2 * zh + jnp.arange(8, dtype=jnp.int32)) % 8 * piece
    expert = 2 * (4 * 2 * lax.axis_index("x") + 2 * lax.axis_index("y") + zl) + core
    starts = jnp.concatenate([starts, expert.astype(jnp.int32).reshape(1)])
    of = jax.ShapeDtypeStruct
    grads = tuple((piece * n, 3 * hid) for n in (2, 1, 2, 2, 1))
    pre_grad, spread, g_own, g_next, g_up, g_down, g_prev = call(
        forward_kernel,
        (of((slots, 2 * hid), BF16), of((slots, 2 * EXPERTS), F32))
        + tuple(of(shape, BF16) for shape in grads),
        (pl.ANY, pltpu.VMEM) + (pl.ANY,) * 5,
        [pltpu.VMEM((slots, hid), BF16), pltpu.VMEM((slots, 2 * hid), BF16)]
        + [pltpu.VMEM(shape, BF16) for shape in grads]
        + [pltpu.SemaphoreType.DMA((6,))],
        starts,
        x,
        s,
        *weight,
    )
    got_up, got_down = both_ways(g_up, g_down)

    wide = width + 2 * EXPERTS
    (back,) = call(
        back_kernel, (of((slots, wide), BF16),), (pltpu.VMEM,), [], starts, spread, pre_grad, *weight
    )
    (back,) = alone(ids, back.reshape(chips, 4 * CAP, wide))
    back, got_up, got_down = lax.optimization_barrier((back, got_up, got_down))
    part = mm(pick, back.reshape(slots, wide), ((0,), (0,)))
    part = part[: 2 * tok] + lax.ppermute(part[2 * tok :].astype(BF16), "core", SWAP).astype(F32)
    other = lax.ppermute(part[tok:].astype(BF16), "zl", SWAP)
    up = (g_next.astype(F32) + got_up[piece:].astype(F32)).astype(BF16)
    down = (g_prev.astype(F32) + got_down[:piece].astype(F32)).astype(BF16)
    other, up, down = lax.optimization_barrier((other, up, down))
    last_up, last_down = both_ways(up, down)
    part = part[:tok] + other.astype(F32)

    taken = part[:, width : width + EXPERTS].T
    mean = jnp.sum(taken, axis=0, keepdims=True)
    dlogits = jnp.where(chosen, (taken - gate * mean) * (1.0 - sig), 0.0).astype(BF16)
    term = mm(dlogits, tokens).astype(BF16).reshape(chips, 4, width)
    grad_tokens = (part[:, :width] + mm(dlogits, router, ((0,), (1,)))).astype(BF16)
    term = jnp.sum(a2a(term, PLANE).astype(F32), axis=0)
    term = term.reshape(2, 2, 8, width // 8).transpose(2, 0, 1, 3).reshape(chips, 2, width // 8)
    grad_router = jnp.sum(a2a(term, ("zh", "core", "zl")), axis=0)

    low = g_own[:piece].astype(F32) + last_up.astype(F32) + got_down[piece:].astype(F32)
    high = g_own[piece:].astype(F32) + got_up[:piece].astype(F32) + last_down.astype(F32)
    total = a2a(jnp.stack([low, high]).astype(BF16).reshape(2, piece, 3 * hid), "core")
    return (
        grad_tokens,
        total[:, :, :hid],
        total[:, :, hid : 2 * hid],
        jnp.swapaxes(total[:, :, 2 * hid :], 1, 2),
        grad_router,
    )


def solution(mesh):
    grid = Mesh(mesh.devices.reshape(4, 2, 4, 4, 2), AXES)
    dp, ex = ("zh", "core"), ("x", "y", "zl")
    rows = P(AXES, None)
    return jax.shard_map(
        per_device,
        mesh=grid,
        in_specs=(rows,) * 5 + (P(), P(ex, dp, None), P(ex, dp, None), P(ex, None, dp)),
        out_specs=(rows, P(ex, dp, None), P(ex, dp, None), P(ex, None, dp), P(ex, dp)),
        check_vma=False,
    )
```

time: 286 us -> 262 us (0.916)
  local copies, waits for them, and re-layouts: 29.2 us -> 14.6 us
  starting transfers between devices: 66.3 us -> 52.7 us
  waiting for transfers between devices: 19.7 us -> 32 us
  other arithmetic: 21.5 us -> 10.8 us
    all_to_all x5 -> x3, starting transfers between devices: 34.3 us -> 19.6 us  [a2a(): return lax.all_to_all(a, axes, split_axis=0, concat_axis=0, tiled=True)]
    slice x17 -> x3, local copies, waits for them, and re-layouts: 12.7 us -> 1.2 us  [the longest x1 1.1 us: per_device(): shard[piece:]]
    all_to_all x5 -> x3, waiting for transfers between devices: 10.7 us -> 20.2 us  [a2a(): return lax.all_to_all(a, axes, split_axis=0, concat_axis=0, tiled=True)]
    ppermute x4 -> x6, waiting for transfers between devices: 0.01 us -> 6.83 us  [the longest x1 5.24 us: per_device(): other = lax.ppermute(part[tok:].astype(BF16), 'zl', SWAP)]
    ppermute x12 -> x6, waiting for transfers between devices: 8.62 us -> 4.92 us  [both_ways(): return (lax.ppermute(up, 'zh', PLUS), lax.ppermute(down, 'zh', MINUS))]
    unnamed x63 -> x55, local copies, waits for them, and re-layouts: 6.36 us -> 2.72 us
    ppermute x4 -> x6, starting transfers between devices: 5.39 us -> 8.95 us  [the longest x2 5.46 us: per_device(): lax.ppermute(h, 'zh', OPPOSITE)]
    convert_element_type x5 -> x4, other arithmetic: 6.32 us -> 2.89 us  [the longest x1 2.59 us: per_device(): down = (g_prev.astype(F32) + got_down[:piece].astype(F32)).astype(BF16)]
  transfers between devices with their start and end apart: 23 -> 17, of which waited for: 5 -> 6; matrix products, arithmetic and copies ran while one was open for 13% -> 8% of each run, Pallas kernels for 2% -> 2%
where the time goes in v2:
time: 262 us; the launch traced here: 261 us
  blocking collectives  119 us (45%)
  starting transfers between devices  52.7 us (20%)
  waiting for transfers between devices  32 us (12%)
  Pallas kernels  18.1 us (7%)
  local copies, waits for them, and re-layouts  14.6 us (6%)
  matrix products  11.3 us (4%)
  other arithmetic  10.8 us (4%)
    all_to_all x4, blocking collectives, a2a(): return lax.all_to_all(a, axes, split_axis=0, concat_axis=0, tiled=True)  119 us
    ppermute x6, starting transfers between devices, both_ways(): return (lax.ppermute(up, 'zh', PLUS), lax.ppermute(down, 'zh', MINUS))  21.6 us
    all_to_all x3, waiting for transfers between devices, a2a(): return lax.all_to_all(a, axes, split_axis=0, concat_axis=0, tiled=True)  20.2 us
    all_to_all x3, starting transfers between devices, a2a(): return lax.all_to_all(a, axes, split_axis=0, concat_axis=0, tiled=True)  19.6 us
    pallas_call x2, Pallas kernels, call(): pl.pallas_call(kernel, out_shape=outs, in_specs=[smem if a.dtype == jnp.i...  18.1 us
    dot_general x8, matrix products, mm(): return lax.dot_general(a, b, (dims, ((), ())), preferred_element_type=F32)  11.3 us
    ppermute x2, starting transfers between devices, per_device(): lax.ppermute(h, 'zh', OPPOSITE)  5.46 us
  transfers between devices with their start and end apart: 17, of which 6 were waited for; matrix products, arithmetic and copies ran while one was open for 8% of the time, Pallas kernels for 2%

profile of v2, /device:TPU:1, one launch (start us, length us, event | category | flops | bytes accessed | tf_op | source)
XLA Modules:
  0.0 260.8 jit_solution(17420568105211678787)
XLA Ops:
  4.2 2.6 collective-permute-start
  11.0 6.4 %all-to-all-start.3 = ((bf16[2,256,1152]{2,1,0:T(8,128)(2,1)}), bf16[2,256,1152]{2,1,0:T(8,128)(2,1)S(1)}, u32[]{:S(2)}, u32[]{:S(2)}) async-start(bf16[2,256,1152]{2,1,0:T(8,128)(2,1)} %pad_maximum_fusion), calls=%async_computation.3 | async-start | bytes 2359296 | tf_op jit(solution)/shard_map/all_to_all | solution.py:29
  21.5 4.3 %collective-permute-start.5 = (bf16[512,1152]{1,0:T(8,128)(2,1)S(1)}, bf16[512,1152]{1,0:T(8,128)(2,1)S(1)}, u32[]{:S(2)}, u32[]{:S(2)}) collective-permute-start(bf16[512,1152]{1,0:T(8,128)(2,1)S(1)} %bitcast.71), channel_id=1, source_target_pairs={{0,192},{64,0},{128,64},{192,128},{1,193},{65,1},{129,65},{193,129... | collective-permute-start | bytes 3538952 | tf_op jit(solution)/shard_map/ppermute | solution.py:25
  28.6 3.6 %collective-permute-start.7 = (bf16[256,1152]{1,0:T(8,128)(2,1)}, bf16[256,1152]{1,0:T(8,128)(2,1)S(1)}, u32[]{:S(2)}, u32[]{:S(2)}) collective-permute-start(bf16[256,1152]{1,0:T(8,128)(2,1)} %get-tuple-element.93), channel_id=1, source_target_pairs={{0,128},{64,192},{128,0},{192,64},{1,129},{65,193},{129,1},{193,65... | collective-permute-start | bytes 1769480 | tf_op jit(solution)/shard_map/ppermute | solution.py:138
  32.2 1.8 collective-permute-start.6
  35.9 2.4 convolution_convert_fusion.1
  38.3 2.3 convolution_convert_fusion
  40.6 77.8 %conditional.2 = ((bf16[16,40,2048]{2,1,0:T(8,128)(2,1)}, bf16[16,40,2048]{2,1,0:T(8,128)(2,1)})) conditional(s32[]{:T(128)} %bitcast.6, (bf16[16,40,2048]{2,1,0:T(8,128)(2,1)}, bf16[16,40,2048]{2,1,0:T(8,128)(2,1)}) %tuple.49, (bf16[16,40,2048]{2,1,0:T(8,128)(2,1)}, bf16[16,40,2048]{2,1,0:T(8,128)(2,1)}) %tuple.50), branch_computations={%region_3.4_spmd, %region_4.5_spmd} | conditional | bytes 31457332 | solution.py:33
  40.6 1.7 copy.39
  42.4 38.4 %all_to_all.32 = bf16[16,40,2048]{2,1,0:T(8,128)(2,1)} all-to-all(bf16[16,40,2048]{2,1,0:T(8,128)(2,1)S(1)} %copy.39), channel_id=1, replica_groups=mesh['zh'=4,'core'=2,'x'=4,'y'=4,'zl'=2] {'x','y'}, dimensions={0} | all-to-all | bytes 5242880 | tf_op jit(solution)/shard_map/cond/branch_1_fun/all_to_all | solution.py:29
  80.8 36.2 %all_to_all.35 = bf16[16,40,2048]{2,1,0:T(8,128)(2,1)S(1)} all-to-all(bf16[16,40,2048]{2,1,0:T(8,128)(2,1)S(1)} %copy-done.8), channel_id=1, replica_groups=mesh['zh'=4,'core'=2,'x'=4,'y'=4,'zl'=2] {'x','y'}, dimensions={0} | all-to-all | bytes 5242880 | tf_op jit(solution)/shard_map/cond/branch_1_fun/all_to_all | solution.py:29
  117.0 1.5 copy.32
  118.5 12.6 %shard_map.128 = (bf16[640,768]{1,0:T(8,128)(2,1)S(1)}, f32[640,128]{1,0:T(8,128)S(1)}, bf16[512,1152]{1,0:T(8,128)(2,1)S(1)}, bf16[256,1152]{1,0:T(8,128)(2,1)S...) custom-call(s32[9]{0:T(128)S(1)} %pad_add_fusion.starts, ...), custom_call_target="tpu_custom_call" | custom-call | tf_op jit(solution)/shard_map/pallas_call | solution.py:101
  131.1 13.6 %collective-permute-start.8 = (bf16[512,1152]{1,0:T(8,128)(2,1)}, bf16[512,1152]{1,0:T(8,128)(2,1)}, u32[]{:S(2)}, u32[]{:S(2)}) collective-permute-start(bf16[512,1152]{1,0:T(8,128)(2,1)} %get-tuple-element.57), channel_id=1, source_target_pairs={{0,64},{64,128},{128,192},{192,0},{1,65},{65,129},{129,193},{193,1... | collective-permute-start | bytes 3538952 | tf_op jit(solution)/shard_map/ppermute | solution.py:25
  144.8 5.5 %shard_map.129 = bf16[640,2176]{1,0:T(8,128)(2,1)} custom-call(s32[9]{0:T(128)S(1)} %pad_add_fusion.starts, f32[640,128]{1,0:T(8,128)S(1)} %get-tuple-element.55.spread, bf16[640,768]{1,0:T(8,128)(2,1)S(1)} %get-tuple-element.56.pre_grad, bf16[512,1152]{1,0:T(8,128)(2,1)S(1)} %bitcast.74, bf16[512,1152]{1,0:T(8,128)(2,1)S(1)} %collective-permute-done.5.after, ...), custom_call_target="tpu_custom_call" | custom-call | tf_op jit(solution)/shard_map/pallas_call | solution.py:101
  150.3 41.9 %conditional.3 = (bf16[16,40,2176]{2,1,0:T(8,128)(2,1)}) conditional(s32[]{:T(128)} %bitcast.6, bf16[16,40,2176]{2,1,0:T(8,128)(2,1)} %bitcast.75, bf16[16,40,2176]{2,1,0:T(8,128)(2,1)} %bitcast.76), branch_computations={%region_5.6_spmd, %region_6.7_spmd} | conditional | bytes 16711716 | solution.py:33
  150.3 1.8 copy-done.7
  152.1 40.1 %all_to_all.33 = bf16[16,40,2176]{2,1,0:T(8,128)(2,1)} all-to-all(bf16[16,40,2176]{2,1,0:T(8,128)(2,1)S(1)} %copy-done.7), channel_id=1, replica_groups=mesh['zh'=4,'core'=2,'x'=4,'y'=4,'zl'=2] {'x','y'}, dimensions={0} | all-to-all | bytes 5570560 | tf_op jit(solution)/shard_map/cond/branch_1_fun/all_to_all | solution.py:29
  192.1 2.8 %collective-permute-done.8 = bf16[512,1152]{1,0:T(8,128)(2,1)} collective-permute-done((bf16[512,1152]{1,0:T(8,128)(2,1)}, bf16[512,1152]{1,0:T(8,128)(2,1)}, u32[]{:S(2)}, u32[]{:S(2)}) %collective-permute-start.8) | collective-permute-done | bytes 1179680 | tf_op jit(solution)/shard_map/ppermute | solution.py:25
  194.9 2.1 collective-permute-done.9
  197.0 3.0 %convolution_bitcast_fusion = f32[256,2176]{1,0:T(8,128)S(1)} fusion(bf16[16,40,2176]{2,1,0:T(8,128)(2,1)} %get-tuple-element.104, f32[16,256]{1,0:T(8,128)S(1)} %fusion.23, f32[40]{0:T(128)S(1)} %copy-done.27, pred[40,256]{1,0:T(8,128)(4,1)S(1)} %broadcast_compare_fusion), kind=kOutput, calls=%fused_computation | convolution fusion | flops 713687040 | bytes 5040288 | tf_op jit(solution)/shard_map/dot_general | solution.py:21
  200.1 1.8 collective-permute-start.10
  201.9 1.6 collective-permute-done.10
  203.7 2.6 add_convert_fusion.2
  206.3 5.2 %collective-permute-done.11 = bf16[64,2176]{1,0:T(8,128)(2,1)S(1)} collective-permute-done((bf16[64,2176]{1,0:T(8,128)(2,1)S(1)}, bf16[64,2176]{1,0:T(8,128)(2,1)S(1)}, u32[]{:S(2)}, u32[]{:S(2)}) %collective-permute-start.11) | collective-permute-done | bytes 278560 | tf_op jit(solution)/shard_map/ppermute | solution.py:195
  212.9 5.5 %all-to-all-start.5 = ((bf16[16,4,2048]{2,1,0:T(4,128)(2,1)}), bf16[16,4,2048]{2,1,0:T(4,128)(2,1)S(1)}, u32[]{:S(2)}, u32[]{:S(2)}) async-start(bf16[16,4,2048]{2,1,0:T(4,128)(2,1)} %reshape.145), calls=%async_computation.5 | async-start | bytes 524288 | tf_op jit(solution)/shard_map/all_to_all | solution.py:29
  218.4 2.5 collective-permute-start.12
  222.0 3.7 %all-to-all-done.5 = bf16[16,4,2048]{2,1,0:T(4,128)(2,1)S(1)} async-done(((bf16[16,4,2048]{2,1,0:T(4,128)(2,1)}), bf16[16,4,2048]{2,1,0:T(4,128)(2,1)S(1)}, u32[]{:S(2)}, u32[]{:S(2)}) %all-to-all-start.5) | async-done | bytes 262176 | tf_op jit(solution)/shard_map/all_to_all | solution.py:29
  226.5 7.7 %all-to-all-start.6 = ((f32[16,2,256]{2,1,0:T(2,128)}), f32[16,2,256]{2,1,0:T(2,128)S(1)}, u32[]{:S(2)}, u32[]{:S(2)}) async-start(f32[16,2,256]{2,1,0:T(2,128)} %bitcast.25), calls=%async_computation.6 | async-start | bytes 65536 | tf_op jit(solution)/shard_map/all_to_all | solution.py:29
  235.2 16.5 %all-to-all-done.6 = f32[16,2,256]{2,1,0:T(2,128)S(1)} async-done(((f32[16,2,256]{2,1,0:T(2,128)}), f32[16,2,256]{2,1,0:T(2,128)S(1)}, u32[]{:S(2)}, u32[]{:S(2)}) %all-to-all-start.6) | async-done | bytes 32800 | tf_op jit(solution)/shard_map/all_to_all | solution.py:29
  252.3 1.7 fusion.7
  254.1 4.7 %all_to_all.34 = bf16[2,256,1152]{2,1,0:T(8,128)(2,1)S(1)} all-to-all(bf16[2,256,1152]{2,1,0:T(8,128)(2,1)S(1)} %pad_maximum_fusion.1), channel_id=1, replica_groups=mesh['zh'=4,'core'=2,'x'=4,'y'=4,'zl'=2] {'core'}, dimensions={0} | all-to-all | bytes 2359296 | tf_op jit(solution)/shard_map/all_to_all | solution.py:29
  (119 shorter events, 22.9 us)
Async XLA Ops:
  0.6 7.0 %copy-start = (bf16[2048,64]{0,1:T(8,128)(2,1)S(1)}, bf16[2048,64]{0,1:T(8,128)(2,1)}, u32[]{:S(2)}) copy-start(bf16[2048,64]{0,1:T(8,128)(2,1)} %param.18) | copy-start | bytes 786436
  0.6 8.8 %copy-start.19 = (bf16[64,2048]{1,0:T(8,128)(2,1)S(1)}, bf16[64,2048]{1,0:T(8,128)(2,1)}, u32[]{:S(2)}) copy-start(bf16[64,2048]{1,0:T(8,128)(2,1)} %param.14) | copy-start | bytes 786436
  0.7 9.0 %copy-start.18 = (bf16[2,384,256]{2,1,0:T(8,128)(2,1)S(1)}, bf16[2,384,256]{2,1,0:T(8,128)(2,1)}, u32[]{:S(2)}) copy-start(bf16[2,384,256]{2,1,0:T(8,128)(2,1)} %param.21) | copy-start | bytes 1179652
  3.1 6.8 %copy-start.16 = (bf16[2,256,384]{2,1,0:T(8,128)(2,1)S(1)}, bf16[2,256,384]{2,1,0:T(8,128)(2,1)}, u32[]{:S(2)}) copy-start(bf16[2,256,384]{2,1,0:T(8,128)(2,1)} %param.20) | copy-start | bytes 1179652
  3.1 6.8 %copy-start.17 = (bf16[2,256,384]{2,1,0:T(8,128)(2,1)S(1)}, bf16[2,256,384]{2,1,0:T(8,128)(2,1)}, u32[]{:S(2)}) copy-start(bf16[2,256,384]{2,1,0:T(8,128)(2,1)} %param.19) | copy-start | bytes 1179652
  4.2 16.5 %collective-permute-start = (bf16[64,2176]{1,0:T(8,128)(2,1)S(1)}, bf16[64,2176]{1,0:T(8,128)(2,1)S(1)}, u32[]{:S(2)}, u32[]{:S(2)}) collective-permute-start(bf16[64,2176]{1,0:T(8,128)(2,1)S(1)} %concatenate.26), channel_id=1, source_target_pairs={{0,1},{1,0},{2,3},{3,2},{4,5},{5,4},{6,7},{7,6},{8,9},{9,8},{10,11... | collective-permute-start | bytes 835592 | tf_op jit(solution)/shard_map/ppermute | solution.py:133
  9.5 17.8 %copy-start.9 = (bf16[64,2176]{1,0:T(8,128)(2,1)}, bf16[64,2176]{1,0:T(8,128)(2,1)S(1)}, u32[]{:S(2)}) copy-start(bf16[64,2176]{1,0:T(8,128)(2,1)S(1)} %concatenate.28) | copy-start | bytes 835588
  9.5 11.2 %collective-permute-start.1 = (bf16[64,2176]{1,0:T(8,128)(2,1)S(1)}, bf16[64,2176]{1,0:T(8,128)(2,1)S(1)}, u32[]{:S(2)}, u32[]{:S(2)}) collective-permute-start(bf16[64,2176]{1,0:T(8,128)(2,1)S(1)} %concatenate.28), channel_id=1, source_target_pairs={{0,1},{1,0},{2,3},{3,2},{4,5},{5,4},{6,7},{7,6},{8,9},{9,8},{10,11... | collective-permute-start | bytes 835592 | tf_op jit(solution)/shard_map/ppermute | solution.py:133
  11.0 9.6 %all-to-all-start.3 = ((bf16[2,256,1152]{2,1,0:T(8,128)(2,1)}), bf16[2,256,1152]{2,1,0:T(8,128)(2,1)S(1)}, u32[]{:S(2)}, u32[]{:S(2)}) async-start(bf16[2,256,1152]{2,1,0:T(8,128)(2,1)} %pad_maximum_fusion), calls=%async_computation.3 | async-start | bytes 2359296 | tf_op jit(solution)/shard_map/all_to_all | solution.py:29
  17.4 11.2 %copy-start.26 = (f32[40]{0:T(128)}, f32[40]{0:T(128)S(1)}, u32[]{:S(2)}) copy-start(f32[40]{0:T(128)S(1)} %fusion.40) | copy-start | bytes 484
  20.7 7.9 %copy-start.11 = (bf16[64,2176]{1,0:T(8,128)(2,1)}, bf16[64,2176]{1,0:T(8,128)(2,1)S(1)}, u32[]{:S(2)}) copy-start(bf16[64,2176]{1,0:T(8,128)(2,1)S(1)} %collective-permute-done) | copy-start | bytes 835588
  21.5 97.0 %collective-permute-start.5 = (bf16[512,1152]{1,0:T(8,128)(2,1)S(1)}, bf16[512,1152]{1,0:T(8,128)(2,1)S(1)}, u32[]{:S(2)}, u32[]{:S(2)}) collective-permute-start(bf16[512,1152]{1,0:T(8,128)(2,1)S(1)} %bitcast.71), channel_id=1, source_target_pairs={{0,192},{64,0},{128,64},{192,128},{1,193},{65,1},{129,65},{193,129... | collective-permute-start | bytes 3538952 | tf_op jit(solution)/shard_map/ppermute | solution.py:25
  25.8 92.7 %collective-permute-start.4 = (bf16[512,1152]{1,0:T(8,128)(2,1)S(1)}, bf16[512,1152]{1,0:T(8,128)(2,1)}, u32[]{:S(2)}, u32[]{:S(2)}) collective-permute-start(bf16[512,1152]{1,0:T(8,128)(2,1)S(1)} %bitcast.72), channel_id=1, source_target_pairs={{0,64},{64,128},{128,192},{192,0},{1,65},{65,129},{129,193},{193,1... | collective-permute-start | bytes 3538952 | tf_op jit(solution)/shard_map/ppermute | solution.py:25
  25.8 6.4 %collective-permute-start.2 = (bf16[128,2176]{1,0:T(8,128)(2,1)S(1)}, bf16[128,2176]{1,0:T(8,128)(2,1)S(1)}, u32[]{:S(2)}, u32[]{:S(2)}) collective-permute-start(bf16[128,2176]{1,0:T(8,128)(2,1)S(1)} %pad_maximum_fusion.10), channel_id=1, source_target_pairs={{0,32},{32,0},{1,33},{33,1},{2,34},{34,2},{3,35},{35,3},{4,36},{36... | collective-permute-start | bytes 1671176 | tf_op jit(solution)/shard_map/ppermute | solution.py:142
  27.4 7.6 %copy-start.22 = (f32[640]{0:T(1024)S(1)}, f32[640]{0:T(1024)}, u32[]{:S(2)}) copy-start(f32[640]{0:T(1024)} %eq.92) | copy-start | bytes 7684
  27.4 7.8 %collective-permute-start.3 = (bf16[128,2176]{1,0:T(8,128)(2,1)S(1)}, bf16[128,2176]{1,0:T(8,128)(2,1)S(1)}, u32[]{:S(2)}, u32[]{:S(2)}) collective-permute-start(bf16[128,2176]{1,0:T(8,128)(2,1)S(1)} %pad_maximum_fusion.11), channel_id=1, source_target_pairs={{0,32},{32,0},{1,33},{33,1},{2,34},{34,2},{3,35},{35,3},{4,36},{36... | collective-permute-start | bytes 1671176 | tf_op jit(solution)/shard_map/ppermute | solution.py:142
  28.6 89.9 %collective-permute-start.7 = (bf16[256,1152]{1,0:T(8,128)(2,1)}, bf16[256,1152]{1,0:T(8,128)(2,1)S(1)}, u32[]{:S(2)}, u32[]{:S(2)}) collective-permute-start(bf16[256,1152]{1,0:T(8,128)(2,1)} %get-tuple-element.93), channel_id=1, source_target_pairs={{0,128},{64,192},{128,0},{192,64},{1,129},{65,193},{129,1},{193,65... | collective-permute-start | bytes 1769480 | tf_op jit(solution)/shard_map/ppermute | solution.py:138
  32.2 86.3 %collective-permute-start.6 = (bf16[256,1152]{1,0:T(8,128)(2,1)}, bf16[256,1152]{1,0:T(8,128)(2,1)}, u32[]{:S(2)}, u32[]{:S(2)}) collective-permute-start(bf16[256,1152]{1,0:T(8,128)(2,1)} %get-tuple-element.94), channel_id=1, source_target_pairs={{0,128},{64,192},{128,0},{192,64},{1,129},{65,193},{129,1},{193,65... | collective-permute-start | bytes 1769480 | tf_op jit(solution)/shard_map/ppermute | solution.py:138
  42.4 38.4 %copy-start.8 = (bf16[16,40,2048]{2,1,0:T(8,128)(2,1)S(1)}, bf16[16,40,2048]{2,1,0:T(8,128)(2,1)}, u32[]{:S(2)}) copy-start(bf16[16,40,2048]{2,1,0:T(8,128)(2,1)} %get-tuple-element.14) | copy-start | bytes 7864324 | tf_op jit(solution)/shard_map/cond
  131.1 19.1 %copy-start.1 = (bf16[512,1152]{1,0:T(8,128)(2,1)}, bf16[512,1152]{1,0:T(8,128)(2,1)S(1)}, u32[]{:S(2)}) copy-start(bf16[512,1152]{1,0:T(8,128)(2,1)S(1)} %get-tuple-element.65) | copy-start | bytes 3538948
  131.1 19.1 %copy-start.3 = (bf16[256,1152]{1,0:T(8,128)(2,1)}, bf16[256,1152]{1,0:T(8,128)(2,1)S(1)}, u32[]{:S(2)}) copy-start(bf16[256,1152]{1,0:T(8,128)(2,1)S(1)} %get-tuple-element.60) | copy-start | bytes 1769476
  131.1 19.1 %copy-start.5 = (bf16[256,1152]{1,0:T(8,128)(2,1)}, bf16[256,1152]{1,0:T(8,128)(2,1)S(1)}, u32[]{:S(2)}) copy-start(bf16[256,1152]{1,0:T(8,128)(2,1)S(1)} %get-tuple-element.62) | copy-start | bytes 1769476
  131.1 63.8 %collective-permute-start.8 = (bf16[512,1152]{1,0:T(8,128)(2,1)}, bf16[512,1152]{1,0:T(8,128)(2,1)}, u32[]{:S(2)}, u32[]{:S(2)}) collective-permute-start(bf16[512,1152]{1,0:T(8,128)(2,1)} %get-tuple-element.57), channel_id=1, source_target_pairs={{0,64},{64,128},{128,192},{192,0},{1,65},{65,129},{129,193},{193,1... | collective-permute-start | bytes 3538952 | tf_op jit(solution)/shard_map/ppermute | solution.py:25
  144.8 52.3 %collective-permute-start.9 = (bf16[512,1152]{1,0:T(8,128)(2,1)}, bf16[512,1152]{1,0:T(8,128)(2,1)}, u32[]{:S(2)}, u32[]{:S(2)}) collective-permute-start(bf16[512,1152]{1,0:T(8,128)(2,1)} %get-tuple-element.58), channel_id=1, source_target_pairs={{0,192},{64,0},{128,64},{192,128},{1,193},{65,1},{129,65},{193,129... | collective-permute-start | bytes 3538952 | tf_op jit(solution)/shard_map/ppermute | solution.py:25
  150.2 46.8 %copy-start.27 = (f32[40]{0:T(128)S(1)}, f32[40]{0:T(128)}, u32[]{:S(2)}) copy-start(f32[40]{0:T(128)} %copy-done.26) | copy-start | bytes 484
  200.1 3.4 %collective-permute-start.10 = (bf16[128,2176]{1,0:T(8,128)(2,1)S(1)}, bf16[128,2176]{1,0:T(8,128)(2,1)S(1)}, u32[]{:S(2)}, u32[]{:S(2)}) collective-permute-start(bf16[128,2176]{1,0:T(8,128)(2,1)S(1)} %slice.126), channel_id=1, source_target_pairs={{0,32},{32,0},{1,33},{33,1},{2,34},{34,2},{3,35},{35,3},{4,36},{36... | collective-permute-start | bytes 1671176 | tf_op jit(solution)/shard_map/ppermute | solution.py:194
  203.6 8.0 %collective-permute-start.11 = (bf16[64,2176]{1,0:T(8,128)(2,1)S(1)}, bf16[64,2176]{1,0:T(8,128)(2,1)S(1)}, u32[]{:S(2)}, u32[]{:S(2)}) collective-permute-start(bf16[64,2176]{1,0:T(8,128)(2,1)S(1)} %slice.127), channel_id=1, source_target_pairs={{0,1},{1,0},{2,3},{3,2},{4,5},{5,4},{6,7},{7,6},{8,9},{9,8},{10,11... | collective-permute-start | bytes 835592 | tf_op jit(solution)/shard_map/ppermute | solution.py:195
  212.1 40.2 %copy-start.2 = (bf16[512,1152]{1,0:T(8,128)(2,1)S(1)}, bf16[512,1152]{1,0:T(8,128)(2,1)}, u32[]{:S(2)}) copy-start(bf16[512,1152]{1,0:T(8,128)(2,1)} %copy-done.1) | copy-start | bytes 3538948
  212.9 12.8 %all-to-all-start.5 = ((bf16[16,4,2048]{2,1,0:T(4,128)(2,1)}), bf16[16,4,2048]{2,1,0:T(4,128)(2,1)S(1)}, u32[]{:S(2)}, u32[]{:S(2)}) async-start(bf16[16,4,2048]{2,1,0:T(4,128)(2,1)} %reshape.145), calls=%async_computation.5 | async-start | bytes 524288 | tf_op jit(solution)/shard_map/all_to_all | solution.py:29
  218.4 33.9 %collective-permute-start.12 = (bf16[256,1152]{1,0:T(8,128)(2,1)}, bf16[256,1152]{1,0:T(8,128)(2,1)S(1)}, u32[]{:S(2)}, u32[]{:S(2)}) collective-permute-start(bf16[256,1152]{1,0:T(8,128)(2,1)} %get-tuple-element.66), channel_id=1, source_target_pairs={{0,64},{64,128},{128,192},{192,0},{1,65},{65,129},{129,193},{193,1... | collective-permute-start | bytes 1769480 | tf_op jit(solution)/shard_map/ppermute | solution.py:25
  220.9 31.4 %collective-permute-start.13 = (bf16[256,1152]{1,0:T(8,128)(2,1)}, bf16[256,1152]{1,0:T(8,128)(2,1)S(1)}, u32[]{:S(2)}, u32[]{:S(2)}) collective-permute-start(bf16[256,1152]{1,0:T(8,128)(2,1)} %get-tuple-element.67), channel_id=1, source_target_pairs={{0,192},{64,0},{128,64},{192,128},{1,193},{65,1},{129,65},{193,129... | collective-permute-start | bytes 1769480 | tf_op jit(solution)/shard_map/ppermute | solution.py:25
  226.5 25.2 %all-to-all-start.6 = ((f32[16,2,256]{2,1,0:T(2,128)}), f32[16,2,256]{2,1,0:T(2,128)S(1)}, u32[]{:S(2)}, u32[]{:S(2)}) async-start(f32[16,2,256]{2,1,0:T(2,128)} %bitcast.25), calls=%async_computation.6 | async-start | bytes 65536 | tf_op jit(solution)/shard_map/all_to_all | solution.py:29
  (13 other events, 50.1 us)

commit v3 on v2

--- a/solution.py
+++ b/solution.py
@@ -13,7 +13,6 @@
 EXPERTS = 64
 PLUS = [(i, (i + 1) % 4) for i in range(4)]
 MINUS = [(i, (i + 3) % 4) for i in range(4)]
-OPPOSITE = [(i, (i + 2) % 4) for i in range(4)]
 SWAP = [(0, 1), (1, 0)]
 
 
@@ -135,7 +134,6 @@
     shard, tok_z, grad_z = lax.optimization_barrier((shard, tok_z, grad_z))
     shard = shard.reshape(2 * piece, 3 * hid)
     near = both_ways(shard, shard)
-    far = [lax.ppermute(h, "zh", OPPOSITE) for h in (shard[:piece], shard[piece:])]
 
     def four(own, other):
         pair = jnp.concatenate([own, other], axis=0)
@@ -159,8 +157,13 @@
     pick_g = jnp.where(match, table(grad_q, EXPERTS)[:, None, :], 0.0).astype(BF16)
     send_x = mm(pick, tok_q[:, :width]).astype(BF16).reshape(chips, 4 * CAP, width)
     send_s = mm(pick_g.reshape(slots, 4 * tok), grad_q[:, :width]).astype(BF16)
-    x, s = alone(ids, send_x, send_s.reshape(chips, 4 * CAP, width))
-    x, s, (before, after), far = lax.optimization_barrier((x, s, near, far))
+    send_x, send_s = lax.optimization_barrier((send_x, send_s))
+    (x,) = alone(ids, send_x)
+    x, send_s, (before, after) = lax.optimization_barrier((x, send_s, near))
+    halves = lax.optimization_barrier((before[:piece], after[piece:], send_s))
+    far = both_ways(*halves[:2])
+    (s,) = alone(ids, halves[2].reshape(chips, 4 * CAP, width))
+    s, far = lax.optimization_barrier((s, far))
     x, s = x.reshape(slots, width), s.reshape(slots, width)
     weight = (shard, after, *far, before)
 
@@ -192,10 +195,11 @@
     back, got_up, got_down = lax.optimization_barrier((back, got_up, got_down))
     part = mm(pick, back.reshape(slots, wide), ((0,), (0,)))
     part = part[: 2 * tok] + lax.ppermute(part[2 * tok :].astype(BF16), "core", SWAP).astype(F32)
-    other = lax.ppermute(part[tok:].astype(BF16), "zl", SWAP)
+    for_other = part[tok:].astype(BF16)
     up = (g_next.astype(F32) + got_up[piece:].astype(F32)).astype(BF16)
     down = (g_prev.astype(F32) + got_down[:piece].astype(F32)).astype(BF16)
-    other, up, down = lax.optimization_barrier((other, up, down))
+    for_other, up, down = lax.optimization_barrier((for_other, up, down))
+    other = lax.ppermute(for_other, "zl", SWAP)
     last_up, last_down = both_ways(up, down)
     part = part[:tok] + other.astype(F32)
 
@@ -206,11 +210,17 @@
     grad_tokens = (part[:, :width] + mm(dlogits, router, ((0,), (1,)))).astype(BF16)
     term = jnp.sum(a2a(term, PLANE).astype(F32), axis=0)
     term = term.reshape(2, 2, 8, width // 8).transpose(2, 0, 1, 3).reshape(chips, 2, width // 8)
-    grad_router = jnp.sum(a2a(term, ("zh", "core", "zl")), axis=0)
+    term, last_up, last_down = lax.optimization_barrier((term, last_up, last_down))
+    term = a2a(term, ("zh", "core", "zl"))
 
     low = g_own[:piece].astype(F32) + last_up.astype(F32) + got_down[piece:].astype(F32)
     high = g_own[piece:].astype(F32) + got_up[:piece].astype(F32) + last_down.astype(F32)
-    total = a2a(jnp.stack([low, high]).astype(BF16).reshape(2, piece, 3 * hid), "core")
+    low, high = low.astype(BF16), high.astype(BF16)
+    other = lax.ppermute(jnp.where(core == 0, high, low), "core", SWAP)
+    mine = jnp.where(core == 0, low, high)
+    total = jnp.stack([jnp.where(core == 0, mine, other), jnp.where(core == 0, other, mine)])
+    total, term = lax.optimization_barrier((total, term))
+    grad_router = jnp.sum(term, axis=0)
     return (
         grad_tokens,
         total[:, :, :hid],

time: 262 us -> 258 us (0.985)
  blocking collectives: 119 us -> 108 us
  matrix products: 11.3 us -> 14.4 us
    all_to_all x4 -> x3, blocking collectives: 119 us -> 108 us  [a2a(): return lax.all_to_all(a, axes, split_axis=0, concat_axis=0, tiled=True)]
    ppermute x3 -> x2, waiting for transfers between devices: 5.24 us -> 15.7 us  [the longest x1 15.7 us: per_device(): other = lax.ppermute(for_other, 'zl', SWAP)]
    ppermute x3 -> x2, starting transfers between devices: 5.55 us -> 11.9 us  [the longest x1 8.8 us: per_device(): other = lax.ppermute(for_other, 'zl', SWAP)]
    all_to_all x3, starting transfers between devices: 19.6 us -> 14.3 us  [a2a(): return lax.all_to_all(a, axes, split_axis=0, concat_axis=0, tiled=True)]
    ppermute x6 -> x8, waiting for transfers between devices: 4.92 us -> 0.02 us  [both_ways(): return (lax.ppermute(up, 'zh', PLUS), lax.ppermute(down, 'zh', MINUS))]
    ppermute x1, starting transfers between devices: 1.8 us -> 6.42 us  [per_device(): lax.ppermute(part[2 * tok:].astype(BF16), 'core', SWAP).astype(F32)]
    ppermute x6 -> x8, starting transfers between devices: 21.6 us -> 17.5 us  [both_ways(): return (lax.ppermute(up, 'zh', PLUS), lax.ppermute(down, 'zh', MINUS))]
    all_to_all x3, waiting for transfers between devices: 20.2 us -> 16.3 us  [a2a(): return lax.all_to_all(a, axes, split_axis=0, concat_axis=0, tiled=True)]
  transfers between devices with their start and end apart: 17 -> 18, of which waited for: 6 -> 4; matrix products, arithmetic and copies ran while one was open for 8% -> 8% of each run, Pallas kernels for 2% -> 2%
where the time goes in v3:
time: 258 us; the launch traced here: 257 us
  blocking collectives  108 us (42%)
  starting transfers between devices  54.1 us (21%)
  waiting for transfers between devices  32 us (12%)
  Pallas kernels  18 us (7%)
  local copies, waits for them, and re-layouts  15.6 us (6%)
  matrix products  14.4 us (6%)
  other arithmetic  13.1 us (5%)
    all_to_all x3, blocking collectives, a2a(): return lax.all_to_all(a, axes, split_axis=0, concat_axis=0, tiled=True)  108 us
    pallas_call x2, Pallas kernels, call(): pl.pallas_call(kernel, out_shape=outs, in_specs=[smem if a.dtype == jnp.i...  18 us
    ppermute x8, starting transfers between devices, both_ways(): return (lax.ppermute(up, 'zh', PLUS), lax.ppermute(down, 'zh', MINUS))  17.5 us
    all_to_all x3, waiting for transfers between devices, a2a(): return lax.all_to_all(a, axes, split_axis=0, concat_axis=0, tiled=True)  16.3 us
    ppermute x1, waiting for transfers between devices, per_device(): other = lax.ppermute(for_other, 'zl', SWAP)  15.7 us
    dot_general x8, matrix products, mm(): return lax.dot_general(a, b, (dims, ((), ())), preferred_element_type=F32)  14.4 us
    all_to_all x3, starting transfers between devices, a2a(): return lax.all_to_all(a, axes, split_axis=0, concat_axis=0, tiled=True)  14.3 us
    ppermute x1, starting transfers between devices, per_device(): other = lax.ppermute(for_other, 'zl', SWAP)  8.8 us
  transfers between devices with their start and end apart: 18, of which 4 were waited for; matrix products, arithmetic and copies ran while one was open for 8% of the time, Pallas kernels for 2%

profile of v3, /device:TPU:1, one launch (start us, length us, event | category | flops | bytes accessed | tf_op | source)
XLA Modules:
  0.0 257.3 jit_solution(2373554242367079314)
XLA Ops:
  4.2 2.6 collective-permute-start
  11.0 6.1 %all-to-all-start.3 = ((bf16[2,256,1152]{1,2,0:T(8,128)(2,1)}), bf16[2,256,1152]{1,2,0:T(8,128)(2,1)S(1)}, u32[]{:S(2)}, u32[]{:S(2)}) async-start(bf16[2,256,1152]{1,2,0:T(8,128)(2,1)} %pad_maximum_fusion), calls=%async_computation.3 | async-start | bytes 2359296 | tf_op jit(solution)/shard_map/all_to_all | solution.py:28
  17.1 1.8 all-to-all-done.3
  22.8 5.9 %collective-permute-start.5 = (bf16[512,1152]{1,0:T(8,128)(2,1)S(1)}, bf16[512,1152]{1,0:T(8,128)(2,1)S(1)}, u32[]{:S(2)}, u32[]{:S(2)}) collective-permute-start(bf16[512,1152]{1,0:T(8,128)(2,1)S(1)} %bitcast.67), channel_id=1, source_target_pairs={{0,192},{64,0},{128,64},{192,128},{1,193},{65,1},{129,65},{193,129... | collective-permute-start | bytes 3538952 | tf_op jit(solution)/shard_map/ppermute | solution.py:24
  33.1 3.4 %convolution_convert_fusion.1 = bf16[640,2048]{1,0:T(8,128)(2,1)} fusion(bf16[640,256]{1,0:T(8,128)(2,1)S(1)} %select_convert_fusion, bf16[128,2176]{1,0:T(8,128)(2,1)} %collective-permute-done.2, bf16[64,2176]{1,0:T(8,128)(2,1)S(1)} %collective-permute-done, bf16[64,2176]{1,0:T(8,128)(2,1)S(1)} %concatenate.26), kind=kOutput, calls=%fused_computation.2 | convolution fusion | flops 675545088 | bytes 4063232 | tf_op jit(solution)/shard_map/dot_general | solution.py:20
  36.6 3.4 %convolution_convert_fusion = bf16[640,2048]{1,0:T(8,128)(2,1)} fusion(bf16[640,256]{1,0:T(8,128)(2,1)S(1)} %fusion.5, bf16[128,2176]{1,0:T(8,128)(2,1)} %collective-permute-done.3, bf16[64,2176]{1,0:T(8,128)(2,1)S(1)} %copy-done.11, bf16[64,2176]{1,0:T(8,128)(2,1)S(1)} %concatenate.28), kind=kOutput, calls=%fused_computation.1 | convolution fusion | flops 675545088 | bytes 4063232 | tf_op jit(solution)/shard_map/dot_general | solution.py:20
  40.0 41.1 %conditional.3 = (bf16[16,40,2048]{2,1,0:T(8,128)(2,1)}) conditional(s32[]{:T(128)} %bitcast.6, bf16[16,40,2048]{2,1,0:T(8,128)(2,1)} %bitcast.76, bf16[16,40,2048]{2,1,0:T(8,128)(2,1)} %bitcast.77), branch_computations={%region_3.4_spmd, %region_4.5_spmd} | conditional | bytes 15728676 | solution.py:32
  40.0 1.7 copy-done.9
  41.8 39.4 %all_to_all.27 = bf16[16,40,2048]{2,1,0:T(8,128)(2,1)} all-to-all(bf16[16,40,2048]{2,1,0:T(8,128)(2,1)S(1)} %copy-done.9), channel_id=1, replica_groups=mesh['zh'=4,'core'=2,'x'=4,'y'=4,'zl'=2] {'x','y'}, dimensions={0} | all-to-all | bytes 5242880 | tf_op jit(solution)/shard_map/cond/branch_1_fun/all_to_all | solution.py:28
  81.2 1.9 slice.75
  85.2 2.3 collective-permute-start.7
  87.6 36.2 %conditional.4 = (bf16[16,40,2048]{2,1,0:T(8,128)(2,1)}) conditional(s32[]{:T(128)} %bitcast.6, bf16[16,40,2048]{2,1,0:T(8,128)(2,1)} %bitcast.73, bf16[16,40,2048]{2,1,0:T(8,128)(2,1)} %bitcast.74), branch_computations={%region_5.6_spmd, %region_6.7_spmd} | conditional | bytes 15728676 | solution.py:32
  87.6 1.7 copy-done.8
  89.4 34.4 %all_to_all.28 = bf16[16,40,2048]{2,1,0:T(8,128)(2,1)} all-to-all(bf16[16,40,2048]{2,1,0:T(8,128)(2,1)S(1)} %copy-done.8), channel_id=1, replica_groups=mesh['zh'=4,'core'=2,'x'=4,'y'=4,'zl'=2] {'x','y'}, dimensions={0} | all-to-all | bytes 5242880 | tf_op jit(solution)/shard_map/cond/branch_1_fun/all_to_all | solution.py:28
  123.8 12.6 %shard_map.128 = (bf16[640,768]{1,0:T(8,128)(2,1)S(1)}, f32[640,128]{1,0:T(8,128)S(1)}, bf16[512,1152]{1,0:T(8,128)(2,1)S(1)}, bf16[256,1152]{1,0:T(8,128)(2,1)S...) custom-call(s32[9]{0:T(128)S(1)} %pad_add_fusion.starts, ...), custom_call_target="tpu_custom_call" | custom-call | tf_op jit(solution)/shard_map/pallas_call | solution.py:100
  137.4 3.4 %collective-permute-start.9 = (bf16[512,1152]{1,0:T(8,128)(2,1)}, bf16[512,1152]{1,0:T(8,128)(2,1)}, u32[]{:S(2)}, u32[]{:S(2)}) collective-permute-start(bf16[512,1152]{1,0:T(8,128)(2,1)} %get-tuple-element.71), channel_id=1, source_target_pairs={{0,192},{64,0},{128,64},{192,128},{1,193},{65,1},{129,65},{193,129... | collective-permute-start | bytes 3538952 | tf_op jit(solution)/shard_map/ppermute | solution.py:24
  140.8 5.5 %shard_map.129 = bf16[640,2176]{1,0:T(8,128)(2,1)} custom-call(s32[9]{0:T(128)S(1)} %pad_add_fusion.starts, f32[640,128]{1,0:T(8,128)S(1)} %get-tuple-element.68.spread, bf16[640,768]{1,0:T(8,128)(2,1)S(1)} %get-tuple-element.69.pre_grad, bf16[512,1152]{1,0:T(8,128)(2,1)S(1)} %bitcast.70, bf16[512,1152]{1,0:T(8,128)(2,1)S(1)} %collective-permute-done.5.after, ...), custom_call_target="tpu_custom_call" | custom-call | tf_op jit(solution)/shard_map/pallas_call | solution.py:100
  146.2 36.4 %conditional.5 = (bf16[16,40,2176]{2,1,0:T(8,128)(2,1)}) conditional(s32[]{:T(128)} %bitcast.6, bf16[16,40,2176]{2,1,0:T(8,128)(2,1)} %bitcast.71, bf16[16,40,2176]{2,1,0:T(8,128)(2,1)} %bitcast.72), branch_computations={%region_7.8_spmd, %region_8.9_spmd} | conditional | bytes 16711716 | solution.py:32
  146.3 1.8 copy-done.7
  148.1 34.6 %all_to_all.29 = bf16[16,40,2176]{2,1,0:T(8,128)(2,1)} all-to-all(bf16[16,40,2176]{2,1,0:T(8,128)(2,1)S(1)} %copy-done.7), channel_id=1, replica_groups=mesh['zh'=4,'core'=2,'x'=4,'y'=4,'zl'=2] {'x','y'}, dimensions={0} | all-to-all | bytes 5570560 | tf_op jit(solution)/shard_map/cond/branch_1_fun/all_to_all | solution.py:28
  182.6 3.0 %convolution_bitcast_fusion = f32[256,2176]{1,0:T(8,128)S(1)} fusion(bf16[16,40,2176]{2,1,0:T(8,128)(2,1)} %get-tuple-element.120, f32[16,256]{1,0:T(8,128)S(1)} %fusion.21, f32[40]{0:T(128)S(1)} %fusion.38, pred[40,256]{1,0:T(8,128)(4,1)S(1)} %broadcast_compare_fusion), kind=kOutput, calls=%fused_computation | convolution fusion | flops 713687040 | bytes 5040288 | tf_op jit(solution)/shard_map/dot_general | solution.py:20
  185.7 6.4 %collective-permute-start.10 = (bf16[128,2176]{1,0:T(8,128)(2,1)S(1)}, bf16[128,2176]{1,0:T(8,128)(2,1)S(1)}, u32[]{:S(2)}, u32[]{:S(2)}) collective-permute-start(bf16[128,2176]{1,0:T(8,128)(2,1)S(1)} %slice.114), channel_id=1, source_target_pairs={{0,32},{32,0},{1,33},{33,1},{2,34},{34,2},{3,35},{35,3},{4,36},{36... | collective-permute-start | bytes 1671176 | tf_op jit(solution)/shard_map/ppermute | solution.py:197
  192.2 2.4 add_convert_fusion.2
  194.7 8.8 %collective-permute-start.11 = (bf16[64,2176]{1,0:T(8,128)(2,1)S(1)}, bf16[64,2176]{1,0:T(8,128)(2,1)S(1)}, u32[]{:S(2)}, u32[]{:S(2)}) collective-permute-start(bf16[64,2176]{1,0:T(8,128)(2,1)S(1)} %slice.115), channel_id=1, source_target_pairs={{0,1},{1,0},{2,3},{3,2},{4,5},{5,4},{6,7},{7,6},{8,9},{9,8},{10,11... | collective-permute-start | bytes 835592 | tf_op jit(solution)/shard_map/ppermute | solution.py:202
  204.1 2.9 %collective-permute-start.13 = (bf16[256,1152]{1,0:T(8,128)(2,1)S(1)}, bf16[256,1152]{1,0:T(8,128)(2,1)}, u32[]{:S(2)}, u32[]{:S(2)}) collective-permute-start(bf16[256,1152]{1,0:T(8,128)(2,1)S(1)} %get-tuple-element.80), channel_id=1, source_target_pairs={{0,192},{64,0},{128,64},{192,128},{1,193},{65,1},{129,65},{193,129... | collective-permute-start | bytes 1769480 | tf_op jit(solution)/shard_map/ppermute | solution.py:24
  207.1 15.7 %collective-permute-done.11 = bf16[64,2176]{1,0:T(8,128)(2,1)S(1)} collective-permute-done((bf16[64,2176]{1,0:T(8,128)(2,1)S(1)}, bf16[64,2176]{1,0:T(8,128)(2,1)S(1)}, u32[]{:S(2)}, u32[]{:S(2)}) %collective-permute-start.11) | collective-permute-done | bytes 278560 | tf_op jit(solution)/shard_map/ppermute | solution.py:202
  224.1 4.3 %all-to-all-start.4 = ((bf16[16,4,2048]{2,1,0:T(4,128)(2,1)}), bf16[16,4,2048]{2,1,0:T(4,128)(2,1)S(1)}, u32[]{:S(2)}, u32[]{:S(2)}) async-start(bf16[16,4,2048]{2,1,0:T(4,128)(2,1)} %reshape.149), calls=%async_computation.4 | async-start | bytes 524288 | tf_op jit(solution)/shard_map/all_to_all | solution.py:28
  228.4 7.3 %all-to-all-done.4 = bf16[16,4,2048]{2,1,0:T(4,128)(2,1)S(1)} async-done(((bf16[16,4,2048]{2,1,0:T(4,128)(2,1)}), bf16[16,4,2048]{2,1,0:T(4,128)(2,1)S(1)}, u32[]{:S(2)}, u32[]{:S(2)}) %all-to-all-start.4) | async-done | bytes 262176 | tf_op jit(solution)/shard_map/all_to_all | solution.py:28
  236.5 2.9 %broadcast_select_fusion = (bf16[256,1152]{1,0:T(8,128)(2,1)}, bf16[256,1152]{1,0:T(8,128)(2,1)S(1)}, bf16[256,1152]{1,0:T(8,128)(2,1)S(1)}) fusion(pred[]{:T(512)S(6)} %eq.101, bf16[512,1152]{1,0:T(8,128)(2,1)} %collective-permute-done.9, bf16[256,1152]{1,0:T(8,128)(2,1)} %collective-permute-done.12, bf16[512,1152]{1,0:T(8,128)(2,1)S(1)} %copy-done.2, ...), kind=kLoop, calls=%fused_computation.30 | loop fusion | flops 3833856 | bytes 5308417 | tf_op jit(solution)/shard_map/jit(_where)/select_n | solution.py:219
  239.4 3.1 %collective-permute-start.14 = (bf16[256,1152]{1,0:T(8,128)(2,1)}, bf16[256,1152]{1,0:T(8,128)(2,1)S(1)}, u32[]{:S(2)}, u32[]{:S(2)}) collective-permute-start(bf16[256,1152]{1,0:T(8,128)(2,1)} %get-tuple-element.106), channel_id=1, source_target_pairs={{0,32},{32,0},{1,33},{33,1},{2,34},{34,2},{3,35},{35,3},{4,36},{36... | collective-permute-start | bytes 1769480 | tf_op jit(solution)/shard_map/ppermute | solution.py:219
  243.5 3.9 %all-to-all-start.5 = ((f32[16,2,256]{2,1,0:T(2,128)}), f32[16,2,256]{2,1,0:T(2,128)S(1)}, u32[]{:S(2)}, u32[]{:S(2)}) async-start(f32[16,2,256]{2,1,0:T(2,128)} %bitcast.20), calls=%async_computation.5 | async-start | bytes 65536 | tf_op jit(solution)/shard_map/all_to_all | solution.py:28
  247.7 7.1 %all-to-all-done.5 = f32[16,2,256]{2,1,0:T(2,128)S(1)} async-done(((f32[16,2,256]{2,1,0:T(2,128)}), f32[16,2,256]{2,1,0:T(2,128)S(1)}, u32[]{:S(2)}, u32[]{:S(2)}) %all-to-all-start.5) | async-done | bytes 32800 | tf_op jit(solution)/shard_map/all_to_all | solution.py:28
  (101 shorter events, 25.2 us)
Async XLA Ops:
  0.6 7.0 %copy-start = (bf16[2048,64]{0,1:T(8,128)(2,1)S(1)}, bf16[2048,64]{0,1:T(8,128)(2,1)}, u32[]{:S(2)}) copy-start(bf16[2048,64]{0,1:T(8,128)(2,1)} %param.20) | copy-start | bytes 786436
  0.6 8.4 %copy-start.16 = (bf16[64,2048]{1,0:T(8,128)(2,1)S(1)}, bf16[64,2048]{1,0:T(8,128)(2,1)}, u32[]{:S(2)}) copy-start(bf16[64,2048]{1,0:T(8,128)(2,1)} %param.16) | copy-start | bytes 786436
  0.7 8.6 %copy-start.14 = (bf16[2,256,384]{2,1,0:T(8,128)(2,1)S(1)}, bf16[2,256,384]{2,1,0:T(8,128)(2,1)}, u32[]{:S(2)}) copy-start(bf16[2,256,384]{2,1,0:T(8,128)(2,1)} %param.21) | copy-start | bytes 1179652
  3.1 6.4 %copy-start.15 = (bf16[2,256,384]{2,1,0:T(8,128)(2,1)S(1)}, bf16[2,256,384]{2,1,0:T(8,128)(2,1)}, u32[]{:S(2)}) copy-start(bf16[2,256,384]{2,1,0:T(8,128)(2,1)} %param.22) | copy-start | bytes 1179652
  4.2 14.8 %collective-permute-start = (bf16[64,2176]{1,0:T(8,128)(2,1)S(1)}, bf16[64,2176]{1,0:T(8,128)(2,1)S(1)}, u32[]{:S(2)}, u32[]{:S(2)}) collective-permute-start(bf16[64,2176]{1,0:T(8,128)(2,1)S(1)} %concatenate.26), channel_id=1, source_target_pairs={{0,1},{1,0},{2,3},{3,2},{4,5},{5,4},{6,7},{7,6},{8,9},{9,8},{10,11... | collective-permute-start | bytes 835592 | tf_op jit(solution)/shard_map/ppermute | solution.py:132
  9.1 9.8 %collective-permute-start.1 = (bf16[64,2176]{1,0:T(8,128)(2,1)S(1)}, bf16[64,2176]{1,0:T(8,128)(2,1)S(1)}, u32[]{:S(2)}, u32[]{:S(2)}) collective-permute-start(bf16[64,2176]{1,0:T(8,128)(2,1)S(1)} %concatenate.28), channel_id=1, source_target_pairs={{0,1},{1,0},{2,3},{3,2},{4,5},{5,4},{6,7},{7,6},{8,9},{9,8},{10,11... | collective-permute-start | bytes 835592 | tf_op jit(solution)/shard_map/ppermute | solution.py:132
  11.0 7.9 %all-to-all-start.3 = ((bf16[2,256,1152]{1,2,0:T(8,128)(2,1)}), bf16[2,256,1152]{1,2,0:T(8,128)(2,1)S(1)}, u32[]{:S(2)}, u32[]{:S(2)}) async-start(bf16[2,256,1152]{1,2,0:T(8,128)(2,1)} %pad_maximum_fusion), calls=%async_computation.3 | async-start | bytes 2359296 | tf_op jit(solution)/shard_map/all_to_all | solution.py:28
  18.9 3.1 %copy-start.10 = (bf16[64,2176]{1,0:T(8,128)(2,1)}, bf16[64,2176]{1,0:T(8,128)(2,1)S(1)}, u32[]{:S(2)}) copy-start(bf16[64,2176]{1,0:T(8,128)(2,1)S(1)} %collective-permute-done.1) | copy-start | bytes 835588
  19.8 10.9 %collective-permute-start.2 = (bf16[128,2176]{1,0:T(8,128)(2,1)}, bf16[128,2176]{1,0:T(8,128)(2,1)}, u32[]{:S(2)}, u32[]{:S(2)}) collective-permute-start(bf16[128,2176]{1,0:T(8,128)(2,1)} %pad_maximum_fusion.10), channel_id=1, source_target_pairs={{0,32},{32,0},{1,33},{33,1},{2,34},{34,2},{3,35},{35,3},{4,36},{36... | collective-permute-start | bytes 1671176 | tf_op jit(solution)/shard_map/ppermute | solution.py:140
  22.0 9.9 %collective-permute-start.3 = (bf16[128,2176]{1,0:T(8,128)(2,1)}, bf16[128,2176]{1,0:T(8,128)(2,1)}, u32[]{:S(2)}, u32[]{:S(2)}) collective-permute-start(bf16[128,2176]{1,0:T(8,128)(2,1)} %pad_maximum_fusion.11), channel_id=1, source_target_pairs={{0,32},{32,0},{1,33},{33,1},{2,34},{34,2},{3,35},{35,3},{4,36},{36... | collective-permute-start | bytes 1671176 | tf_op jit(solution)/shard_map/ppermute | solution.py:140
  22.8 58.3 %collective-permute-start.5 = (bf16[512,1152]{1,0:T(8,128)(2,1)S(1)}, bf16[512,1152]{1,0:T(8,128)(2,1)S(1)}, u32[]{:S(2)}, u32[]{:S(2)}) collective-permute-start(bf16[512,1152]{1,0:T(8,128)(2,1)S(1)} %bitcast.67), channel_id=1, source_target_pairs={{0,192},{64,0},{128,64},{192,128},{1,193},{65,1},{129,65},{193,129... | collective-permute-start | bytes 3538952 | tf_op jit(solution)/shard_map/ppermute | solution.py:24
  28.8 52.4 %collective-permute-start.4 = (bf16[512,1152]{1,0:T(8,128)(2,1)S(1)}, bf16[512,1152]{1,0:T(8,128)(2,1)}, u32[]{:S(2)}, u32[]{:S(2)}) collective-permute-start(bf16[512,1152]{1,0:T(8,128)(2,1)S(1)} %bitcast.68), channel_id=1, source_target_pairs={{0,64},{64,128},{128,192},{192,0},{1,65},{65,129},{129,193},{193,1... | collective-permute-start | bytes 3538952 | tf_op jit(solution)/shard_map/ppermute | solution.py:24
  40.0 1.7 copy-start.9
  83.9 39.8 %collective-permute-start.6 = (bf16[256,1152]{1,0:T(8,128)(2,1)}, bf16[256,1152]{1,0:T(8,128)(2,1)S(1)}, u32[]{:S(2)}, u32[]{:S(2)}) collective-permute-start(bf16[256,1152]{1,0:T(8,128)(2,1)} %slice.75), channel_id=1, source_target_pairs={{0,64},{64,128},{128,192},{192,0},{1,65},{65,129},{129,193},{193,1... | collective-permute-start | bytes 1769480 | tf_op jit(solution)/shard_map/ppermute | solution.py:24
  85.2 38.6 %collective-permute-start.7 = (bf16[256,1152]{1,0:T(8,128)(2,1)}, bf16[256,1152]{1,0:T(8,128)(2,1)}, u32[]{:S(2)}, u32[]{:S(2)}) collective-permute-start(bf16[256,1152]{1,0:T(8,128)(2,1)} %slice.76), channel_id=1, source_target_pairs={{0,192},{64,0},{128,64},{192,128},{1,193},{65,1},{129,65},{193,129... | collective-permute-start | bytes 1769480 | tf_op jit(solution)/shard_map/ppermute | solution.py:24
  136.4 9.9 %copy-start.1 = (bf16[512,1152]{1,0:T(8,128)(2,1)}, bf16[512,1152]{1,0:T(8,128)(2,1)S(1)}, u32[]{:S(2)}) copy-start(bf16[512,1152]{1,0:T(8,128)(2,1)S(1)} %get-tuple-element.78) | copy-start | bytes 3538948
  136.4 9.9 %copy-start.3 = (bf16[256,1152]{1,0:T(8,128)(2,1)}, bf16[256,1152]{1,0:T(8,128)(2,1)S(1)}, u32[]{:S(2)}) copy-start(bf16[256,1152]{1,0:T(8,128)(2,1)S(1)} %get-tuple-element.73) | copy-start | bytes 1769476
  136.4 9.9 %copy-start.5 = (bf16[256,1152]{1,0:T(8,128)(2,1)}, bf16[256,1152]{1,0:T(8,128)(2,1)S(1)}, u32[]{:S(2)}) copy-start(bf16[256,1152]{1,0:T(8,128)(2,1)S(1)} %get-tuple-element.75) | copy-start | bytes 1769476
  136.4 46.2 %collective-permute-start.8 = (bf16[512,1152]{1,0:T(8,128)(2,1)}, bf16[512,1152]{1,0:T(8,128)(2,1)}, u32[]{:S(2)}, u32[]{:S(2)}) collective-permute-start(bf16[512,1152]{1,0:T(8,128)(2,1)} %get-tuple-element.70), channel_id=1, source_target_pairs={{0,64},{64,128},{128,192},{192,0},{1,65},{65,129},{129,193},{193,1... | collective-permute-start | bytes 3538952 | tf_op jit(solution)/shard_map/ppermute | solution.py:24
  137.4 45.2 %collective-permute-start.9 = (bf16[512,1152]{1,0:T(8,128)(2,1)}, bf16[512,1152]{1,0:T(8,128)(2,1)}, u32[]{:S(2)}, u32[]{:S(2)}) collective-permute-start(bf16[512,1152]{1,0:T(8,128)(2,1)} %get-tuple-element.71), channel_id=1, source_target_pairs={{0,192},{64,0},{128,64},{192,128},{1,193},{65,1},{129,65},{193,129... | collective-permute-start | bytes 3538952 | tf_op jit(solution)/shard_map/ppermute | solution.py:24
  146.3 1.8 copy-start.7
  182.6 9.5 %copy-start.6 = (bf16[256,1152]{1,0:T(8,128)(2,1)S(1)}, bf16[256,1152]{1,0:T(8,128)(2,1)}, u32[]{:S(2)}) copy-start(bf16[256,1152]{1,0:T(8,128)(2,1)} %copy-done.5) | copy-start | bytes 1769476
  185.7 6.5 %copy-start.4 = (bf16[256,1152]{1,0:T(8,128)(2,1)S(1)}, bf16[256,1152]{1,0:T(8,128)(2,1)}, u32[]{:S(2)}) copy-start(bf16[256,1152]{1,0:T(8,128)(2,1)} %copy-done.3) | copy-start | bytes 1769476
  185.7 8.8 %collective-permute-start.10 = (bf16[128,2176]{1,0:T(8,128)(2,1)S(1)}, bf16[128,2176]{1,0:T(8,128)(2,1)S(1)}, u32[]{:S(2)}, u32[]{:S(2)}) collective-permute-start(bf16[128,2176]{1,0:T(8,128)(2,1)S(1)} %slice.114), channel_id=1, source_target_pairs={{0,32},{32,0},{1,33},{33,1},{2,34},{34,2},{3,35},{35,3},{4,36},{36... | collective-permute-start | bytes 1671176 | tf_op jit(solution)/shard_map/ppermute | solution.py:197
  194.7 28.3 %copy-start.12 = (bf16[64,2048]{1,0:T(8,128)(2,1)S(1)}, bf16[64,2048]{1,0:T(8,128)(2,1)}, u32[]{:S(2)}) copy-start(bf16[64,2048]{1,0:T(8,128)(2,1)} %param.15) | copy-start | bytes 786436
  194.7 28.0 %collective-permute-start.11 = (bf16[64,2176]{1,0:T(8,128)(2,1)S(1)}, bf16[64,2176]{1,0:T(8,128)(2,1)S(1)}, u32[]{:S(2)}, u32[]{:S(2)}) collective-permute-start(bf16[64,2176]{1,0:T(8,128)(2,1)S(1)} %slice.115), channel_id=1, source_target_pairs={{0,1},{1,0},{2,3},{3,2},{4,5},{5,4},{6,7},{7,6},{8,9},{9,8},{10,11... | collective-permute-start | bytes 835592 | tf_op jit(solution)/shard_map/ppermute | solution.py:202
  203.5 33.0 %collective-permute-start.12 = (bf16[256,1152]{1,0:T(8,128)(2,1)}, bf16[256,1152]{1,0:T(8,128)(2,1)}, u32[]{:S(2)}, u32[]{:S(2)}) collective-permute-start(bf16[256,1152]{1,0:T(8,128)(2,1)} %get-tuple-element.79), channel_id=1, source_target_pairs={{0,64},{64,128},{128,192},{192,0},{1,65},{65,129},{129,193},{193,1... | collective-permute-start | bytes 1769480 | tf_op jit(solution)/shard_map/ppermute | solution.py:24
  204.1 32.4 %collective-permute-start.13 = (bf16[256,1152]{1,0:T(8,128)(2,1)S(1)}, bf16[256,1152]{1,0:T(8,128)(2,1)}, u32[]{:S(2)}, u32[]{:S(2)}) collective-permute-start(bf16[256,1152]{1,0:T(8,128)(2,1)S(1)} %get-tuple-element.80), channel_id=1, source_target_pairs={{0,192},{64,0},{128,64},{192,128},{1,193},{65,1},{129,65},{193,129... | collective-permute-start | bytes 1769480 | tf_op jit(solution)/shard_map/ppermute | solution.py:24
  222.8 13.7 %copy-start.2 = (bf16[512,1152]{1,0:T(8,128)(2,1)S(1)}, bf16[512,1152]{1,0:T(8,128)(2,1)}, u32[]{:S(2)}) copy-start(bf16[512,1152]{1,0:T(8,128)(2,1)} %copy-done.1) | copy-start | bytes 3538948
  224.1 11.7 %all-to-all-start.4 = ((bf16[16,4,2048]{2,1,0:T(4,128)(2,1)}), bf16[16,4,2048]{2,1,0:T(4,128)(2,1)S(1)}, u32[]{:S(2)}, u32[]{:S(2)}) async-start(bf16[16,4,2048]{2,1,0:T(4,128)(2,1)} %reshape.149), calls=%async_computation.4 | async-start | bytes 524288 | tf_op jit(solution)/shard_map/all_to_all | solution.py:28
  239.4 8.0 %collective-permute-start.14 = (bf16[256,1152]{1,0:T(8,128)(2,1)}, bf16[256,1152]{1,0:T(8,128)(2,1)S(1)}, u32[]{:S(2)}, u32[]{:S(2)}) collective-permute-start(bf16[256,1152]{1,0:T(8,128)(2,1)} %get-tuple-element.106), channel_id=1, source_target_pairs={{0,32},{32,0},{1,33},{33,1},{2,34},{34,2},{3,35},{35,3},{4,36},{36... | collective-permute-start | bytes 1769480 | tf_op jit(solution)/shard_map/ppermute | solution.py:219
  243.5 11.3 %all-to-all-start.5 = ((f32[16,2,256]{2,1,0:T(2,128)}), f32[16,2,256]{2,1,0:T(2,128)S(1)}, u32[]{:S(2)}, u32[]{:S(2)}) async-start(f32[16,2,256]{2,1,0:T(2,128)} %bitcast.20), calls=%async_computation.5 | async-start | bytes 65536 | tf_op jit(solution)/shard_map/all_to_all | solution.py:28
  (3 other events, 4.0 us)

commit v4 on v3

--- a/solution.py
+++ b/solution.py
@@ -193,25 +193,30 @@
     )
     (back,) = alone(ids, back.reshape(chips, 4 * CAP, wide))
     back, got_up, got_down = lax.optimization_barrier((back, got_up, got_down))
-    part = mm(pick, back.reshape(slots, wide), ((0,), (0,)))
+    back = back.reshape(slots, wide)
+    taken = mm(pick, back[:, width:], ((0,), (0,)))
+    taken = taken[: 2 * tok] + lax.ppermute(taken[2 * tok :].astype(BF16), "core", SWAP).astype(F32)
+    other_taken = lax.ppermute(taken[tok:].astype(BF16), "zl", SWAP)
+    part = mm(pick, back[:, :width], ((0,), (0,)))
     part = part[: 2 * tok] + lax.ppermute(part[2 * tok :].astype(BF16), "core", SWAP).astype(F32)
     for_other = part[tok:].astype(BF16)
     up = (g_next.astype(F32) + got_up[piece:].astype(F32)).astype(BF16)
     down = (g_prev.astype(F32) + got_down[:piece].astype(F32)).astype(BF16)
-    for_other, up, down = lax.optimization_barrier((for_other, up, down))
+    for_other, up, down, other_taken = lax.optimization_barrier(
+        (for_other, up, down, other_taken)
+    )
     other = lax.ppermute(for_other, "zl", SWAP)
     last_up, last_down = both_ways(up, down)
-    part = part[:tok] + other.astype(F32)
-
-    taken = part[:, width : width + EXPERTS].T
+    taken = (taken[:tok] + other_taken.astype(F32))[:, :EXPERTS].T
     mean = jnp.sum(taken, axis=0, keepdims=True)
     dlogits = jnp.where(chosen, (taken - gate * mean) * (1.0 - sig), 0.0).astype(BF16)
     term = mm(dlogits, tokens).astype(BF16).reshape(chips, 4, width)
-    grad_tokens = (part[:, :width] + mm(dlogits, router, ((0,), (1,)))).astype(BF16)
     term = jnp.sum(a2a(term, PLANE).astype(F32), axis=0)
     term = term.reshape(2, 2, 8, width // 8).transpose(2, 0, 1, 3).reshape(chips, 2, width // 8)
-    term, last_up, last_down = lax.optimization_barrier((term, last_up, last_down))
+    term, other, last_up, last_down = lax.optimization_barrier((term, other, last_up, last_down))
     term = a2a(term, ("zh", "core", "zl"))
+    part = part[:tok] + other.astype(F32)
+    grad_tokens = (part + mm(dlogits, router, ((0,), (1,)))).astype(BF16)
 
     low = g_own[:piece].astype(F32) + last_up.astype(F32) + got_down[piece:].astype(F32)
     high = g_own[piece:].astype(F32) + got_up[:piece].astype(F32) + last_down.astype(F32)

time: 258 us -> 261 us (1.012)
    ppermute x0 -> x2, starting transfers between devices: none -> 15.3 us  [the longest x1 8.85 us: per_device(): other_taken = lax.ppermute(taken[tok:].astype(BF16), 'zl', SWAP)]
    ppermute x1, starting transfers between devices: 8.8 us -> 1.55 us  [per_device(): other = lax.ppermute(for_other, 'zl', SWAP)]
    ppermute x1, starting transfers between devices: 6.42 us -> 0.1 us  [per_device(): lax.ppermute(part[2 * tok:].astype(BF16), 'core', SWAP).astype(F32)]
    all_to_all x3, waiting for transfers between devices: 16.3 us -> 12.9 us  [a2a(): return lax.all_to_all(a, axes, split_axis=0, concat_axis=0, tiled=True)]
    dot_general x8 -> x9, matrix products: 14.4 us -> 16.2 us  [mm(): return lax.dot_general(a, b, (dims, ((), ())), preferred_element_type=F32)]
  transfers between devices with their start and end apart: 18 -> 20, of which waited for: 4 -> 5; matrix products, arithmetic and copies ran while one was open for 8% -> 9% of each run, Pallas kernels for 2% -> 2%
where the time goes in v4:
time: 261 us; the launch traced here: 259 us
  blocking collectives  107 us (41%)
  starting transfers between devices  53.5 us (20%)
  waiting for transfers between devices  31.5 us (12%)
  Pallas kernels  18 us (7%)
  local copies, waits for them, and re-layouts  17.2 us (7%)
  matrix products  16.2 us (6%)
  other arithmetic  14.1 us (5%)
    all_to_all x3, blocking collectives, a2a(): return lax.all_to_all(a, axes, split_axis=0, concat_axis=0, tiled=True)  107 us
    ppermute x1, waiting for transfers between devices, per_device(): other = lax.ppermute(for_other, 'zl', SWAP)  18.3 us
    pallas_call x2, Pallas kernels, call(): pl.pallas_call(kernel, out_shape=outs, in_specs=[smem if a.dtype == jnp.i...  18 us
    ppermute x8, starting transfers between devices, both_ways(): return (lax.ppermute(up, 'zh', PLUS), lax.ppermute(down, 'zh', MINUS))  17.7 us
    dot_general x9, matrix products, mm(): return lax.dot_general(a, b, (dims, ((), ())), preferred_element_type=F32)  16.2 us
    all_to_all x3, starting transfers between devices, a2a(): return lax.all_to_all(a, axes, split_axis=0, concat_axis=0, tiled=True)  14.3 us
    all_to_all x3, waiting for transfers between devices, a2a(): return lax.all_to_all(a, axes, split_axis=0, concat_axis=0, tiled=True)  12.9 us
    ppermute x1, starting transfers between devices, per_device(): other_taken = lax.ppermute(taken[tok:].astype(BF16), 'zl', SWAP)  8.85 us
  transfers between devices with their start and end apart: 20, of which 5 were waited for; matrix products, arithmetic and copies ran while one was open for 9% of the time, Pallas kernels for 2%

profile of v4, /device:TPU:1, one launch (start us, length us, event | category | flops | bytes accessed | tf_op | source)
XLA Modules:
  0.0 259.5 jit_solution(7469753630781479778)
XLA Ops:
  4.2 2.6 collective-permute-start
  11.3 6.4 %all-to-all-start.3 = ((bf16[2,256,1152]{1,2,0:T(8,128)(2,1)}), bf16[2,256,1152]{1,2,0:T(8,128)(2,1)S(1)}, u32[]{:S(2)}, u32[]{:S(2)}) async-start(bf16[2,256,1152]{1,2,0:T(8,128)(2,1)} %pad_maximum_fusion), calls=%async_computation.3 | async-start | bytes 2359296 | tf_op jit(solution)/shard_map/all_to_all | solution.py:28
  17.7 1.8 all-to-all-done.3
  22.9 5.9 %collective-permute-start.5 = (bf16[512,1152]{1,0:T(8,128)(2,1)S(1)}, bf16[512,1152]{1,0:T(8,128)(2,1)S(1)}, u32[]{:S(2)}, u32[]{:S(2)}) collective-permute-start(bf16[512,1152]{1,0:T(8,128)(2,1)S(1)} %bitcast.67), channel_id=1, source_target_pairs={{0,192},{64,0},{128,64},{192,128},{1,193},{65,1},{129,65},{193,129... | collective-permute-start | bytes 3538952 | tf_op jit(solution)/shard_map/ppermute | solution.py:24
  34.4 3.4 %convolution_convert_fusion = bf16[640,2048]{1,0:T(8,128)(2,1)} fusion(bf16[640,256]{1,0:T(8,128)(2,1)S(1)} %fusion.7, bf16[128,2176]{1,0:T(8,128)(2,1)} %collective-permute-done.3, bf16[64,2176]{1,0:T(8,128)(2,1)S(1)} %copy-done.14, bf16[64,2176]{1,0:T(8,128)(2,1)S(1)} %concatenate.28), kind=kOutput, calls=%fused_computation | convolution fusion | flops 675545088 | bytes 4063232 | tf_op jit(solution)/shard_map/dot_general | solution.py:20
  37.9 3.4 %convolution_convert_fusion.1 = bf16[640,2048]{1,0:T(8,128)(2,1)} fusion(bf16[640,256]{1,0:T(8,128)(2,1)S(1)} %select_convert_fusion, bf16[128,2176]{1,0:T(8,128)(2,1)} %collective-permute-done.2, bf16[64,2176]{1,0:T(8,128)(2,1)S(1)} %copy-done.12, bf16[64,2176]{1,0:T(8,128)(2,1)S(1)} %concatenate.26), kind=kOutput, calls=%fused_computation.1 | convolution fusion | flops 675545088 | bytes 4063232 | tf_op jit(solution)/shard_map/dot_general | solution.py:20
  41.3 41.1 %conditional.3 = (bf16[16,40,2048]{2,1,0:T(8,128)(2,1)}) conditional(s32[]{:T(128)} %bitcast.8, bf16[16,40,2048]{2,1,0:T(8,128)(2,1)} %bitcast.78, bf16[16,40,2048]{2,1,0:T(8,128)(2,1)} %bitcast.79), branch_computations={%region_3.4_spmd, %region_4.5_spmd} | conditional | bytes 15728676 | solution.py:32
  41.3 1.7 copy-done.9
  43.0 39.4 %all_to_all.27 = bf16[16,40,2048]{2,1,0:T(8,128)(2,1)} all-to-all(bf16[16,40,2048]{2,1,0:T(8,128)(2,1)S(1)} %copy-done.9), channel_id=1, replica_groups=mesh['zh'=4,'core'=2,'x'=4,'y'=4,'zl'=2] {'x','y'}, dimensions={0} | all-to-all | bytes 5242880 | tf_op jit(solution)/shard_map/cond/branch_1_fun/all_to_all | solution.py:28
  82.4 1.9 slice.92
  86.5 2.3 collective-permute-start.7
  88.9 34.9 %conditional.4 = (bf16[16,40,2048]{2,1,0:T(8,128)(2,1)}) conditional(s32[]{:T(128)} %bitcast.8, bf16[16,40,2048]{2,1,0:T(8,128)(2,1)} %bitcast.75, bf16[16,40,2048]{2,1,0:T(8,128)(2,1)} %bitcast.76), branch_computations={%region_5.6_spmd, %region_6.7_spmd} | conditional | bytes 15728676 | solution.py:32
  88.9 1.7 copy-done.8
  90.6 33.2 %all_to_all.28 = bf16[16,40,2048]{2,1,0:T(8,128)(2,1)} all-to-all(bf16[16,40,2048]{2,1,0:T(8,128)(2,1)S(1)} %copy-done.8), channel_id=1, replica_groups=mesh['zh'=4,'core'=2,'x'=4,'y'=4,'zl'=2] {'x','y'}, dimensions={0} | all-to-all | bytes 5242880 | tf_op jit(solution)/shard_map/cond/branch_1_fun/all_to_all | solution.py:28
  123.8 12.6 %shard_map.128 = (bf16[640,768]{1,0:T(8,128)(2,1)S(1)}, f32[640,128]{1,0:T(8,128)S(1)}, bf16[512,1152]{1,0:T(8,128)(2,1)S(1)}, bf16[256,1152]{1,0:T(8,128)(2,1)S...) custom-call(s32[9]{0:T(128)S(1)} %pad_add_fusion.starts, ...), custom_call_target="tpu_custom_call" | custom-call | tf_op jit(solution)/shard_map/pallas_call | solution.py:100
  137.4 3.4 %collective-permute-start.9 = (bf16[512,1152]{1,0:T(8,128)(2,1)}, bf16[512,1152]{1,0:T(8,128)(2,1)}, u32[]{:S(2)}, u32[]{:S(2)}) collective-permute-start(bf16[512,1152]{1,0:T(8,128)(2,1)} %get-tuple-element.73), channel_id=1, source_target_pairs={{0,192},{64,0},{128,64},{192,128},{1,193},{65,1},{129,65},{193,129... | collective-permute-start | bytes 3538952 | tf_op jit(solution)/shard_map/ppermute | solution.py:24
  140.8 5.5 %shard_map.129 = bf16[640,2176]{1,0:T(8,128)(2,1)} custom-call(s32[9]{0:T(128)S(1)} %pad_add_fusion.starts, f32[640,128]{1,0:T(8,128)S(1)} %get-tuple-element.70.spread, bf16[640,768]{1,0:T(8,128)(2,1)S(1)} %get-tuple-element.71.pre_grad, bf16[512,1152]{1,0:T(8,128)(2,1)S(1)} %bitcast.70, bf16[512,1152]{1,0:T(8,128)(2,1)S(1)} %collective-permute-done.5.after, ...), custom_call_target="tpu_custom_call" | custom-call | tf_op jit(solution)/shard_map/pallas_call | solution.py:100
  146.3 36.4 %conditional.5 = (bf16[16,40,2176]{2,1,0:T(8,128)(2,1)}) conditional(s32[]{:T(128)} %bitcast.8, bf16[16,40,2176]{2,1,0:T(8,128)(2,1)} %bitcast.71, bf16[16,40,2176]{2,1,0:T(8,128)(2,1)} %bitcast.72), branch_computations={%region_7.8_spmd, %region_8.9_spmd} | conditional | bytes 16711716 | solution.py:32
  146.3 1.8 copy-done.7
  148.1 34.6 %all_to_all.29 = bf16[16,40,2176]{2,1,0:T(8,128)(2,1)} all-to-all(bf16[16,40,2176]{2,1,0:T(8,128)(2,1)S(1)} %copy-done.7), channel_id=1, replica_groups=mesh['zh'=4,'core'=2,'x'=4,'y'=4,'zl'=2] {'x','y'}, dimensions={0} | all-to-all | bytes 5570560 | tf_op jit(solution)/shard_map/cond/branch_1_fun/all_to_all | solution.py:28
  183.9 2.8 %fusion = f32[256,2048]{1,0:T(8,128)S(1)} fusion(bf16[640,256]{1,0:T(8,128)(2,1)S(1)} %select_convert_fusion, bf16[640,2176]{1,0:T(8,128)(2,1)} %bitcast.74), kind=kOutput, calls=%fused_computation.2 | convolution fusion | flops 671088640 | bytes 5046272 | tf_op jit(solution)/shard_map/dot_general | solution.py:20
  186.7 6.4 %collective-permute-start.11 = (bf16[128,128]{1,0:T(8,128)(2,1)S(1)}, bf16[128,128]{1,0:T(8,128)(2,1)S(1)}, u32[]{:S(2)}, u32[]{:S(2)}) collective-permute-start(bf16[128,128]{1,0:T(8,128)(2,1)S(1)} %slice.157), channel_id=1, source_target_pairs={{0,32},{32,0},{1,33},{33,1},{2,34},{34,2},{3,35},{35,3},{4,36},{36... | collective-permute-start | bytes 98312 | tf_op jit(solution)/shard_map/ppermute | solution.py:198
  193.3 2.4 add_convert_fusion.2
  195.8 8.9 %collective-permute-start.12 = (bf16[64,128]{1,0:T(8,128)(2,1)S(1)}, bf16[64,128]{1,0:T(8,128)(2,1)S(1)}, u32[]{:S(2)}, u32[]{:S(2)}) collective-permute-start(bf16[64,128]{1,0:T(8,128)(2,1)S(1)} %slice.158), channel_id=1, source_target_pairs={{0,1},{1,0},{2,3},{3,2},{4,5},{5,4},{6,7},{7,6},{8,9},{9,8},{10,11... | collective-permute-start | bytes 49160 | tf_op jit(solution)/shard_map/ppermute | solution.py:199
  206.8 3.1 %collective-permute-start.15 = (bf16[256,1152]{1,0:T(8,128)(2,1)S(1)}, bf16[256,1152]{1,0:T(8,128)(2,1)}, u32[]{:S(2)}, u32[]{:S(2)}) collective-permute-start(bf16[256,1152]{1,0:T(8,128)(2,1)S(1)} %get-tuple-element.82), channel_id=1, source_target_pairs={{0,192},{64,0},{128,64},{192,128},{1,193},{65,1},{129,65},{193,129... | collective-permute-start | bytes 1769480 | tf_op jit(solution)/shard_map/ppermute | solution.py:24
  210.9 4.4 %all-to-all-start.4 = ((bf16[16,4,2048]{2,1,0:T(4,128)(2,1)}), bf16[16,4,2048]{2,1,0:T(4,128)(2,1)S(1)}, u32[]{:S(2)}, u32[]{:S(2)}) async-start(bf16[16,4,2048]{2,1,0:T(4,128)(2,1)} %reshape.152), calls=%async_computation.4 | async-start | bytes 524288 | tf_op jit(solution)/shard_map/all_to_all | solution.py:28
  216.8 5.8 %all-to-all-done.4 = bf16[16,4,2048]{2,1,0:T(4,128)(2,1)S(1)} async-done(((bf16[16,4,2048]{2,1,0:T(4,128)(2,1)}), bf16[16,4,2048]{2,1,0:T(4,128)(2,1)S(1)}, u32[]{:S(2)}, u32[]{:S(2)}) %all-to-all-start.4) | async-done | bytes 262176 | tf_op jit(solution)/shard_map/all_to_all | solution.py:28
  223.4 18.3 %collective-permute-done.13 = bf16[64,2048]{1,0:T(8,128)(2,1)} collective-permute-done((bf16[64,2048]{1,0:T(8,128)(2,1)}, bf16[64,2048]{1,0:T(8,128)(2,1)}, u32[]{:S(2)}, u32[]{:S(2)}) %collective-permute-start.13) | collective-permute-done | bytes 262176 | tf_op jit(solution)/shard_map/ppermute | solution.py:208
  241.7 3.1 %broadcast_select_fusion = (bf16[256,1152]{1,0:T(8,128)(2,1)}, bf16[256,1152]{1,0:T(8,128)(2,1)S(1)}, bf16[256,1152]{1,0:T(8,128)(2,1)}) fusion(pred[]{:T(512)S(6)} %eq.89, bf16[512,1152]{1,0:T(8,128)(2,1)} %collective-permute-done.9, bf16[256,1152]{1,0:T(8,128)(2,1)} %collective-permute-done.14, bf16[512,1152]{1,0:T(8,128)(2,1)S(1)} %copy-done.2, ...), kind=kLoop, calls=%fused_computation.30 | loop fusion | flops 3833856 | bytes 5308417 | tf_op jit(solution)/shard_map/jit(_where)/select_n | solution.py:224
  245.9 3.6 %all-to-all-start.5 = ((f32[16,2,256]{2,1,0:T(2,128)}), f32[16,2,256]{2,1,0:T(2,128)S(1)}, u32[]{:S(2)}, u32[]{:S(2)}) async-start(f32[16,2,256]{2,1,0:T(2,128)} %bitcast.20), calls=%async_computation.5 | async-start | bytes 65536 | tf_op jit(solution)/shard_map/all_to_all | solution.py:28
  249.5 1.9 fusion.10
  251.7 5.3 %all-to-all-done.5 = f32[16,2,256]{2,1,0:T(2,128)S(1)} async-done(((f32[16,2,256]{2,1,0:T(2,128)}), f32[16,2,256]{2,1,0:T(2,128)S(1)}, u32[]{:S(2)}, u32[]{:S(2)}) %all-to-all-start.5) | async-done | bytes 32800 | tf_op jit(solution)/shard_map/all_to_all | solution.py:28
  (130 shorter events, 30.3 us)
Async XLA Ops:
  0.6 9.0 %copy-start.19 = (bf16[64,2048]{1,0:T(8,128)(2,1)S(1)}, bf16[64,2048]{1,0:T(8,128)(2,1)}, u32[]{:S(2)}) copy-start(bf16[64,2048]{1,0:T(8,128)(2,1)} %param.16) | copy-start | bytes 786436
  0.7 9.2 %copy-start.17 = (bf16[2,256,384]{2,1,0:T(8,128)(2,1)S(1)}, bf16[2,256,384]{2,1,0:T(8,128)(2,1)}, u32[]{:S(2)}) copy-start(bf16[2,256,384]{2,1,0:T(8,128)(2,1)} %param.21) | copy-start | bytes 1179652
  4.2 15.4 %collective-permute-start = (bf16[64,2176]{1,0:T(8,128)(2,1)S(1)}, bf16[64,2176]{1,0:T(8,128)(2,1)S(1)}, u32[]{:S(2)}, u32[]{:S(2)}) collective-permute-start(bf16[64,2176]{1,0:T(8,128)(2,1)S(1)} %concatenate.26), channel_id=1, source_target_pairs={{0,1},{1,0},{2,3},{3,2},{4,5},{5,4},{6,7},{7,6},{8,9},{9,8},{10,11... | collective-permute-start | bytes 835592 | tf_op jit(solution)/shard_map/ppermute | solution.py:132
  9.7 9.8 %collective-permute-start.1 = (bf16[64,2176]{1,0:T(8,128)(2,1)S(1)}, bf16[64,2176]{1,0:T(8,128)(2,1)S(1)}, u32[]{:S(2)}, u32[]{:S(2)}) collective-permute-start(bf16[64,2176]{1,0:T(8,128)(2,1)S(1)} %concatenate.28), channel_id=1, source_target_pairs={{0,1},{1,0},{2,3},{3,2},{4,5},{5,4},{6,7},{7,6},{8,9},{9,8},{10,11... | collective-permute-start | bytes 835592 | tf_op jit(solution)/shard_map/ppermute | solution.py:132
  11.3 8.2 %all-to-all-start.3 = ((bf16[2,256,1152]{1,2,0:T(8,128)(2,1)}), bf16[2,256,1152]{1,2,0:T(8,128)(2,1)S(1)}, u32[]{:S(2)}, u32[]{:S(2)}) async-start(bf16[2,256,1152]{1,2,0:T(8,128)(2,1)} %pad_maximum_fusion), calls=%async_computation.3 | async-start | bytes 2359296 | tf_op jit(solution)/shard_map/all_to_all | solution.py:28
  19.6 11.8 %copy-start.11 = (bf16[64,2176]{1,0:T(8,128)(2,1)}, bf16[64,2176]{1,0:T(8,128)(2,1)S(1)}, u32[]{:S(2)}) copy-start(bf16[64,2176]{1,0:T(8,128)(2,1)S(1)} %collective-permute-done) | copy-start | bytes 835588
  20.5 10.9 %collective-permute-start.2 = (bf16[128,2176]{1,0:T(8,128)(2,1)}, bf16[128,2176]{1,0:T(8,128)(2,1)}, u32[]{:S(2)}, u32[]{:S(2)}) collective-permute-start(bf16[128,2176]{1,0:T(8,128)(2,1)} %pad_maximum_fusion.10), channel_id=1, source_target_pairs={{0,32},{32,0},{1,33},{33,1},{2,34},{34,2},{3,35},{35,3},{4,36},{36... | collective-permute-start | bytes 1671176 | tf_op jit(solution)/shard_map/ppermute | solution.py:140
  22.1 11.2 %collective-permute-start.3 = (bf16[128,2176]{1,0:T(8,128)(2,1)}, bf16[128,2176]{1,0:T(8,128)(2,1)}, u32[]{:S(2)}, u32[]{:S(2)}) collective-permute-start(bf16[128,2176]{1,0:T(8,128)(2,1)} %pad_maximum_fusion.11), channel_id=1, source_target_pairs={{0,32},{32,0},{1,33},{33,1},{2,34},{34,2},{3,35},{35,3},{4,36},{36... | collective-permute-start | bytes 1671176 | tf_op jit(solution)/shard_map/ppermute | solution.py:140
  22.9 59.6 %collective-permute-start.5 = (bf16[512,1152]{1,0:T(8,128)(2,1)S(1)}, bf16[512,1152]{1,0:T(8,128)(2,1)S(1)}, u32[]{:S(2)}, u32[]{:S(2)}) collective-permute-start(bf16[512,1152]{1,0:T(8,128)(2,1)S(1)} %bitcast.67), channel_id=1, source_target_pairs={{0,192},{64,0},{128,64},{192,128},{1,193},{65,1},{129,65},{193,129... | collective-permute-start | bytes 3538952 | tf_op jit(solution)/shard_map/ppermute | solution.py:24
  28.8 53.7 %collective-permute-start.4 = (bf16[512,1152]{1,0:T(8,128)(2,1)S(1)}, bf16[512,1152]{1,0:T(8,128)(2,1)}, u32[]{:S(2)}, u32[]{:S(2)}) collective-permute-start(bf16[512,1152]{1,0:T(8,128)(2,1)S(1)} %bitcast.68), channel_id=1, source_target_pairs={{0,64},{64,128},{128,192},{192,0},{1,65},{65,129},{129,193},{193,1... | collective-permute-start | bytes 3538952 | tf_op jit(solution)/shard_map/ppermute | solution.py:24
  85.2 38.6 %collective-permute-start.6 = (bf16[256,1152]{1,0:T(8,128)(2,1)}, bf16[256,1152]{1,0:T(8,128)(2,1)S(1)}, u32[]{:S(2)}, u32[]{:S(2)}) collective-permute-start(bf16[256,1152]{1,0:T(8,128)(2,1)} %slice.92), channel_id=1, source_target_pairs={{0,64},{64,128},{128,192},{192,0},{1,65},{65,129},{129,193},{193,1... | collective-permute-start | bytes 1769480 | tf_op jit(solution)/shard_map/ppermute | solution.py:24
  86.5 37.3 %collective-permute-start.7 = (bf16[256,1152]{1,0:T(8,128)(2,1)}, bf16[256,1152]{1,0:T(8,128)(2,1)}, u32[]{:S(2)}, u32[]{:S(2)}) collective-permute-start(bf16[256,1152]{1,0:T(8,128)(2,1)} %slice.93), channel_id=1, source_target_pairs={{0,192},{64,0},{128,64},{192,128},{1,193},{65,1},{129,65},{193,129... | collective-permute-start | bytes 1769480 | tf_op jit(solution)/shard_map/ppermute | solution.py:24
  136.4 9.9 %copy-start.1 = (bf16[512,1152]{1,0:T(8,128)(2,1)}, bf16[512,1152]{1,0:T(8,128)(2,1)S(1)}, u32[]{:S(2)}) copy-start(bf16[512,1152]{1,0:T(8,128)(2,1)S(1)} %get-tuple-element.84) | copy-start | bytes 3538948
  136.4 9.8 %copy-start.3 = (bf16[256,1152]{1,0:T(8,128)(2,1)}, bf16[256,1152]{1,0:T(8,128)(2,1)S(1)}, u32[]{:S(2)}) copy-start(bf16[256,1152]{1,0:T(8,128)(2,1)S(1)} %get-tuple-element.75) | copy-start | bytes 1769476
  136.4 9.8 %copy-start.5 = (bf16[256,1152]{1,0:T(8,128)(2,1)}, bf16[256,1152]{1,0:T(8,128)(2,1)S(1)}, u32[]{:S(2)}) copy-start(bf16[256,1152]{1,0:T(8,128)(2,1)S(1)} %get-tuple-element.77) | copy-start | bytes 1769476
  136.4 46.2 %collective-permute-start.8 = (bf16[512,1152]{1,0:T(8,128)(2,1)}, bf16[512,1152]{1,0:T(8,128)(2,1)}, u32[]{:S(2)}, u32[]{:S(2)}) collective-permute-start(bf16[512,1152]{1,0:T(8,128)(2,1)} %get-tuple-element.72), channel_id=1, source_target_pairs={{0,64},{64,128},{128,192},{192,0},{1,65},{65,129},{129,193},{193,1... | collective-permute-start | bytes 3538952 | tf_op jit(solution)/shard_map/ppermute | solution.py:24
  137.4 45.2 %collective-permute-start.9 = (bf16[512,1152]{1,0:T(8,128)(2,1)}, bf16[512,1152]{1,0:T(8,128)(2,1)}, u32[]{:S(2)}, u32[]{:S(2)}) collective-permute-start(bf16[512,1152]{1,0:T(8,128)(2,1)} %get-tuple-element.73), channel_id=1, source_target_pairs={{0,192},{64,0},{128,64},{192,128},{1,193},{65,1},{129,65},{193,129... | collective-permute-start | bytes 3538952 | tf_op jit(solution)/shard_map/ppermute | solution.py:24
  183.9 9.4 %copy-start.6 = (bf16[256,1152]{1,0:T(8,128)(2,1)S(1)}, bf16[256,1152]{1,0:T(8,128)(2,1)}, u32[]{:S(2)}) copy-start(bf16[256,1152]{1,0:T(8,128)(2,1)} %copy-done.5) | copy-start | bytes 1769476
  186.7 9.0 %collective-permute-start.11 = (bf16[128,128]{1,0:T(8,128)(2,1)S(1)}, bf16[128,128]{1,0:T(8,128)(2,1)S(1)}, u32[]{:S(2)}, u32[]{:S(2)}) collective-permute-start(bf16[128,128]{1,0:T(8,128)(2,1)S(1)} %slice.157), channel_id=1, source_target_pairs={{0,32},{32,0},{1,33},{33,1},{2,34},{34,2},{3,35},{35,3},{4,36},{36... | collective-permute-start | bytes 98312 | tf_op jit(solution)/shard_map/ppermute | solution.py:198
  193.2 11.4 %collective-permute-start.10 = (bf16[128,2048]{1,0:T(8,128)(2,1)S(1)}, bf16[128,2048]{1,0:T(8,128)(2,1)S(1)}, u32[]{:S(2)}, u32[]{:S(2)}) collective-permute-start(bf16[128,2048]{1,0:T(8,128)(2,1)S(1)} %slice.155), channel_id=1, source_target_pairs={{0,32},{32,0},{1,33},{33,1},{2,34},{34,2},{3,35},{35,3},{4,36},{36... | collective-permute-start | bytes 1572872 | tf_op jit(solution)/shard_map/ppermute | solution.py:201
  195.7 10.1 %copy-start.21 = (f32[64,64]{0,1:T(8,128)S(1)}, f32[64,64]{0,1:T(8,128)}, u32[]{:S(2)}) copy-start(f32[64,64]{0,1:T(8,128)} %copy-done.20) | copy-start | bytes 49156
  195.7 10.1 %copy-start.23 = (pred[64,64]{0,1:T(32,128)(4,1)S(1)}, pred[64,64]{0,1:T(32,128)(4,1)}, u32[]{:S(2)}) copy-start(pred[64,64]{0,1:T(32,128)(4,1)} %copy-done.22) | copy-start | bytes 12292
  195.8 10.1 %copy-start.26 = (f32[64]{0:T(128)S(1)}, f32[64]{0:T(128)}, u32[]{:S(2)}) copy-start(f32[64]{0:T(128)} %copy-done.25) | copy-start | bytes 772
  195.8 14.1 %copy-start.15 = (bf16[64,2048]{1,0:T(8,128)(2,1)S(1)}, bf16[64,2048]{1,0:T(8,128)(2,1)}, u32[]{:S(2)}) copy-start(bf16[64,2048]{1,0:T(8,128)(2,1)} %param.15) | copy-start | bytes 786436
  195.8 10.0 %collective-permute-start.12 = (bf16[64,128]{1,0:T(8,128)(2,1)S(1)}, bf16[64,128]{1,0:T(8,128)(2,1)S(1)}, u32[]{:S(2)}, u32[]{:S(2)}) collective-permute-start(bf16[64,128]{1,0:T(8,128)(2,1)S(1)} %slice.158), channel_id=1, source_target_pairs={{0,1},{1,0},{2,3},{3,2},{4,5},{5,4},{6,7},{7,6},{8,9},{9,8},{10,11... | collective-permute-start | bytes 49160 | tf_op jit(solution)/shard_map/ppermute | solution.py:199
  205.5 36.2 %copy-start.2 = (bf16[512,1152]{1,0:T(8,128)(2,1)S(1)}, bf16[512,1152]{1,0:T(8,128)(2,1)}, u32[]{:S(2)}) copy-start(bf16[512,1152]{1,0:T(8,128)(2,1)} %copy-done.1) | copy-start | bytes 3538948
  206.0 35.7 %collective-permute-start.14 = (bf16[256,1152]{1,0:T(8,128)(2,1)}, bf16[256,1152]{1,0:T(8,128)(2,1)}, u32[]{:S(2)}, u32[]{:S(2)}) collective-permute-start(bf16[256,1152]{1,0:T(8,128)(2,1)} %get-tuple-element.81), channel_id=1, source_target_pairs={{0,64},{64,128},{128,192},{192,0},{1,65},{65,129},{129,193},{193,1... | collective-permute-start | bytes 1769480 | tf_op jit(solution)/shard_map/ppermute | solution.py:24
  206.8 34.9 %collective-permute-start.15 = (bf16[256,1152]{1,0:T(8,128)(2,1)S(1)}, bf16[256,1152]{1,0:T(8,128)(2,1)}, u32[]{:S(2)}, u32[]{:S(2)}) collective-permute-start(bf16[256,1152]{1,0:T(8,128)(2,1)S(1)} %get-tuple-element.82), channel_id=1, source_target_pairs={{0,192},{64,0},{128,64},{192,128},{1,193},{65,1},{129,65},{193,129... | collective-permute-start | bytes 1769480 | tf_op jit(solution)/shard_map/ppermute | solution.py:24
  210.9 11.7 %all-to-all-start.4 = ((bf16[16,4,2048]{2,1,0:T(4,128)(2,1)}), bf16[16,4,2048]{2,1,0:T(4,128)(2,1)S(1)}, u32[]{:S(2)}, u32[]{:S(2)}) async-start(bf16[16,4,2048]{2,1,0:T(4,128)(2,1)} %reshape.152), calls=%async_computation.4 | async-start | bytes 524288 | tf_op jit(solution)/shard_map/all_to_all | solution.py:28
  215.3 26.4 %collective-permute-start.13 = (bf16[64,2048]{1,0:T(8,128)(2,1)}, bf16[64,2048]{1,0:T(8,128)(2,1)}, u32[]{:S(2)}, u32[]{:S(2)}) collective-permute-start(bf16[64,2048]{1,0:T(8,128)(2,1)} %slice.156), channel_id=1, source_target_pairs={{0,1},{1,0},{2,3},{3,2},{4,5},{5,4},{6,7},{7,6},{8,9},{9,8},{10,11... | collective-permute-start | bytes 786440 | tf_op jit(solution)/shard_map/ppermute | solution.py:208
  244.8 6.6 %collective-permute-start.16 = (bf16[256,1152]{1,0:T(8,128)(2,1)}, bf16[256,1152]{1,0:T(8,128)(2,1)S(1)}, u32[]{:S(2)}, u32[]{:S(2)}) collective-permute-start(bf16[256,1152]{1,0:T(8,128)(2,1)} %get-tuple-element.110), channel_id=1, source_target_pairs={{0,32},{32,0},{1,33},{33,1},{2,34},{34,2},{3,35},{35,3},{4,36},{36... | collective-permute-start | bytes 1769480 | tf_op jit(solution)/shard_map/ppermute | solution.py:224
  245.9 11.0 %all-to-all-start.5 = ((f32[16,2,256]{2,1,0:T(2,128)}), f32[16,2,256]{2,1,0:T(2,128)S(1)}, u32[]{:S(2)}, u32[]{:S(2)}) async-start(f32[16,2,256]{2,1,0:T(2,128)} %bitcast.20), calls=%async_computation.5 | async-start | bytes 65536 | tf_op jit(solution)/shard_map/all_to_all | solution.py:28
  (15 other events, 47.0 us)

commit v5 on v4

--- a/solution.py
+++ b/solution.py
@@ -213,8 +213,8 @@
     term = mm(dlogits, tokens).astype(BF16).reshape(chips, 4, width)
     term = jnp.sum(a2a(term, PLANE).astype(F32), axis=0)
     term = term.reshape(2, 2, 8, width // 8).transpose(2, 0, 1, 3).reshape(chips, 2, width // 8)
+    term = a2a(term, ("zh", "core", "zl"))
     term, other, last_up, last_down = lax.optimization_barrier((term, other, last_up, last_down))
-    term = a2a(term, ("zh", "core", "zl"))
     part = part[:tok] + other.astype(F32)
     grad_tokens = (part + mm(dlogits, router, ((0,), (1,)))).astype(BF16)
 
@@ -223,14 +223,18 @@
     low, high = low.astype(BF16), high.astype(BF16)
     other = lax.ppermute(jnp.where(core == 0, high, low), "core", SWAP)
     mine = jnp.where(core == 0, low, high)
-    total = jnp.stack([jnp.where(core == 0, mine, other), jnp.where(core == 0, other, mine)])
-    total, term = lax.optimization_barrier((total, term))
     grad_router = jnp.sum(term, axis=0)
+
+    def by_expert(at):
+        cols = slice(at * hid, (at + 1) * hid)
+        a, b = mine[:, cols], other[:, cols]
+        return jnp.stack([jnp.where(core == 0, a, b), jnp.where(core == 0, b, a)])
+
     return (
         grad_tokens,
-        total[:, :, :hid],
-        total[:, :, hid : 2 * hid],
-        jnp.swapaxes(total[:, :, 2 * hid :], 1, 2),
+        by_expert(0),
+        by_expert(1),
+        jnp.swapaxes(by_expert(2), 1, 2),
         grad_router,
     )
 

time: 261 us -> 256 us (0.981)
  waiting for transfers between devices: 31.5 us -> 21 us
    ppermute x1, waiting for transfers between devices: 18.3 us -> 11.8 us  [per_device(): other = lax.ppermute(for_other, 'zl', SWAP)]
    all_to_all x3, waiting for transfers between devices: 12.9 us -> 8.87 us  [a2a(): return lax.all_to_all(a, axes, split_axis=0, concat_axis=0, tiled=True)]
    all_to_all x3, starting transfers between devices: 14.3 us -> 17.6 us  [a2a(): return lax.all_to_all(a, axes, split_axis=0, concat_axis=0, tiled=True)]
  transfers between devices with their start and end apart: 20 -> 20, of which waited for: 5 -> 5; matrix products, arithmetic and copies ran while one was open for 9% -> 10% of each run, Pallas kernels for 2% -> 2%
where the time goes in v5:
time: 256 us; the launch traced here: 255 us
  blocking collectives  107 us (42%)
  starting transfers between devices  56 us (22%)
  waiting for transfers between devices  21 us (8%)
  Pallas kernels  18 us (7%)
  local copies, waits for them, and re-layouts  17.9 us (7%)
  other arithmetic  16.7 us (7%)
  matrix products  16.2 us (6%)
    all_to_all x3, blocking collectives, a2a(): return lax.all_to_all(a, axes, split_axis=0, concat_axis=0, tiled=True)  107 us
    pallas_call x2, Pallas kernels, call(): pl.pallas_call(kernel, out_shape=outs, in_specs=[smem if a.dtype == jnp.i...  18 us
    ppermute x8, starting transfers between devices, both_ways(): return (lax.ppermute(up, 'zh', PLUS), lax.ppermute(down, 'zh', MINUS))  17.7 us
    all_to_all x3, starting transfers between devices, a2a(): return lax.all_to_all(a, axes, split_axis=0, concat_axis=0, tiled=True)  17.6 us
    dot_general x9, matrix products, mm(): return lax.dot_general(a, b, (dims, ((), ())), preferred_element_type=F32)  16.2 us
    ppermute x1, waiting for transfers between devices, per_device(): other = lax.ppermute(for_other, 'zl', SWAP)  11.8 us
    all_to_all x3, waiting for transfers between devices, a2a(): return lax.all_to_all(a, axes, split_axis=0, concat_axis=0, tiled=True)  8.87 us
    ppermute x1, starting transfers between devices, per_device(): other_taken = lax.ppermute(taken[tok:].astype(BF16), 'zl', SWAP)  8.85 us
  transfers between devices with their start and end apart: 20, of which 5 were waited for; matrix products, arithmetic and copies ran while one was open for 10% of the time, Pallas kernels for 2%

profile of v5, /device:TPU:1, one launch (start us, length us, event | category | flops | bytes accessed | tf_op | source)
XLA Modules:
  0.0 254.8 jit_solution(8746720109701305555)
XLA Ops:
  4.2 2.6 %collective-permute-start = (bf16[64,2176]{1,0:T(8,128)(2,1)S(1)}, bf16[64,2176]{1,0:T(8,128)(2,1)S(1)}, u32[]{:S(2)}, u32[]{:S(2)}) collective-permute-start(bf16[64,2176]{1,0:T(8,128)(2,1)S(1)} %concatenate.26), channel_id=1, source_target_pairs={{0,1},{1,0},{2,3},{3,2},{4,5},{5,4},{6,7},{7,6},{8,9},{9,8},{10,11... | collective-permute-start | bytes 835592 | tf_op jit(solution)/shard_map/ppermute | solution.py:132
  11.3 6.4 %all-to-all-start.3 = ((bf16[2,256,1152]{1,2,0:T(8,128)(2,1)}), bf16[2,256,1152]{1,2,0:T(8,128)(2,1)S(1)}, u32[]{:S(2)}, u32[]{:S(2)}) async-start(bf16[2,256,1152]{1,2,0:T(8,128)(2,1)} %pad_maximum_fusion), calls=%async_computation.3 | async-start | bytes 2359296 | tf_op jit(solution)/shard_map/all_to_all | solution.py:28
  17.7 1.8 all-to-all-done.3
  22.9 5.9 %collective-permute-start.5 = (bf16[512,1152]{1,0:T(8,128)(2,1)S(1)}, bf16[512,1152]{1,0:T(8,128)(2,1)S(1)}, u32[]{:S(2)}, u32[]{:S(2)}) collective-permute-start(bf16[512,1152]{1,0:T(8,128)(2,1)S(1)} %bitcast.75), channel_id=1, source_target_pairs={{0,192},{64,0},{128,64},{192,128},{1,193},{65,1},{129,65},{193,129... | collective-permute-start | bytes 3538952 | tf_op jit(solution)/shard_map/ppermute | solution.py:24
  34.4 3.4 %convolution_convert_fusion = bf16[640,2048]{1,0:T(8,128)(2,1)} fusion(bf16[640,256]{1,0:T(8,128)(2,1)S(1)} %fusion.7, bf16[128,2176]{1,0:T(8,128)(2,1)} %collective-permute-done.3, bf16[64,2176]{1,0:T(8,128)(2,1)S(1)} %copy-done.13, bf16[64,2176]{1,0:T(8,128)(2,1)S(1)} %concatenate.28), kind=kOutput, calls=%fused_computation | convolution fusion | flops 675545088 | bytes 4063232 | tf_op jit(solution)/shard_map/dot_general | solution.py:20
  37.9 3.4 %convolution_convert_fusion.1 = bf16[640,2048]{1,0:T(8,128)(2,1)} fusion(bf16[640,256]{1,0:T(8,128)(2,1)S(1)} %select_convert_fusion, bf16[128,2176]{1,0:T(8,128)(2,1)} %collective-permute-done.2, bf16[64,2176]{1,0:T(8,128)(2,1)S(1)} %copy-done.11, bf16[64,2176]{1,0:T(8,128)(2,1)S(1)} %concatenate.26), kind=kOutput, calls=%fused_computation.1 | convolution fusion | flops 675545088 | bytes 4063232 | tf_op jit(solution)/shard_map/dot_general | solution.py:20
  41.3 41.1 %conditional.3 = (bf16[16,40,2048]{2,1,0:T(8,128)(2,1)}) conditional(s32[]{:T(128)} %bitcast.8, bf16[16,40,2048]{2,1,0:T(8,128)(2,1)} %bitcast.86, bf16[16,40,2048]{2,1,0:T(8,128)(2,1)} %bitcast.87), branch_computations={%region_3.4_spmd, %region_4.5_spmd} | conditional | bytes 15728676 | solution.py:32
  41.3 1.7 copy-done.9
  43.0 39.4 %all_to_all.27 = bf16[16,40,2048]{2,1,0:T(8,128)(2,1)} all-to-all(bf16[16,40,2048]{2,1,0:T(8,128)(2,1)S(1)} %copy-done.9), channel_id=1, replica_groups=mesh['zh'=4,'core'=2,'x'=4,'y'=4,'zl'=2] {'x','y'}, dimensions={0} | all-to-all | bytes 5242880 | tf_op jit(solution)/shard_map/cond/branch_1_fun/all_to_all | solution.py:28
  82.4 1.9 slice.101
  86.5 2.3 collective-permute-start.7
  88.9 34.9 %conditional.4 = (bf16[16,40,2048]{2,1,0:T(8,128)(2,1)}) conditional(s32[]{:T(128)} %bitcast.8, bf16[16,40,2048]{2,1,0:T(8,128)(2,1)} %bitcast.83, bf16[16,40,2048]{2,1,0:T(8,128)(2,1)} %bitcast.84), branch_computations={%region_5.6_spmd, %region_6.7_spmd} | conditional | bytes 15728676 | solution.py:32
  88.9 1.7 copy-done.8
  90.6 33.2 %all_to_all.28 = bf16[16,40,2048]{2,1,0:T(8,128)(2,1)} all-to-all(bf16[16,40,2048]{2,1,0:T(8,128)(2,1)S(1)} %copy-done.8), channel_id=1, replica_groups=mesh['zh'=4,'core'=2,'x'=4,'y'=4,'zl'=2] {'x','y'}, dimensions={0} | all-to-all | bytes 5242880 | tf_op jit(solution)/shard_map/cond/branch_1_fun/all_to_all | solution.py:28
  123.8 12.6 %shard_map.128 = (bf16[640,768]{1,0:T(8,128)(2,1)S(1)}, f32[640,128]{1,0:T(8,128)S(1)}, bf16[512,1152]{1,0:T(8,128)(2,1)S(1)}, bf16[256,1152]{1,0:T(8,128)(2,1)S...) custom-call(s32[9]{0:T(128)S(1)} %pad_add_fusion.starts, ...), custom_call_target="tpu_custom_call" | custom-call | tf_op jit(solution)/shard_map/pallas_call | solution.py:100
  137.4 3.4 %collective-permute-start.9 = (bf16[512,1152]{1,0:T(8,128)(2,1)}, bf16[512,1152]{1,0:T(8,128)(2,1)}, u32[]{:S(2)}, u32[]{:S(2)}) collective-permute-start(bf16[512,1152]{1,0:T(8,128)(2,1)} %get-tuple-element.71), channel_id=1, source_target_pairs={{0,192},{64,0},{128,64},{192,128},{1,193},{65,1},{129,65},{193,129... | collective-permute-start | bytes 3538952 | tf_op jit(solution)/shard_map/ppermute | solution.py:24
  140.8 5.5 %shard_map.129 = bf16[640,2176]{1,0:T(8,128)(2,1)} custom-call(s32[9]{0:T(128)S(1)} %pad_add_fusion.starts, f32[640,128]{1,0:T(8,128)S(1)} %get-tuple-element.68.spread, bf16[640,768]{1,0:T(8,128)(2,1)S(1)} %get-tuple-element.69.pre_grad, bf16[512,1152]{1,0:T(8,128)(2,1)S(1)} %bitcast.78, bf16[512,1152]{1,0:T(8,128)(2,1)S(1)} %collective-permute-done.5.after, ...), custom_call_target="tpu_custom_call" | custom-call | tf_op jit(solution)/shard_map/pallas_call | solution.py:100
  146.3 36.4 %conditional.5 = (bf16[16,40,2176]{2,1,0:T(8,128)(2,1)}) conditional(s32[]{:T(128)} %bitcast.8, bf16[16,40,2176]{2,1,0:T(8,128)(2,1)} %bitcast.79, bf16[16,40,2176]{2,1,0:T(8,128)(2,1)} %bitcast.80), branch_computations={%region_7.8_spmd, %region_8.9_spmd} | conditional | bytes 16711716 | solution.py:32
  146.3 1.8 copy-done.7
  148.1 34.6 %all_to_all.29 = bf16[16,40,2176]{2,1,0:T(8,128)(2,1)} all-to-all(bf16[16,40,2176]{2,1,0:T(8,128)(2,1)S(1)} %copy-done.7), channel_id=1, replica_groups=mesh['zh'=4,'core'=2,'x'=4,'y'=4,'zl'=2] {'x','y'}, dimensions={0} | all-to-all | bytes 5570560 | tf_op jit(solution)/shard_map/cond/branch_1_fun/all_to_all | solution.py:28
  183.9 2.8 %fusion = f32[256,2048]{1,0:T(8,128)S(1)} fusion(bf16[640,256]{1,0:T(8,128)(2,1)S(1)} %select_convert_fusion, bf16[640,2176]{1,0:T(8,128)(2,1)} %bitcast.82), kind=kOutput, calls=%fused_computation.2 | convolution fusion | flops 671088640 | bytes 5046272 | tf_op jit(solution)/shard_map/dot_general | solution.py:20
  186.7 6.4 %collective-permute-start.11 = (bf16[128,128]{1,0:T(8,128)(2,1)S(1)}, bf16[128,128]{1,0:T(8,128)(2,1)S(1)}, u32[]{:S(2)}, u32[]{:S(2)}) collective-permute-start(bf16[128,128]{1,0:T(8,128)(2,1)S(1)} %slice.202), channel_id=1, source_target_pairs={{0,32},{32,0},{1,33},{33,1},{2,34},{34,2},{3,35},{35,3},{4,36},{36... | collective-permute-start | bytes 98312 | tf_op jit(solution)/shard_map/ppermute | solution.py:198
  193.3 2.6 %add_convert_fusion.2 = (bf16[256,1152]{1,0:T(8,128)(2,1)}, bf16[256,1152]{1,0:T(8,128)(2,1)}) fusion(bf16[256,1152]{1,0:T(8,128)(2,1)S(1)} %copy-done.6, bf16[512,1152]{1,0:T(8,128)(2,1)} %collective-permute-done.9, bf16[512,1152]{1,0:T(8,128)(2,1)} %collective-permute-done.8, bf16[256,1152]{1,0:T(8,128)(2,1)S(1)} %copy-done.4), kind=kLoop, calls=%fused_computation.8 | loop fusion | flops 2359296 | bytes 3538944 | tf_op jit(solution)/shard_map/convert_element_type | solution.py:204
  196.0 8.9 %collective-permute-start.12 = (bf16[64,128]{1,0:T(8,128)(2,1)S(1)}, bf16[64,128]{1,0:T(8,128)(2,1)S(1)}, u32[]{:S(2)}, u32[]{:S(2)}) collective-permute-start(bf16[64,128]{1,0:T(8,128)(2,1)S(1)} %slice.203), channel_id=1, source_target_pairs={{0,1},{1,0},{2,3},{3,2},{4,5},{5,4},{6,7},{7,6},{8,9},{9,8},{10,11... | collective-permute-start | bytes 49160 | tf_op jit(solution)/shard_map/ppermute | solution.py:199
  206.9 3.1 %collective-permute-start.15 = (bf16[256,1152]{1,0:T(8,128)(2,1)}, bf16[256,1152]{1,0:T(8,128)(2,1)}, u32[]{:S(2)}, u32[]{:S(2)}) collective-permute-start(bf16[256,1152]{1,0:T(8,128)(2,1)} %get-tuple-element.80), channel_id=1, source_target_pairs={{0,192},{64,0},{128,64},{192,128},{1,193},{65,1},{129,65},{193,129... | collective-permute-start | bytes 1769480 | tf_op jit(solution)/shard_map/ppermute | solution.py:24
  211.1 4.4 %all-to-all-start.4 = ((bf16[16,4,2048]{2,1,0:T(4,128)(2,1)}), bf16[16,4,2048]{2,1,0:T(4,128)(2,1)S(1)}, u32[]{:S(2)}, u32[]{:S(2)}) async-start(bf16[16,4,2048]{2,1,0:T(4,128)(2,1)} %reshape.152), calls=%async_computation.4 | async-start | bytes 524288 | tf_op jit(solution)/shard_map/all_to_all | solution.py:28
  215.5 1.5 collective-permute-start.13
  217.0 5.8 %all-to-all-done.4 = bf16[16,4,2048]{2,1,0:T(4,128)(2,1)S(1)} async-done(((bf16[16,4,2048]{2,1,0:T(4,128)(2,1)}), bf16[16,4,2048]{2,1,0:T(4,128)(2,1)S(1)}, u32[]{:S(2)}, u32[]{:S(2)}) %all-to-all-start.4) | async-done | bytes 262176 | tf_op jit(solution)/shard_map/all_to_all | solution.py:28
  223.6 6.9 %all-to-all-start.5 = ((f32[16,2,256]{2,1,0:T(2,128)}), f32[16,2,256]{2,1,0:T(2,128)S(1)}, u32[]{:S(2)}, u32[]{:S(2)}) async-start(f32[16,2,256]{2,1,0:T(2,128)} %bitcast.20), calls=%async_computation.5 | async-start | bytes 65536 | tf_op jit(solution)/shard_map/all_to_all | solution.py:28
  230.5 11.8 %collective-permute-done.13 = bf16[64,2048]{1,0:T(8,128)(2,1)} collective-permute-done((bf16[64,2048]{1,0:T(8,128)(2,1)}, bf16[64,2048]{1,0:T(8,128)(2,1)}, u32[]{:S(2)}, u32[]{:S(2)}) %collective-permute-start.13) | collective-permute-done | bytes 262176 | tf_op jit(solution)/shard_map/ppermute | solution.py:208
  244.4 2.9 %broadcast_select_fusion.1 = (bf16[256,1152]{1,0:T(8,128)(2,1)S(1)}, bf16[256,1152]{1,0:T(8,128)(2,1)}) fusion(pred[]{:T(512)S(6)} %eq.93, bf16[512,1152]{1,0:T(8,128)(2,1)} %collective-permute-done.9, bf16[256,1152]{1,0:T(8,128)(2,1)} %copy-done.15, bf16[512,1152]{1,0:T(8,128)(2,1)S(1)} %copy-done.2, bf16[256,1152]{1,0:T(8,128)(2,1)} %collective-permute-done.15, ...), kind=kLoop, calls=%fused_computation.28 | loop fusion | flops 4128768 | bytes 4718593 | tf_op jit(solution)/shard_map/jit(_where)/select_n | solution.py:225
  248.3 1.9 fusion.10
  (133 shorter events, 32.4 us)
Async XLA Ops:
  0.6 9.0 %copy-start.20 = (bf16[64,2048]{1,0:T(8,128)(2,1)S(1)}, bf16[64,2048]{1,0:T(8,128)(2,1)}, u32[]{:S(2)}) copy-start(bf16[64,2048]{1,0:T(8,128)(2,1)} %param.16) | copy-start | bytes 786436
  0.7 9.2 %copy-start.18 = (bf16[2,256,384]{2,1,0:T(8,128)(2,1)S(1)}, bf16[2,256,384]{2,1,0:T(8,128)(2,1)}, u32[]{:S(2)}) copy-start(bf16[2,256,384]{2,1,0:T(8,128)(2,1)} %param.21) | copy-start | bytes 1179652
  4.2 15.4 %collective-permute-start = (bf16[64,2176]{1,0:T(8,128)(2,1)S(1)}, bf16[64,2176]{1,0:T(8,128)(2,1)S(1)}, u32[]{:S(2)}, u32[]{:S(2)}) collective-permute-start(bf16[64,2176]{1,0:T(8,128)(2,1)S(1)} %concatenate.26), channel_id=1, source_target_pairs={{0,1},{1,0},{2,3},{3,2},{4,5},{5,4},{6,7},{7,6},{8,9},{9,8},{10,11... | collective-permute-start | bytes 835592 | tf_op jit(solution)/shard_map/ppermute | solution.py:132
  9.7 9.8 %collective-permute-start.1 = (bf16[64,2176]{1,0:T(8,128)(2,1)S(1)}, bf16[64,2176]{1,0:T(8,128)(2,1)S(1)}, u32[]{:S(2)}, u32[]{:S(2)}) collective-permute-start(bf16[64,2176]{1,0:T(8,128)(2,1)S(1)} %concatenate.28), channel_id=1, source_target_pairs={{0,1},{1,0},{2,3},{3,2},{4,5},{5,4},{6,7},{7,6},{8,9},{9,8},{10,11... | collective-permute-start | bytes 835592 | tf_op jit(solution)/shard_map/ppermute | solution.py:132
  11.3 8.2 %all-to-all-start.3 = ((bf16[2,256,1152]{1,2,0:T(8,128)(2,1)}), bf16[2,256,1152]{1,2,0:T(8,128)(2,1)S(1)}, u32[]{:S(2)}, u32[]{:S(2)}) async-start(bf16[2,256,1152]{1,2,0:T(8,128)(2,1)} %pad_maximum_fusion), calls=%async_computation.3 | async-start | bytes 2359296 | tf_op jit(solution)/shard_map/all_to_all | solution.py:28
  19.6 11.8 %copy-start.10 = (bf16[64,2176]{1,0:T(8,128)(2,1)}, bf16[64,2176]{1,0:T(8,128)(2,1)S(1)}, u32[]{:S(2)}) copy-start(bf16[64,2176]{1,0:T(8,128)(2,1)S(1)} %collective-permute-done) | copy-start | bytes 835588
  20.5 10.8 %collective-permute-start.2 = (bf16[128,2176]{1,0:T(8,128)(2,1)}, bf16[128,2176]{1,0:T(8,128)(2,1)}, u32[]{:S(2)}, u32[]{:S(2)}) collective-permute-start(bf16[128,2176]{1,0:T(8,128)(2,1)} %pad_maximum_fusion.9), channel_id=1, source_target_pairs={{0,32},{32,0},{1,33},{33,1},{2,34},{34,2},{3,35},{35,3},{4,36},{36... | collective-permute-start | bytes 1671176 | tf_op jit(solution)/shard_map/ppermute | solution.py:140
  22.1 11.2 %collective-permute-start.3 = (bf16[128,2176]{1,0:T(8,128)(2,1)}, bf16[128,2176]{1,0:T(8,128)(2,1)}, u32[]{:S(2)}, u32[]{:S(2)}) collective-permute-start(bf16[128,2176]{1,0:T(8,128)(2,1)} %pad_maximum_fusion.10), channel_id=1, source_target_pairs={{0,32},{32,0},{1,33},{33,1},{2,34},{34,2},{3,35},{35,3},{4,36},{36... | collective-permute-start | bytes 1671176 | tf_op jit(solution)/shard_map/ppermute | solution.py:140
  22.9 59.6 %collective-permute-start.5 = (bf16[512,1152]{1,0:T(8,128)(2,1)S(1)}, bf16[512,1152]{1,0:T(8,128)(2,1)S(1)}, u32[]{:S(2)}, u32[]{:S(2)}) collective-permute-start(bf16[512,1152]{1,0:T(8,128)(2,1)S(1)} %bitcast.75), channel_id=1, source_target_pairs={{0,192},{64,0},{128,64},{192,128},{1,193},{65,1},{129,65},{193,129... | collective-permute-start | bytes 3538952 | tf_op jit(solution)/shard_map/ppermute | solution.py:24
  28.8 53.7 %collective-permute-start.4 = (bf16[512,1152]{1,0:T(8,128)(2,1)S(1)}, bf16[512,1152]{1,0:T(8,128)(2,1)}, u32[]{:S(2)}, u32[]{:S(2)}) collective-permute-start(bf16[512,1152]{1,0:T(8,128)(2,1)S(1)} %bitcast.76), channel_id=1, source_target_pairs={{0,64},{64,128},{128,192},{192,0},{1,65},{65,129},{129,193},{193,1... | collective-permute-start | bytes 3538952 | tf_op jit(solution)/shard_map/ppermute | solution.py:24
  85.2 38.6 %collective-permute-start.6 = (bf16[256,1152]{1,0:T(8,128)(2,1)}, bf16[256,1152]{1,0:T(8,128)(2,1)S(1)}, u32[]{:S(2)}, u32[]{:S(2)}) collective-permute-start(bf16[256,1152]{1,0:T(8,128)(2,1)} %slice.101), channel_id=1, source_target_pairs={{0,64},{64,128},{128,192},{192,0},{1,65},{65,129},{129,193},{193,1... | collective-permute-start | bytes 1769480 | tf_op jit(solution)/shard_map/ppermute | solution.py:24
  86.5 37.3 %collective-permute-start.7 = (bf16[256,1152]{1,0:T(8,128)(2,1)}, bf16[256,1152]{1,0:T(8,128)(2,1)}, u32[]{:S(2)}, u32[]{:S(2)}) collective-permute-start(bf16[256,1152]{1,0:T(8,128)(2,1)} %slice.102), channel_id=1, source_target_pairs={{0,192},{64,0},{128,64},{192,128},{1,193},{65,1},{129,65},{193,129... | collective-permute-start | bytes 1769480 | tf_op jit(solution)/shard_map/ppermute | solution.py:24
  136.4 9.9 %copy-start.1 = (bf16[512,1152]{1,0:T(8,128)(2,1)}, bf16[512,1152]{1,0:T(8,128)(2,1)S(1)}, u32[]{:S(2)}) copy-start(bf16[512,1152]{1,0:T(8,128)(2,1)S(1)} %get-tuple-element.82) | copy-start | bytes 3538948
  136.4 9.8 %copy-start.3 = (bf16[256,1152]{1,0:T(8,128)(2,1)}, bf16[256,1152]{1,0:T(8,128)(2,1)S(1)}, u32[]{:S(2)}) copy-start(bf16[256,1152]{1,0:T(8,128)(2,1)S(1)} %get-tuple-element.73) | copy-start | bytes 1769476
  136.4 9.8 %copy-start.5 = (bf16[256,1152]{1,0:T(8,128)(2,1)}, bf16[256,1152]{1,0:T(8,128)(2,1)S(1)}, u32[]{:S(2)}) copy-start(bf16[256,1152]{1,0:T(8,128)(2,1)S(1)} %get-tuple-element.75) | copy-start | bytes 1769476
  136.4 46.2 %collective-permute-start.8 = (bf16[512,1152]{1,0:T(8,128)(2,1)}, bf16[512,1152]{1,0:T(8,128)(2,1)}, u32[]{:S(2)}, u32[]{:S(2)}) collective-permute-start(bf16[512,1152]{1,0:T(8,128)(2,1)} %get-tuple-element.70), channel_id=1, source_target_pairs={{0,64},{64,128},{128,192},{192,0},{1,65},{65,129},{129,193},{193,1... | collective-permute-start | bytes 3538952 | tf_op jit(solution)/shard_map/ppermute | solution.py:24
  137.4 45.2 %collective-permute-start.9 = (bf16[512,1152]{1,0:T(8,128)(2,1)}, bf16[512,1152]{1,0:T(8,128)(2,1)}, u32[]{:S(2)}, u32[]{:S(2)}) collective-permute-start(bf16[512,1152]{1,0:T(8,128)(2,1)} %get-tuple-element.71), channel_id=1, source_target_pairs={{0,192},{64,0},{128,64},{192,128},{1,193},{65,1},{129,65},{193,129... | collective-permute-start | bytes 3538952 | tf_op jit(solution)/shard_map/ppermute | solution.py:24
  183.9 9.4 %copy-start.6 = (bf16[256,1152]{1,0:T(8,128)(2,1)S(1)}, bf16[256,1152]{1,0:T(8,128)(2,1)}, u32[]{:S(2)}) copy-start(bf16[256,1152]{1,0:T(8,128)(2,1)} %copy-done.5) | copy-start | bytes 1769476
  186.7 9.2 %collective-permute-start.11 = (bf16[128,128]{1,0:T(8,128)(2,1)S(1)}, bf16[128,128]{1,0:T(8,128)(2,1)S(1)}, u32[]{:S(2)}, u32[]{:S(2)}) collective-permute-start(bf16[128,128]{1,0:T(8,128)(2,1)S(1)} %slice.202), channel_id=1, source_target_pairs={{0,32},{32,0},{1,33},{33,1},{2,34},{34,2},{3,35},{35,3},{4,36},{36... | collective-permute-start | bytes 98312 | tf_op jit(solution)/shard_map/ppermute | solution.py:198
  193.2 11.6 %collective-permute-start.10 = (bf16[128,2048]{1,0:T(8,128)(2,1)S(1)}, bf16[128,2048]{1,0:T(8,128)(2,1)S(1)}, u32[]{:S(2)}, u32[]{:S(2)}) collective-permute-start(bf16[128,2048]{1,0:T(8,128)(2,1)S(1)} %slice.200), channel_id=1, source_target_pairs={{0,32},{32,0},{1,33},{33,1},{2,34},{34,2},{3,35},{35,3},{4,36},{36... | collective-permute-start | bytes 1572872 | tf_op jit(solution)/shard_map/ppermute | solution.py:201
  195.9 10.1 %copy-start.22 = (f32[64,64]{0,1:T(8,128)S(1)}, f32[64,64]{0,1:T(8,128)}, u32[]{:S(2)}) copy-start(f32[64,64]{0,1:T(8,128)} %copy-done.21) | copy-start | bytes 49156
  195.9 10.1 %copy-start.24 = (pred[64,64]{0,1:T(32,128)(4,1)S(1)}, pred[64,64]{0,1:T(32,128)(4,1)}, u32[]{:S(2)}) copy-start(pred[64,64]{0,1:T(32,128)(4,1)} %copy-done.23) | copy-start | bytes 12292
  196.0 10.1 %copy-start.27 = (f32[64]{0:T(128)S(1)}, f32[64]{0:T(128)}, u32[]{:S(2)}) copy-start(f32[64]{0:T(128)} %copy-done.26) | copy-start | bytes 772
  196.0 14.1 %copy-start.14 = (bf16[64,2048]{1,0:T(8,128)(2,1)S(1)}, bf16[64,2048]{1,0:T(8,128)(2,1)}, u32[]{:S(2)}) copy-start(bf16[64,2048]{1,0:T(8,128)(2,1)} %param.15) | copy-start | bytes 786436
  196.0 10.0 %collective-permute-start.12 = (bf16[64,128]{1,0:T(8,128)(2,1)S(1)}, bf16[64,128]{1,0:T(8,128)(2,1)S(1)}, u32[]{:S(2)}, u32[]{:S(2)}) collective-permute-start(bf16[64,128]{1,0:T(8,128)(2,1)S(1)} %slice.203), channel_id=1, source_target_pairs={{0,1},{1,0},{2,3},{3,2},{4,5},{5,4},{6,7},{7,6},{8,9},{9,8},{10,11... | collective-permute-start | bytes 49160 | tf_op jit(solution)/shard_map/ppermute | solution.py:199
  205.7 38.7 %copy-start.2 = (bf16[512,1152]{1,0:T(8,128)(2,1)S(1)}, bf16[512,1152]{1,0:T(8,128)(2,1)}, u32[]{:S(2)}) copy-start(bf16[512,1152]{1,0:T(8,128)(2,1)} %copy-done.1) | copy-start | bytes 3538948
  206.2 37.3 %collective-permute-start.14 = (bf16[256,1152]{1,0:T(8,128)(2,1)}, bf16[256,1152]{1,0:T(8,128)(2,1)S(1)}, u32[]{:S(2)}, u32[]{:S(2)}) collective-permute-start(bf16[256,1152]{1,0:T(8,128)(2,1)} %get-tuple-element.79), channel_id=1, source_target_pairs={{0,64},{64,128},{128,192},{192,0},{1,65},{65,129},{129,193},{193,1... | collective-permute-start | bytes 1769480 | tf_op jit(solution)/shard_map/ppermute | solution.py:24
  206.9 36.6 %collective-permute-start.15 = (bf16[256,1152]{1,0:T(8,128)(2,1)}, bf16[256,1152]{1,0:T(8,128)(2,1)}, u32[]{:S(2)}, u32[]{:S(2)}) collective-permute-start(bf16[256,1152]{1,0:T(8,128)(2,1)} %get-tuple-element.80), channel_id=1, source_target_pairs={{0,192},{64,0},{128,64},{192,128},{1,193},{65,1},{129,65},{193,129... | collective-permute-start | bytes 1769480 | tf_op jit(solution)/shard_map/ppermute | solution.py:24
  211.1 11.7 %all-to-all-start.4 = ((bf16[16,4,2048]{2,1,0:T(4,128)(2,1)}), bf16[16,4,2048]{2,1,0:T(4,128)(2,1)S(1)}, u32[]{:S(2)}, u32[]{:S(2)}) async-start(bf16[16,4,2048]{2,1,0:T(4,128)(2,1)} %reshape.152), calls=%async_computation.4 | async-start | bytes 524288 | tf_op jit(solution)/shard_map/all_to_all | solution.py:28
  215.5 26.8 %collective-permute-start.13 = (bf16[64,2048]{1,0:T(8,128)(2,1)}, bf16[64,2048]{1,0:T(8,128)(2,1)}, u32[]{:S(2)}, u32[]{:S(2)}) collective-permute-start(bf16[64,2048]{1,0:T(8,128)(2,1)} %slice.201), channel_id=1, source_target_pairs={{0,1},{1,0},{2,3},{3,2},{4,5},{5,4},{6,7},{7,6},{8,9},{9,8},{10,11... | collective-permute-start | bytes 786440 | tf_op jit(solution)/shard_map/ppermute | solution.py:208
  223.6 19.9 %all-to-all-start.5 = ((f32[16,2,256]{2,1,0:T(2,128)}), f32[16,2,256]{2,1,0:T(2,128)S(1)}, u32[]{:S(2)}, u32[]{:S(2)}) async-start(f32[16,2,256]{2,1,0:T(2,128)} %bitcast.20), calls=%async_computation.5 | async-start | bytes 65536 | tf_op jit(solution)/shard_map/all_to_all | solution.py:28
  247.3 2.9 %collective-permute-start.16 = (bf16[256,1152]{1,0:T(8,128)(2,1)}, bf16[256,1152]{1,0:T(8,128)(2,1)S(1)}, u32[]{:S(2)}, u32[]{:S(2)}) collective-permute-start(bf16[256,1152]{1,0:T(8,128)(2,1)} %get-tuple-element.107), channel_id=1, source_target_pairs={{0,32},{32,0},{1,33},{33,1},{2,34},{34,2},{3,35},{35,3},{4,36},{36... | collective-permute-start | bytes 1769480 | tf_op jit(solution)/shard_map/ppermute | solution.py:224
  (16 other events, 42.0 us)

commit v6 on v5

--- a/solution.py
+++ b/solution.py
@@ -42,10 +42,10 @@
     pre_out, spread, *outs = refs[:7]
     hidden, pre_grad, *grads, sems = refs[7:]
     hid = own.shape[1] // 3
-    rows = x.shape[0] // 2
+    rows = x.shape[0]
     pieces = ((own, 0), (after, 2), (far_lo, 4), (far_hi, 5), (prev, 6))
 
-    @pl.loop(0, 2)
+    @pl.loop(0, 1)
     def _(i):
         tile = pl.ds(pl.multiple_of(i * rows, rows), rows)
         pre = jnp.zeros((rows, 2 * hid), F32)
@@ -83,9 +83,9 @@
 
 def back_kernel(starts, spread, pre_grad, own, after, far_lo, far_hi, prev, back):
     hid = own.shape[1] // 3
-    rows = pre_grad.shape[0] // 2
-
-    @pl.loop(0, 2)
+    rows = pre_grad.shape[0]
+
+    @pl.loop(0, 1)
     def _(i):
         tile = pl.ds(pl.multiple_of(i * rows, rows), rows)
         for w, u in ((own, 0), (after, 2), (far_lo, 4), (far_hi, 5), (prev, 6)):

time: 256 us -> 257 us (level)
  no operation moved by 1% of the time
where the time goes in v6:
time: 257 us; the launch traced here: 256 us
  blocking collectives  107 us (42%)
  starting transfers between devices  56 us (22%)
  waiting for transfers between devices  20.9 us (8%)
  Pallas kernels  18.9 us (7%)
  local copies, waits for them, and re-layouts  17.9 us (7%)
  other arithmetic  16.7 us (6%)
  matrix products  16.2 us (6%)
    all_to_all x3, blocking collectives, a2a(): return lax.all_to_all(a, axes, split_axis=0, concat_axis=0, tiled=True)  107 us
    pallas_call x2, Pallas kernels, call(): pl.pallas_call(kernel, out_shape=outs, in_specs=[smem if a.dtype == jnp.i...  18.9 us
    all_to_all x3, starting transfers between devices, a2a(): return lax.all_to_all(a, axes, split_axis=0, concat_axis=0, tiled=True)  17.7 us
    ppermute x8, starting transfers between devices, both_ways(): return (lax.ppermute(up, 'zh', PLUS), lax.ppermute(down, 'zh', MINUS))  17.6 us
    dot_general x9, matrix products, mm(): return lax.dot_general(a, b, (dims, ((), ())), preferred_element_type=F32)  16.2 us
    ppermute x1, waiting for transfers between devices, per_device(): other = lax.ppermute(for_other, 'zl', SWAP)  11.6 us
    ppermute x1, starting transfers between devices, per_device(): other_taken = lax.ppermute(taken[tok:].astype(BF16), 'zl', SWAP)  8.99 us
    all_to_all x3, waiting for transfers between devices, a2a(): return lax.all_to_all(a, axes, split_axis=0, concat_axis=0, tiled=True)  8.98 us
  transfers between devices with their start and end apart: 20, of which 5 were waited for; matrix products, arithmetic and copies ran while one was open for 10% of the time, Pallas kernels for 2%

profile of v6, /device:TPU:1, one launch (start us, length us, event | category | flops | bytes accessed | tf_op | source)
XLA Modules:
  0.0 255.6 jit_solution(11028831383286875096)
XLA Ops:
  4.2 2.6 collective-permute-start
  11.3 6.4 %all-to-all-start.3 = ((bf16[2,256,1152]{1,2,0:T(8,128)(2,1)}), bf16[2,256,1152]{1,2,0:T(8,128)(2,1)S(1)}, u32[]{:S(2)}, u32[]{:S(2)}) async-start(bf16[2,256,1152]{1,2,0:T(8,128)(2,1)} %pad_maximum_fusion), calls=%async_computation.3 | async-start | bytes 2359296 | tf_op jit(solution)/shard_map/all_to_all | solution.py:28
  17.7 1.8 all-to-all-done.3
  22.9 5.9 %collective-permute-start.5 = (bf16[512,1152]{1,0:T(8,128)(2,1)S(1)}, bf16[512,1152]{1,0:T(8,128)(2,1)S(1)}, u32[]{:S(2)}, u32[]{:S(2)}) collective-permute-start(bf16[512,1152]{1,0:T(8,128)(2,1)S(1)} %bitcast.75), channel_id=1, source_target_pairs={{0,192},{64,0},{128,64},{192,128},{1,193},{65,1},{129,65},{193,129... | collective-permute-start | bytes 3538952 | tf_op jit(solution)/shard_map/ppermute | solution.py:24
  34.4 3.4 %convolution_convert_fusion = bf16[640,2048]{1,0:T(8,128)(2,1)} fusion(bf16[640,256]{1,0:T(8,128)(2,1)S(1)} %fusion.7, bf16[128,2176]{1,0:T(8,128)(2,1)} %collective-permute-done.3, bf16[64,2176]{1,0:T(8,128)(2,1)S(1)} %copy-done.13, bf16[64,2176]{1,0:T(8,128)(2,1)S(1)} %concatenate.28), kind=kOutput, calls=%fused_computation | convolution fusion | flops 675545088 | bytes 4063232 | tf_op jit(solution)/shard_map/dot_general | solution.py:20
  37.9 3.4 %convolution_convert_fusion.1 = bf16[640,2048]{1,0:T(8,128)(2,1)} fusion(bf16[640,256]{1,0:T(8,128)(2,1)S(1)} %select_convert_fusion, bf16[128,2176]{1,0:T(8,128)(2,1)} %collective-permute-done.2, bf16[64,2176]{1,0:T(8,128)(2,1)S(1)} %copy-done.11, bf16[64,2176]{1,0:T(8,128)(2,1)S(1)} %concatenate.26), kind=kOutput, calls=%fused_computation.1 | convolution fusion | flops 675545088 | bytes 4063232 | tf_op jit(solution)/shard_map/dot_general | solution.py:20
  41.3 41.1 %conditional.3 = (bf16[16,40,2048]{2,1,0:T(8,128)(2,1)}) conditional(s32[]{:T(128)} %bitcast.8, bf16[16,40,2048]{2,1,0:T(8,128)(2,1)} %bitcast.86, bf16[16,40,2048]{2,1,0:T(8,128)(2,1)} %bitcast.87), branch_computations={%region_3.4_spmd, %region_4.5_spmd} | conditional | bytes 15728676 | solution.py:32
  41.3 1.7 copy-done.9
  43.0 39.4 %all_to_all.27 = bf16[16,40,2048]{2,1,0:T(8,128)(2,1)} all-to-all(bf16[16,40,2048]{2,1,0:T(8,128)(2,1)S(1)} %copy-done.9), channel_id=1, replica_groups=mesh['zh'=4,'core'=2,'x'=4,'y'=4,'zl'=2] {'x','y'}, dimensions={0} | all-to-all | bytes 5242880 | tf_op jit(solution)/shard_map/cond/branch_1_fun/all_to_all | solution.py:28
  82.4 1.9 slice.101
  86.5 2.3 collective-permute-start.7
  88.9 34.9 %conditional.4 = (bf16[16,40,2048]{2,1,0:T(8,128)(2,1)}) conditional(s32[]{:T(128)} %bitcast.8, bf16[16,40,2048]{2,1,0:T(8,128)(2,1)} %bitcast.83, bf16[16,40,2048]{2,1,0:T(8,128)(2,1)} %bitcast.84), branch_computations={%region_5.6_spmd, %region_6.7_spmd} | conditional | bytes 15728676 | solution.py:32
  88.9 1.7 copy-done.8
  90.6 33.2 %all_to_all.28 = bf16[16,40,2048]{2,1,0:T(8,128)(2,1)} all-to-all(bf16[16,40,2048]{2,1,0:T(8,128)(2,1)S(1)} %copy-done.8), channel_id=1, replica_groups=mesh['zh'=4,'core'=2,'x'=4,'y'=4,'zl'=2] {'x','y'}, dimensions={0} | all-to-all | bytes 5242880 | tf_op jit(solution)/shard_map/cond/branch_1_fun/all_to_all | solution.py:28
  123.8 13.6 %shard_map.128 = (bf16[640,768]{1,0:T(8,128)(2,1)S(1)}, f32[640,128]{1,0:T(8,128)S(1)}, bf16[512,1152]{1,0:T(8,128)(2,1)S(1)}, bf16[256,1152]{1,0:T(8,128)(2,1)S...) custom-call(s32[9]{0:T(128)S(1)} %pad_add_fusion.starts, ...), custom_call_target="tpu_custom_call" | custom-call | tf_op jit(solution)/shard_map/pallas_call | solution.py:100
  138.5 3.4 %collective-permute-start.9 = (bf16[512,1152]{1,0:T(8,128)(2,1)}, bf16[512,1152]{1,0:T(8,128)(2,1)}, u32[]{:S(2)}, u32[]{:S(2)}) collective-permute-start(bf16[512,1152]{1,0:T(8,128)(2,1)} %get-tuple-element.71), channel_id=1, source_target_pairs={{0,192},{64,0},{128,64},{192,128},{1,193},{65,1},{129,65},{193,129... | collective-permute-start | bytes 3538952 | tf_op jit(solution)/shard_map/ppermute | solution.py:24
  141.9 5.3 %shard_map.129 = bf16[640,2176]{1,0:T(8,128)(2,1)} custom-call(s32[9]{0:T(128)S(1)} %pad_add_fusion.starts, f32[640,128]{1,0:T(8,128)S(1)} %get-tuple-element.68.spread, bf16[640,768]{1,0:T(8,128)(2,1)S(1)} %get-tuple-element.69.pre_grad, bf16[512,1152]{1,0:T(8,128)(2,1)S(1)} %bitcast.78, bf16[512,1152]{1,0:T(8,128)(2,1)S(1)} %collective-permute-done.5.after, ...), custom_call_target="tpu_custom_call" | custom-call | tf_op jit(solution)/shard_map/pallas_call | solution.py:100
  147.1 36.4 %conditional.5 = (bf16[16,40,2176]{2,1,0:T(8,128)(2,1)}) conditional(s32[]{:T(128)} %bitcast.8, bf16[16,40,2176]{2,1,0:T(8,128)(2,1)} %bitcast.79, bf16[16,40,2176]{2,1,0:T(8,128)(2,1)} %bitcast.80), branch_computations={%region_7.8_spmd, %region_8.9_spmd} | conditional | bytes 16711716 | solution.py:32
  147.2 1.8 copy-done.7
  149.0 34.6 %all_to_all.29 = bf16[16,40,2176]{2,1,0:T(8,128)(2,1)} all-to-all(bf16[16,40,2176]{2,1,0:T(8,128)(2,1)S(1)} %copy-done.7), channel_id=1, replica_groups=mesh['zh'=4,'core'=2,'x'=4,'y'=4,'zl'=2] {'x','y'}, dimensions={0} | all-to-all | bytes 5570560 | tf_op jit(solution)/shard_map/cond/branch_1_fun/all_to_all | solution.py:28
  184.8 2.8 %fusion = f32[256,2048]{1,0:T(8,128)S(1)} fusion(bf16[640,256]{1,0:T(8,128)(2,1)S(1)} %select_convert_fusion, bf16[640,2176]{1,0:T(8,128)(2,1)} %bitcast.82), kind=kOutput, calls=%fused_computation.2 | convolution fusion | flops 671088640 | bytes 5046272 | tf_op jit(solution)/shard_map/dot_general | solution.py:20
  187.7 6.4 %collective-permute-start.11 = (bf16[128,128]{1,0:T(8,128)(2,1)S(1)}, bf16[128,128]{1,0:T(8,128)(2,1)S(1)}, u32[]{:S(2)}, u32[]{:S(2)}) collective-permute-start(bf16[128,128]{1,0:T(8,128)(2,1)S(1)} %slice.202), channel_id=1, source_target_pairs={{0,32},{32,0},{1,33},{33,1},{2,34},{34,2},{3,35},{35,3},{4,36},{36... | collective-permute-start | bytes 98312 | tf_op jit(solution)/shard_map/ppermute | solution.py:198
  194.2 2.6 %add_convert_fusion.2 = (bf16[256,1152]{1,0:T(8,128)(2,1)}, bf16[256,1152]{1,0:T(8,128)(2,1)}) fusion(bf16[256,1152]{1,0:T(8,128)(2,1)S(1)} %copy-done.6, bf16[512,1152]{1,0:T(8,128)(2,1)} %collective-permute-done.9, bf16[512,1152]{1,0:T(8,128)(2,1)} %collective-permute-done.8, bf16[256,1152]{1,0:T(8,128)(2,1)S(1)} %copy-done.4), kind=kLoop, calls=%fused_computation.8 | loop fusion | flops 2359296 | bytes 3538944 | tf_op jit(solution)/shard_map/convert_element_type | solution.py:204
  196.9 9.0 %collective-permute-start.12 = (bf16[64,128]{1,0:T(8,128)(2,1)S(1)}, bf16[64,128]{1,0:T(8,128)(2,1)S(1)}, u32[]{:S(2)}, u32[]{:S(2)}) collective-permute-start(bf16[64,128]{1,0:T(8,128)(2,1)S(1)} %slice.203), channel_id=1, source_target_pairs={{0,1},{1,0},{2,3},{3,2},{4,5},{5,4},{6,7},{7,6},{8,9},{9,8},{10,11... | collective-permute-start | bytes 49160 | tf_op jit(solution)/shard_map/ppermute | solution.py:199
  207.8 3.1 %collective-permute-start.15 = (bf16[256,1152]{1,0:T(8,128)(2,1)}, bf16[256,1152]{1,0:T(8,128)(2,1)}, u32[]{:S(2)}, u32[]{:S(2)}) collective-permute-start(bf16[256,1152]{1,0:T(8,128)(2,1)} %get-tuple-element.80), channel_id=1, source_target_pairs={{0,192},{64,0},{128,64},{192,128},{1,193},{65,1},{129,65},{193,129... | collective-permute-start | bytes 1769480 | tf_op jit(solution)/shard_map/ppermute | solution.py:24
  212.0 4.3 %all-to-all-start.4 = ((bf16[16,4,2048]{2,1,0:T(4,128)(2,1)}), bf16[16,4,2048]{2,1,0:T(4,128)(2,1)S(1)}, u32[]{:S(2)}, u32[]{:S(2)}) async-start(bf16[16,4,2048]{2,1,0:T(4,128)(2,1)} %reshape.152), calls=%async_computation.4 | async-start | bytes 524288 | tf_op jit(solution)/shard_map/all_to_all | solution.py:28
  216.3 1.6 collective-permute-start.13
  217.9 5.8 %all-to-all-done.4 = bf16[16,4,2048]{2,1,0:T(4,128)(2,1)S(1)} async-done(((bf16[16,4,2048]{2,1,0:T(4,128)(2,1)}), bf16[16,4,2048]{2,1,0:T(4,128)(2,1)S(1)}, u32[]{:S(2)}, u32[]{:S(2)}) %all-to-all-start.4) | async-done | bytes 262176 | tf_op jit(solution)/shard_map/all_to_all | solution.py:28
  224.4 7.0 %all-to-all-start.5 = ((f32[16,2,256]{2,1,0:T(2,128)}), f32[16,2,256]{2,1,0:T(2,128)S(1)}, u32[]{:S(2)}, u32[]{:S(2)}) async-start(f32[16,2,256]{2,1,0:T(2,128)} %bitcast.20), calls=%async_computation.5 | async-start | bytes 65536 | tf_op jit(solution)/shard_map/all_to_all | solution.py:28
  231.4 11.6 %collective-permute-done.13 = bf16[64,2048]{1,0:T(8,128)(2,1)} collective-permute-done((bf16[64,2048]{1,0:T(8,128)(2,1)}, bf16[64,2048]{1,0:T(8,128)(2,1)}, u32[]{:S(2)}, u32[]{:S(2)}) %collective-permute-start.13) | collective-permute-done | bytes 262176 | tf_op jit(solution)/shard_map/ppermute | solution.py:208
  245.2 2.9 %broadcast_select_fusion.1 = (bf16[256,1152]{1,0:T(8,128)(2,1)S(1)}, bf16[256,1152]{1,0:T(8,128)(2,1)}) fusion(pred[]{:T(512)S(6)} %eq.93, bf16[512,1152]{1,0:T(8,128)(2,1)} %collective-permute-done.9, bf16[256,1152]{1,0:T(8,128)(2,1)} %copy-done.15, bf16[512,1152]{1,0:T(8,128)(2,1)S(1)} %copy-done.2, bf16[256,1152]{1,0:T(8,128)(2,1)} %collective-permute-done.15, ...), kind=kLoop, calls=%fused_computation.28 | loop fusion | flops 4128768 | bytes 4718593 | tf_op jit(solution)/shard_map/jit(_where)/select_n | solution.py:225
  249.1 1.9 fusion.10
  (133 shorter events, 32.4 us)
Async XLA Ops:
  0.6 9.0 %copy-start.20 = (bf16[64,2048]{1,0:T(8,128)(2,1)S(1)}, bf16[64,2048]{1,0:T(8,128)(2,1)}, u32[]{:S(2)}) copy-start(bf16[64,2048]{1,0:T(8,128)(2,1)} %param.16) | copy-start | bytes 786436
  0.7 9.2 %copy-start.18 = (bf16[2,256,384]{2,1,0:T(8,128)(2,1)S(1)}, bf16[2,256,384]{2,1,0:T(8,128)(2,1)}, u32[]{:S(2)}) copy-start(bf16[2,256,384]{2,1,0:T(8,128)(2,1)} %param.21) | copy-start | bytes 1179652
  4.2 15.4 %collective-permute-start = (bf16[64,2176]{1,0:T(8,128)(2,1)S(1)}, bf16[64,2176]{1,0:T(8,128)(2,1)S(1)}, u32[]{:S(2)}, u32[]{:S(2)}) collective-permute-start(bf16[64,2176]{1,0:T(8,128)(2,1)S(1)} %concatenate.26), channel_id=1, source_target_pairs={{0,1},{1,0},{2,3},{3,2},{4,5},{5,4},{6,7},{7,6},{8,9},{9,8},{10,11... | collective-permute-start | bytes 835592 | tf_op jit(solution)/shard_map/ppermute | solution.py:132
  9.7 9.8 %collective-permute-start.1 = (bf16[64,2176]{1,0:T(8,128)(2,1)S(1)}, bf16[64,2176]{1,0:T(8,128)(2,1)S(1)}, u32[]{:S(2)}, u32[]{:S(2)}) collective-permute-start(bf16[64,2176]{1,0:T(8,128)(2,1)S(1)} %concatenate.28), channel_id=1, source_target_pairs={{0,1},{1,0},{2,3},{3,2},{4,5},{5,4},{6,7},{7,6},{8,9},{9,8},{10,11... | collective-permute-start | bytes 835592 | tf_op jit(solution)/shard_map/ppermute | solution.py:132
  11.3 8.2 %all-to-all-start.3 = ((bf16[2,256,1152]{1,2,0:T(8,128)(2,1)}), bf16[2,256,1152]{1,2,0:T(8,128)(2,1)S(1)}, u32[]{:S(2)}, u32[]{:S(2)}) async-start(bf16[2,256,1152]{1,2,0:T(8,128)(2,1)} %pad_maximum_fusion), calls=%async_computation.3 | async-start | bytes 2359296 | tf_op jit(solution)/shard_map/all_to_all | solution.py:28
  19.6 11.8 %copy-start.10 = (bf16[64,2176]{1,0:T(8,128)(2,1)}, bf16[64,2176]{1,0:T(8,128)(2,1)S(1)}, u32[]{:S(2)}) copy-start(bf16[64,2176]{1,0:T(8,128)(2,1)S(1)} %collective-permute-done) | copy-start | bytes 835588
  20.5 10.8 %collective-permute-start.2 = (bf16[128,2176]{1,0:T(8,128)(2,1)}, bf16[128,2176]{1,0:T(8,128)(2,1)}, u32[]{:S(2)}, u32[]{:S(2)}) collective-permute-start(bf16[128,2176]{1,0:T(8,128)(2,1)} %pad_maximum_fusion.9), channel_id=1, source_target_pairs={{0,32},{32,0},{1,33},{33,1},{2,34},{34,2},{3,35},{35,3},{4,36},{36... | collective-permute-start | bytes 1671176 | tf_op jit(solution)/shard_map/ppermute | solution.py:140
  22.1 11.2 %collective-permute-start.3 = (bf16[128,2176]{1,0:T(8,128)(2,1)}, bf16[128,2176]{1,0:T(8,128)(2,1)}, u32[]{:S(2)}, u32[]{:S(2)}) collective-permute-start(bf16[128,2176]{1,0:T(8,128)(2,1)} %pad_maximum_fusion.10), channel_id=1, source_target_pairs={{0,32},{32,0},{1,33},{33,1},{2,34},{34,2},{3,35},{35,3},{4,36},{36... | collective-permute-start | bytes 1671176 | tf_op jit(solution)/shard_map/ppermute | solution.py:140
  22.9 59.6 %collective-permute-start.5 = (bf16[512,1152]{1,0:T(8,128)(2,1)S(1)}, bf16[512,1152]{1,0:T(8,128)(2,1)S(1)}, u32[]{:S(2)}, u32[]{:S(2)}) collective-permute-start(bf16[512,1152]{1,0:T(8,128)(2,1)S(1)} %bitcast.75), channel_id=1, source_target_pairs={{0,192},{64,0},{128,64},{192,128},{1,193},{65,1},{129,65},{193,129... | collective-permute-start | bytes 3538952 | tf_op jit(solution)/shard_map/ppermute | solution.py:24
  28.8 53.7 %collective-permute-start.4 = (bf16[512,1152]{1,0:T(8,128)(2,1)S(1)}, bf16[512,1152]{1,0:T(8,128)(2,1)}, u32[]{:S(2)}, u32[]{:S(2)}) collective-permute-start(bf16[512,1152]{1,0:T(8,128)(2,1)S(1)} %bitcast.76), channel_id=1, source_target_pairs={{0,64},{64,128},{128,192},{192,0},{1,65},{65,129},{129,193},{193,1... | collective-permute-start | bytes 3538952 | tf_op jit(solution)/shard_map/ppermute | solution.py:24
  85.2 38.6 %collective-permute-start.6 = (bf16[256,1152]{1,0:T(8,128)(2,1)}, bf16[256,1152]{1,0:T(8,128)(2,1)S(1)}, u32[]{:S(2)}, u32[]{:S(2)}) collective-permute-start(bf16[256,1152]{1,0:T(8,128)(2,1)} %slice.101), channel_id=1, source_target_pairs={{0,64},{64,128},{128,192},{192,0},{1,65},{65,129},{129,193},{193,1... | collective-permute-start | bytes 1769480 | tf_op jit(solution)/shard_map/ppermute | solution.py:24
  86.5 37.3 %collective-permute-start.7 = (bf16[256,1152]{1,0:T(8,128)(2,1)}, bf16[256,1152]{1,0:T(8,128)(2,1)}, u32[]{:S(2)}, u32[]{:S(2)}) collective-permute-start(bf16[256,1152]{1,0:T(8,128)(2,1)} %slice.102), channel_id=1, source_target_pairs={{0,192},{64,0},{128,64},{192,128},{1,193},{65,1},{129,65},{193,129... | collective-permute-start | bytes 1769480 | tf_op jit(solution)/shard_map/ppermute | solution.py:24
  137.4 9.7 %copy-start.1 = (bf16[512,1152]{1,0:T(8,128)(2,1)}, bf16[512,1152]{1,0:T(8,128)(2,1)S(1)}, u32[]{:S(2)}) copy-start(bf16[512,1152]{1,0:T(8,128)(2,1)S(1)} %get-tuple-element.82) | copy-start | bytes 3538948
  137.4 9.7 %copy-start.3 = (bf16[256,1152]{1,0:T(8,128)(2,1)}, bf16[256,1152]{1,0:T(8,128)(2,1)S(1)}, u32[]{:S(2)}) copy-start(bf16[256,1152]{1,0:T(8,128)(2,1)S(1)} %get-tuple-element.73) | copy-start | bytes 1769476
  137.4 9.7 %copy-start.5 = (bf16[256,1152]{1,0:T(8,128)(2,1)}, bf16[256,1152]{1,0:T(8,128)(2,1)S(1)}, u32[]{:S(2)}) copy-start(bf16[256,1152]{1,0:T(8,128)(2,1)S(1)} %get-tuple-element.75) | copy-start | bytes 1769476
  137.5 46.1 %collective-permute-start.8 = (bf16[512,1152]{1,0:T(8,128)(2,1)}, bf16[512,1152]{1,0:T(8,128)(2,1)}, u32[]{:S(2)}, u32[]{:S(2)}) collective-permute-start(bf16[512,1152]{1,0:T(8,128)(2,1)} %get-tuple-element.70), channel_id=1, source_target_pairs={{0,64},{64,128},{128,192},{192,0},{1,65},{65,129},{129,193},{193,1... | collective-permute-start | bytes 3538952 | tf_op jit(solution)/shard_map/ppermute | solution.py:24
  138.5 45.1 %collective-permute-start.9 = (bf16[512,1152]{1,0:T(8,128)(2,1)}, bf16[512,1152]{1,0:T(8,128)(2,1)}, u32[]{:S(2)}, u32[]{:S(2)}) collective-permute-start(bf16[512,1152]{1,0:T(8,128)(2,1)} %get-tuple-element.71), channel_id=1, source_target_pairs={{0,192},{64,0},{128,64},{192,128},{1,193},{65,1},{129,65},{193,129... | collective-permute-start | bytes 3538952 | tf_op jit(solution)/shard_map/ppermute | solution.py:24
  184.8 9.4 %copy-start.6 = (bf16[256,1152]{1,0:T(8,128)(2,1)S(1)}, bf16[256,1152]{1,0:T(8,128)(2,1)}, u32[]{:S(2)}) copy-start(bf16[256,1152]{1,0:T(8,128)(2,1)} %copy-done.5) | copy-start | bytes 1769476
  187.7 9.1 %collective-permute-start.11 = (bf16[128,128]{1,0:T(8,128)(2,1)S(1)}, bf16[128,128]{1,0:T(8,128)(2,1)S(1)}, u32[]{:S(2)}, u32[]{:S(2)}) collective-permute-start(bf16[128,128]{1,0:T(8,128)(2,1)S(1)} %slice.202), channel_id=1, source_target_pairs={{0,32},{32,0},{1,33},{33,1},{2,34},{34,2},{3,35},{35,3},{4,36},{36... | collective-permute-start | bytes 98312 | tf_op jit(solution)/shard_map/ppermute | solution.py:198
  194.1 11.8 %collective-permute-start.10 = (bf16[128,2048]{1,0:T(8,128)(2,1)S(1)}, bf16[128,2048]{1,0:T(8,128)(2,1)S(1)}, u32[]{:S(2)}, u32[]{:S(2)}) collective-permute-start(bf16[128,2048]{1,0:T(8,128)(2,1)S(1)} %slice.200), channel_id=1, source_target_pairs={{0,32},{32,0},{1,33},{33,1},{2,34},{34,2},{3,35},{35,3},{4,36},{36... | collective-permute-start | bytes 1572872 | tf_op jit(solution)/shard_map/ppermute | solution.py:201
  196.8 10.3 %copy-start.22 = (f32[64,64]{0,1:T(8,128)S(1)}, f32[64,64]{0,1:T(8,128)}, u32[]{:S(2)}) copy-start(f32[64,64]{0,1:T(8,128)} %copy-done.21) | copy-start | bytes 49156
  196.8 10.3 %copy-start.24 = (pred[64,64]{0,1:T(32,128)(4,1)S(1)}, pred[64,64]{0,1:T(32,128)(4,1)}, u32[]{:S(2)}) copy-start(pred[64,64]{0,1:T(32,128)(4,1)} %copy-done.23) | copy-start | bytes 12292
  196.9 10.3 %copy-start.27 = (f32[64]{0:T(128)S(1)}, f32[64]{0:T(128)}, u32[]{:S(2)}) copy-start(f32[64]{0:T(128)} %copy-done.26) | copy-start | bytes 772
  196.9 14.0 %copy-start.14 = (bf16[64,2048]{1,0:T(8,128)(2,1)S(1)}, bf16[64,2048]{1,0:T(8,128)(2,1)}, u32[]{:S(2)}) copy-start(bf16[64,2048]{1,0:T(8,128)(2,1)} %param.15) | copy-start | bytes 786436
  196.9 10.1 %collective-permute-start.12 = (bf16[64,128]{1,0:T(8,128)(2,1)S(1)}, bf16[64,128]{1,0:T(8,128)(2,1)S(1)}, u32[]{:S(2)}, u32[]{:S(2)}) collective-permute-start(bf16[64,128]{1,0:T(8,128)(2,1)S(1)} %slice.203), channel_id=1, source_target_pairs={{0,1},{1,0},{2,3},{3,2},{4,5},{5,4},{6,7},{7,6},{8,9},{9,8},{10,11... | collective-permute-start | bytes 49160 | tf_op jit(solution)/shard_map/ppermute | solution.py:199
  206.7 38.4 %copy-start.2 = (bf16[512,1152]{1,0:T(8,128)(2,1)S(1)}, bf16[512,1152]{1,0:T(8,128)(2,1)}, u32[]{:S(2)}) copy-start(bf16[512,1152]{1,0:T(8,128)(2,1)} %copy-done.1) | copy-start | bytes 3538948
  207.2 37.1 %collective-permute-start.14 = (bf16[256,1152]{1,0:T(8,128)(2,1)}, bf16[256,1152]{1,0:T(8,128)(2,1)S(1)}, u32[]{:S(2)}, u32[]{:S(2)}) collective-permute-start(bf16[256,1152]{1,0:T(8,128)(2,1)} %get-tuple-element.79), channel_id=1, source_target_pairs={{0,64},{64,128},{128,192},{192,0},{1,65},{65,129},{129,193},{193,1... | collective-permute-start | bytes 1769480 | tf_op jit(solution)/shard_map/ppermute | solution.py:24
  207.8 36.6 %collective-permute-start.15 = (bf16[256,1152]{1,0:T(8,128)(2,1)}, bf16[256,1152]{1,0:T(8,128)(2,1)}, u32[]{:S(2)}, u32[]{:S(2)}) collective-permute-start(bf16[256,1152]{1,0:T(8,128)(2,1)} %get-tuple-element.80), channel_id=1, source_target_pairs={{0,192},{64,0},{128,64},{192,128},{1,193},{65,1},{129,65},{193,129... | collective-permute-start | bytes 1769480 | tf_op jit(solution)/shard_map/ppermute | solution.py:24
  212.0 11.7 %all-to-all-start.4 = ((bf16[16,4,2048]{2,1,0:T(4,128)(2,1)}), bf16[16,4,2048]{2,1,0:T(4,128)(2,1)S(1)}, u32[]{:S(2)}, u32[]{:S(2)}) async-start(bf16[16,4,2048]{2,1,0:T(4,128)(2,1)} %reshape.152), calls=%async_computation.4 | async-start | bytes 524288 | tf_op jit(solution)/shard_map/all_to_all | solution.py:28
  216.3 26.7 %collective-permute-start.13 = (bf16[64,2048]{1,0:T(8,128)(2,1)}, bf16[64,2048]{1,0:T(8,128)(2,1)}, u32[]{:S(2)}, u32[]{:S(2)}) collective-permute-start(bf16[64,2048]{1,0:T(8,128)(2,1)} %slice.201), channel_id=1, source_target_pairs={{0,1},{1,0},{2,3},{3,2},{4,5},{5,4},{6,7},{7,6},{8,9},{9,8},{10,11... | collective-permute-start | bytes 786440 | tf_op jit(solution)/shard_map/ppermute | solution.py:208
  224.4 19.9 %all-to-all-start.5 = ((f32[16,2,256]{2,1,0:T(2,128)}), f32[16,2,256]{2,1,0:T(2,128)S(1)}, u32[]{:S(2)}, u32[]{:S(2)}) async-start(f32[16,2,256]{2,1,0:T(2,128)} %bitcast.20), calls=%async_computation.5 | async-start | bytes 65536 | tf_op jit(solution)/shard_map/all_to_all | solution.py:28
  248.1 2.9 %collective-permute-start.16 = (bf16[256,1152]{1,0:T(8,128)(2,1)}, bf16[256,1152]{1,0:T(8,128)(2,1)S(1)}, u32[]{:S(2)}, u32[]{:S(2)}) collective-permute-start(bf16[256,1152]{1,0:T(8,128)(2,1)} %get-tuple-element.107), channel_id=1, source_target_pairs={{0,32},{32,0},{1,33},{33,1},{2,34},{34,2},{3,35},{35,3},{4,36},{36... | collective-permute-start | bytes 1769480 | tf_op jit(solution)/shard_map/ppermute | solution.py:224
  (16 other events, 42.0 us)
